TPU v7x, 512 devices: a whole 4x4x16 slice. The times are simulated.
512 devices in a mesh: row: 16 (over y, z_hi, core), col: 32 (over x, z_lo).
Axes of the slice: x: 4, y: 4, z: 16 (z_hi: 2, z_lo: 8; z = z_hi * 8 + z_lo), core: 2. Of those that a mesh axis runs over, the one named last changes fastest.
Arguments:
- embedding: bfloat16 [2048, 128], P('row'), may hold values from -6 to 6
- kernel: bfloat16 [3, 3, 64, 64], replicated, may hold values from -0.25 to 0.25
- cotangent: bfloat16 [2048, 2048, 64], P('row', 'col'), may hold values from -6 to 6
Outputs:
- prediction: float32 [2048, 2048, 64], P('row', 'col')
- grad_kernel: float32 [3, 3, 64, 64], replicated
- grad_embedding: float32 [2048, 128], P('row')
All inputs are finite; a program needn't handle non-finite values.
Results may differ from a plain program's by a relative error of at most 0.0031.
Values may be sent and summed in bfloat16 or wider, within the bound.
No kernel may reach another device: no remote copies, remote signals or barrier semaphores. Data moves between devices by JAX's collectives and lax.ppermute only.
A program may use at most 128 MiB of HBM per device.

v0:
```python
import jax
import jax.numpy as jnp
from jax import lax
from jax.sharding import PartitionSpec as P

DILATION_STEP = 8


def from_root(shard, axis, root):
    mine = lax.axis_index(axis) == root
    return lax.psum(jnp.where(mine, shard, jnp.zeros_like(shard)), axis)


def padded(cells, sides, width):
    for axis, dim in sides:
        count = lax.axis_size(axis)
        ends = count - 1
        head = lax.slice_in_dim(cells, 0, width, axis=dim)
        tail = lax.slice_in_dim(cells, cells.shape[dim] - width, cells.shape[dim], axis=dim)
        cells = jnp.concatenate(
            [
                lax.ppermute(tail, axis, [(i, (i + 1) % count) for i in range(ends)]),
                cells,
                lax.ppermute(head, axis, [((i + 1) % count, i) for i in range(ends)]),
            ],
            axis=dim,
        )
    return cells


def build_pairs(row_embedding, col_embed, channels):
    return (
        row_embedding[:, None, :channels] * col_embed[None, :, :channels]
        + row_embedding[:, None, channels:]
        + col_embed[None, :, channels:]
    )


def on_device(embedding, kernel, cotangent):
    rows_local = embedding.shape[0]
    columns_local = cotangent.shape[1]
    channels = kernel.shape[2]
    col_ratio = lax.axis_size("col") // lax.axis_size("row")
    bin_count = rows_local * lax.axis_size("row")
    row_id = lax.axis_index("row")
    col_id = lax.axis_index("col")
    own_slice = lax.dynamic_slice_in_dim(
        embedding, col_id % col_ratio * columns_local, columns_local, 0
    )
    col_embed = from_root(own_slice, "row", col_id // col_ratio)
    row_float = embedding.astype(jnp.float32)
    col_float = col_embed.astype(jnp.float32)
    row_wide = padded(embedding, (("row", 0),), DILATION_STEP).astype(jnp.float32)
    col_wide = padded(col_embed, (("col", 0),), DILATION_STEP).astype(jnp.float32)
    row_pos = (
        row_id * rows_local
        - DILATION_STEP
        + jnp.arange(rows_local + 2 * DILATION_STEP, dtype=jnp.int32)
    )
    col_pos = (
        col_id * columns_local
        - DILATION_STEP
        + jnp.arange(columns_local + 2 * DILATION_STEP, dtype=jnp.int32)
    )
    row_valid = ((row_pos >= 0) & (row_pos < bin_count)).astype(jnp.float32)
    col_valid = ((col_pos >= 0) & (col_pos < bin_count)).astype(jnp.float32)
    valid_wide = row_valid[:, None, None] * col_valid[None, :, None]
    wide_pre = build_pairs(row_wide, col_wide, channels)
    activation_wide = (jax.nn.silu(wide_pre) * valid_wide).astype(jnp.bfloat16)
    preactivation = wide_pre[
        DILATION_STEP : DILATION_STEP + rows_local, DILATION_STEP : DILATION_STEP + columns_local
    ]
    cotangent_wide = padded(cotangent, (("row", 0), ("col", 1)), DILATION_STEP)
    forward = jnp.zeros((rows_local, columns_local, channels), jnp.float32)
    backward = jnp.zeros((rows_local, columns_local, channels), jnp.float32)
    kernel_rows = []
    for kernel_tap_row in range(3):
        kernel_cols = []
        for kernel_tap_column in range(3):
            shifted_pairs = activation_wide[
                kernel_tap_row * DILATION_STEP : kernel_tap_row * DILATION_STEP + rows_local,
                kernel_tap_column * DILATION_STEP : kernel_tap_column * DILATION_STEP
                + columns_local,
            ]
            forward = forward + jnp.einsum(
                "ijc,cd->ijd",
                shifted_pairs,
                kernel[kernel_tap_row, kernel_tap_column],
                preferred_element_type=jnp.float32,
            )
            kernel_cols.append(
                jnp.einsum(
                    "ijc,ijd->cd", shifted_pairs, cotangent, preferred_element_type=jnp.float32
                )
            )
            cotangent_shifted = cotangent_wide[
                (2 - kernel_tap_row) * DILATION_STEP : (2 - kernel_tap_row) * DILATION_STEP
                + rows_local,
                (2 - kernel_tap_column) * DILATION_STEP : (2 - kernel_tap_column) * DILATION_STEP
                + columns_local,
            ]
            backward = backward + jnp.einsum(
                "ijd,cd->ijc",
                cotangent_shifted,
                kernel[kernel_tap_row, kernel_tap_column],
                preferred_element_type=jnp.float32,
            )
        kernel_rows.append(jnp.stack(kernel_cols))
    kernel_local = jnp.stack(kernel_rows)
    sigmoid_val = jax.nn.sigmoid(preactivation)
    grad_pre = backward * sigmoid_val * (1.0 + preactivation * (1.0 - sigmoid_val))
    row_part = jnp.concatenate(
        [jnp.sum(grad_pre * col_float[None, :, :channels], axis=1), jnp.sum(grad_pre, axis=1)],
        axis=1,
    )
    col_part = jnp.concatenate(
        [jnp.sum(grad_pre * row_float[:, None, :channels], axis=0), jnp.sum(grad_pre, axis=0)],
        axis=1,
    )
    kernel_total = lax.psum(kernel_local, ("row", "col"))
    row_total = lax.psum(row_part, "col")
    col_total = lax.psum(col_part, "row")
    pieces = []
    for part_index in range(col_ratio):
        pieces.append(from_root(col_total, "col", row_id * col_ratio + part_index))
    col_full = jnp.concatenate(pieces, axis=0)
    grad_kernel = kernel_total / bin_count
    grad_embedding = (row_total + col_full) * float(bin_count) ** (-0.5)
    return (forward, grad_kernel, grad_embedding)


def solution(mesh):
    in_specs = (P("row", None), P(), P("row", "col", None))
    out_specs = (P("row", "col", None), P(), P("row", None))
    return jax.shard_map(
        on_device, mesh=mesh, in_specs=in_specs, out_specs=out_specs, check_vma=False
    )
```

profile of v0, /device:TPU:1, one launch (start us, length us, event | category | flops | bytes accessed | tf_op | source)
XLA Modules:
  0.0 1502.5 jit_solution(9372366426042510501)
XLA Ops:
  7.2 0.7 dynamic-slice_select_fusion
  8.0 126.7 %psum.42 = bf16[64,128]{1,0:T(8,128)(2,1)S(1)} all-reduce(bf16[64,128]{1,0:T(8,128)(2,1)S(1)} %dynamic-slice_select_fusion), channel_id=1, replica_groups=mesh['row'=16,'col'=32] {'row'}, use_global_device_ids=true, to_apply=%region_0.1 | all-reduce | flops 8192 | bytes 32768 | tf_op jit(solution)/shard_map/psum | solution.py:11
  134.6 2.6 collective-permute-start.2
  137.2 1.3 collective-permute-start.3
  138.5 0.7 fusion.87
  139.2 12.5 collective-permute-start
  151.8 4.2 collective-permute-start.1
  155.9 2.1 fusion.84
  158.0 0.4 copy.142
  158.4 10.2 collective-permute-start.4
  168.8 1.7 fusion.53
  170.6 0.4 copy.143
  171.0 0.1 copy.144
  171.1 1.9 collective-permute-start.5
  173.2 0.1 fusion.85
  173.3 0.1 copy.85
  173.5 4.2 add_add_fusion
  177.7 0.5 convolution_bitcast_fusion.3
  178.2 0.5 convolution_bitcast_fusion.4
  178.7 0.5 convolution_bitcast_fusion.5
  179.3 0.4 convolution_bitcast_fusion.6
  179.7 0.4 convolution_bitcast_fusion.7
  180.1 0.4 convolution_bitcast_fusion.8
  180.5 0.5 convolution_bitcast_fusion
  181.1 0.5 convolution_bitcast_fusion.1
  181.6 0.5 convolution_bitcast_fusion.2
  182.1 1.9 fusion.21
  184.0 1.9 fusion.24
  186.0 1.8 fusion.27
  187.8 2.0 fusion.30
  189.8 1.8 fusion.33
  191.6 1.8 fusion.36
  193.4 1.8 fusion.39
  195.2 1.8 fusion.42
  197.0 0.7 pad_maximum_fusion.5
  197.8 0.2 all-reduce.9.cloned.1.call-start
  198.0 8.5 add_add_fusion.1
  206.5 1.4 copy.99
  207.9 3.6 fusion.14
  211.5 1.4 copy.98
  212.9 0.3 pad_maximum_fusion.6
  213.2 1.3 collective-permute-start.6
  214.5 4.9 collective-permute-start.7
  219.4 0.7 fusion.4
  220.1 1.1 collective-permute-done.6
  221.2 1.5 collective-permute-done.7
  222.7 2.9 maximum_maximum_fusion
  225.6 0.5 fusion.10
  226.2 0.5 fusion.16
  226.7 0.4 fusion.6
  227.2 0.5 fusion.12
  227.7 0.5 fusion.8
  228.3 0.5 copy-done.4
  228.8 0.8 copy-done.3
  229.5 5.0 multiply_reduce_fusion
  234.7 112.1 %psum.45 = f32[64,128]{0,1:T(8,128)S(1)} all-reduce(f32[64,128]{0,1:T(8,128)S(1)} %pad_maximum_fusion.10), channel_id=1, replica_groups=mesh['row'=16,'col'=32] {'row'}, use_global_device_ids=true, to_apply=%region_7.8 | all-reduce | flops 8192 | bytes 65536 | tf_op jit(solution)/shard_map/psum | solution.py:122
  346.8 0.7 broadcast_select_fusion.1
  347.5 0.6 pad_maximum_fusion.9
  348.2 315.5 %all-reduce.5.cloned.1.call-done = f32[3,3,64,64]{3,2,1,0:T(8,128)} async-done(((f32[3,3,64,64]{3,2,1,0:T(8,128)}), f32[3,3,64,64]{3,2,1,0:T(8,128)}) %all-reduce.5.cloned.1.call-update) | async-done | bytes 147472 | tf_op jit(solution)/shard_map/psum | solution.py:120
  663.7 1.7 broadcast_multiply_fusion
  665.4 409.8 %all-reduce.9.cloned.1.call-done = (f32[64,128]{0,1:T(8,128)}, f32[64,128]{0,1:T(8,128)}) async-done(((f32[64,128]{0,1:T(8,128)}, f32[64,128]{0,1:T(8,128)}), (f32[64,128]{0,1:T(8,128)}, f32[64,128]{0,1:T(8,128)})) %all-reduce.9.cloned.1.call-update) | async-done | bytes 65552 | tf_op jit(solution)/shard_map/psum | solution.py:11
  1075.2 419.0 %all-reduce.7.cloned.1.call-done = f32[128,128]{0,1:T(8,128)} async-done(((f32[128,128]{0,1:T(8,128)}), f32[128,128]{0,1:T(8,128)}) %all-reduce.7.cloned.1.call-update) | async-done | bytes 65552 | tf_op jit(solution)/shard_map/psum | solution.py:121
  1494.3 1.0 fusion.44
  1495.2 0.7 copy.114
  (38 shorter events, 0.7 us)
Async XLA Ops:
  7.2 656.5 %all-reduce.5.cloned.1.call-start = ((), (), s32[]{:S(2)}) async-start(), calls=%async_computation | async-start | bytes 589824 | tf_op jit(solution)/shard_map/psum | solution.py:120
  134.6 36.5 %collective-permute-start.2 = (bf16[8,128]{1,0:T(8,128)(2,1)S(1)}, bf16[8,128]{1,0:T(8,128)(2,1)S(1)}, u32[]{:S(2)}, u32[]{:S(2)}) collective-permute-start(bf16[8,128]{1,0:T(8,128)(2,1)S(1)} %get-tuple-element.34), channel_id=1, source_target_pairs={{0,1},{1,2},{2,3},{3,4},{4,5},{5,6},{6,7},{7,8},{8,9},{9,10},{10,1... | collective-permute-start | bytes 6152 | tf_op jit(solution)/shard_map/ppermute | solution.py:22
  137.2 35.8 %collective-permute-start.3 = (bf16[8,128]{1,0:T(8,128)(2,1)S(1)}, bf16[8,128]{1,0:T(8,128)(2,1)S(1)}, u32[]{:S(2)}, u32[]{:S(2)}) collective-permute-start(bf16[8,128]{1,0:T(8,128)(2,1)S(1)} %get-tuple-element.35), channel_id=1, source_target_pairs={{1,0},{2,1},{3,2},{4,3},{5,4},{6,5},{7,6},{8,7},{9,8},{10,9},{11,1... | collective-permute-start | bytes 6152 | tf_op jit(solution)/shard_map/ppermute | solution.py:24
  139.2 33.9 %collective-permute-start = (bf16[8,128]{1,0:T(8,128)(2,1)S(1)}, bf16[8,128]{1,0:T(8,128)(2,1)S(1)}, u32[]{:S(2)}, u32[]{:S(2)}) collective-permute-start(bf16[8,128]{1,0:T(8,128)(2,1)S(1)} %get-tuple-element.32), channel_id=1, source_target_pairs={{0,32},{32,64},{64,96},{96,128},{128,160},{160,192},{192,224},{224... | collective-permute-start | bytes 6152 | tf_op jit(solution)/shard_map/ppermute | solution.py:22
  151.7 17.0 %copy-start = (bf16[128,64,64]{0,2,1:T(8,128)(2,1)S(1)}, bf16[128,64,64]{0,2,1:T(8,128)(2,1)}, u32[]{:S(2)}) copy-start(bf16[128,64,64]{0,2,1:T(8,128)(2,1)} %param.5) | copy-start | bytes 3145732
  151.8 17.0 %copy-start.5 = (bf16[3,3,64,64]{3,2,1,0:T(8,128)(2,1)S(1)}, bf16[3,3,64,64]{3,2,1,0:T(8,128)(2,1)}, u32[]{:S(2)}) copy-start(bf16[3,3,64,64]{3,2,1,0:T(8,128)(2,1)} %param.4) | copy-start | bytes 221188
  151.8 21.4 %collective-permute-start.1 = (bf16[8,128]{1,0:T(8,128)(2,1)S(1)}, bf16[8,128]{1,0:T(8,128)(2,1)S(1)}, u32[]{:S(2)}, u32[]{:S(2)}) collective-permute-start(bf16[8,128]{1,0:T(8,128)(2,1)S(1)} %get-tuple-element.33), channel_id=1, source_target_pairs={{32,0},{64,32},{96,64},{128,96},{160,128},{192,160},{224,192},{256... | collective-permute-start | bytes 6152 | tf_op jit(solution)/shard_map/ppermute | solution.py:24
  158.4 12.6 copy-start.6
  158.4 53.0 %collective-permute-start.4 = (bf16[8,64,64]{2,1,0:T(8,128)(2,1)S(1)}, bf16[8,64,64]{2,1,0:T(8,128)(2,1)}, u32[]{:S(2)}, u32[]{:S(2)}) collective-permute-start(bf16[8,64,64]{2,1,0:T(8,128)(2,1)S(1)} %copy.142), channel_id=1, source_target_pairs={{0,32},{32,64},{64,96},{96,128},{128,160},{160,192},{192,224},{224... | collective-permute-start | bytes 196616 | tf_op jit(solution)/shard_map/ppermute | solution.py:22
  171.1 35.3 %collective-permute-start.5 = (bf16[8,64,64]{2,1,0:T(8,128)(2,1)S(1)}, bf16[8,64,64]{2,1,0:T(8,128)(2,1)}, u32[]{:S(2)}, u32[]{:S(2)}) collective-permute-start(bf16[8,64,64]{2,1,0:T(8,128)(2,1)S(1)} %copy.143), channel_id=1, source_target_pairs={{32,0},{64,32},{96,64},{128,96},{160,128},{192,160},{224,192},{256... | collective-permute-start | bytes 196616 | tf_op jit(solution)/shard_map/ppermute | solution.py:24
  173.5 4.2 copy-start.1
  197.8 877.5 %all-reduce.9.cloned.1.call-start = ((), (), s32[]{:S(2)}) async-start(), calls=%async_computation.2 | async-start | bytes 262144 | tf_op jit(solution)/shard_map/psum | solution.py:11
  207.9 5.0 copy-start.2
  213.2 8.0 collective-permute-start.6
  214.5 8.3 collective-permute-start.7
  227.2 1.6 copy-start.4
  227.7 1.8 copy-start.3
  347.5 1146.8 %all-reduce.7.cloned.1.call-start = ((), (), s32[]{:S(2)}) async-start(), calls=%async_computation.1 | async-start | bytes 131072 | tf_op jit(solution)/shard_map/psum | solution.py:121
Sparse Core Ops, SparseCore 0:
  197.9 465.7 all-reduce.4
  667.0 408.2 all-reduce.8
  1078.7 415.4 all-reduce.6
where the time goes:
time: 1510 us; the launch traced here: 1500 us
  waiting for transfers between devices  1150 us (76%)
  blocking collectives  239 us (16%)
  matrix products  41.3 us (3%)
  starting transfers between devices  39.2 us (3%)
    psum x1, waiting for transfers between devices, on_device(): row_total = lax.psum(row_part, 'col')  419 us
    psum x1, waiting for transfers between devices, from_root(): return lax.psum(jnp.where(mine, shard, jnp.zeros_like(shard)), axis)  410 us
    psum x1, waiting for transfers between devices, on_device(): kernel_total = lax.psum(kernel_local, ('row', 'col'))  316 us
    psum x1, blocking collectives, from_root(): return lax.psum(jnp.where(mine, shard, jnp.zeros_like(shard)), axis)  127 us
    psum x1, blocking collectives, on_device(): col_total = lax.psum(col_part, 'row')  112 us
    ppermute x4, starting transfers between devices, padded(): lax.ppermute(tail, axis, [(i, (i + 1) % count) for i in range(ends)])  30.2 us
  transfers between devices with their start and end apart: 11, of which 5 were waited for; matrix products, arithmetic and copies ran while one was open for 4% of the time, Pallas kernels for 0%

commit v1 on v0

v1 whole, which is shorter than its diff:
```python
import jax
import jax.numpy as jnp
from jax import lax
from jax.experimental import pallas as pl
from jax.experimental.pallas import tpu as pltpu
from jax.sharding import PartitionSpec as P

BF16 = jnp.bfloat16
F32 = jnp.float32

ROWS, COLS = 16, 32


def device_id(y, z_hi, core, x, z_lo):
    return (y * 4 + z_hi * 2 + core) * COLS + x * 8 + z_lo


PLANE_GROUPS = [
    [device_id(y, zh, k, x, zl) for y in range(4) for k in range(2) for x in range(4)]
    for zh in range(2)
    for zl in range(8)
]
LINE_GROUPS = [
    [device_id(y, zh, k, x, zl) for zh in range(2) for zl in range(8)]
    for y in range(4)
    for k in range(2)
    for x in range(4)
]
ROW_GROUPS = [
    [
        device_id(r // 4, r // 2 % 2, r % 2, x, (zl + 4 * (r // 2 % 2)) % 8)
        for r in range(ROWS)
    ]
    for x in range(4)
    for zl in range(8)
]


def exchange(parts, groups):
    return lax.all_to_all(parts, ("row", "col"), 0, 0, axis_index_groups=groups)


C = 64
I = 128
J = 64
G = 8


def lanes():
    return lax.broadcasted_iota(jnp.int32, (C, I), 1)


def turn(x, shift):
    return pltpu.roll(x.astype(F32), shift % I, 1).astype(x.dtype)


def dot(a, b):
    return lax.dot_general(a, b, (((1,), (0,)), ((), ())), preferred_element_type=F32)


def dot_lanes(a, b):
    return lax.dot_general(a, b, (((1,), (1,)), ((), ())), preferred_element_type=F32)


def split_dot(x, picks):
    high = x.astype(BF16)
    low = (x - high.astype(F32)).astype(BF16)
    return dot(high, picks) + dot(low, picks)


def shifted(act, edge, jj, lane):
    ends = turn(edge, -(16 * jj + 8))
    wide = act.astype(F32)
    before = jnp.where(lane < 8, ends.astype(F32), pltpu.roll(wide, 8, 1)).astype(BF16)
    after = jnp.where(lane >= 120, ends.astype(F32), pltpu.roll(wide, I - 8, 1)).astype(BF16)
    return jnp.concatenate([before, act, after], axis=0)


def main_kernel(cot, w, row_wide, col_wide, ids, out, act_out, edge_out, ga, gae, gk, acc):
    lane = lanes()
    slot = lane % 16
    weights = jnp.concatenate(
        [jnp.concatenate([w[3 * a + b] for a in range(3)], axis=1) for b in range(3)], axis=0
    )
    edge_weights = jnp.concatenate(
        [jnp.concatenate([w[b], w[6 + b]], axis=1) for b in range(3)], axis=0
    )

    def put(ref, place, value, fresh):
        ref[place] = value if fresh else ref[place] + value

    def back(k, first):
        fresh = [first, first, True]
        packed = jnp.zeros((C, I), F32)
        for p in range(0, G, 2):
            stacks = []
            for q in (p, p + 1):
                x = cot[G * k + q]
                wide = x.astype(F32)
                later = jnp.where(lane < 120, pltpu.roll(wide, I - 8, 1), 0.0).astype(BF16)
                earlier = jnp.where(lane >= 8, pltpu.roll(wide, 8, 1), 0.0).astype(BF16)
                stacks.append(jnp.concatenate([later, x, earlier], axis=0))
                packed = jnp.where(lane // 16 == q, pltpu.roll(wide, (16 * q + 8) % I, 1), packed)
            part = dot(weights, jnp.concatenate(stacks, axis=1))
            for b in range(3):
                for n, q in enumerate((p, p + 1)):
                    value = part[C * b : C * b + C, I * n : I * n + I]
                    put(ga, G * (k + b) + q, value, fresh[b])
        both = jnp.concatenate(
            [jnp.where(slot >= 8, packed, 0.0), jnp.where(slot < 8, packed, 0.0)], axis=0
        ).astype(BF16)
        part = dot(edge_weights, both)
        for b in range(3):
            put(gae, k + b, part[C * b : C * b + C], fresh[b])

    back(0, True)

    @pl.loop(1, 8)
    def _(k):
        back(k, False)

    acc[...] = jnp.zeros_like(acc)
    gk[...] = jnp.zeros_like(gk)
    wide = row_wide[...].astype(F32)
    row = wide[G : G + I].T
    ends = jnp.concatenate([wide[G + I :], wide[:G]], axis=0)
    edge_row = jnp.concatenate([ends] * 8, axis=0).T
    u_row, v_row = row[:C], row[C:]
    u_edge, v_edge = edge_row[:C], edge_row[C:]
    col_f = col_wide[...].astype(F32).T
    col = col_f.astype(BF16)
    has_low = (ids[0] > 0).astype(F32)
    has_high = (ids[0] < ROWS - 1).astype(F32)
    edge_mask = jnp.where(slot < 8, has_high, has_low)
    m0 = lax.broadcasted_iota(jnp.int32, (I, I), 0)
    m1 = lax.broadcasted_iota(jnp.int32, (I, I), 1)

    def gate(x):
        s = 0.5 + 0.5 * jnp.tanh(0.5 * x)
        y = x * s
        return y, s + y * (1.0 - s)

    def group(k, taps, mask):
        spread = (m0 == G * k + m1 // 16).astype(BF16)
        gather = (m1 == G * k + m0 // 16).astype(BF16)
        here = dot(col, spread)
        edge_on = edge_mask * mask
        y, slope = gate(u_edge * here[:C] + (v_edge + here[C:]))
        edge_act = y * edge_on
        edge_out[k] = edge_act.astype(BF16)
        g = gae[k] * (slope * edge_on)
        acc[4] += g * here[:C]
        acc[5] += g
        acc[2] += split_dot(g * u_edge, gather)
        acc[3] += split_dot(g, gather)
        near = pltpu.roll(col_f, (I - G * k) % I, 1)
        stacks = []
        for q in range(G):
            uc, vc = near[:C, q : q + 1], near[C:, q : q + 1]
            y, slope = gate(u_row * uc + (v_row + vc))
            act = (y * mask).astype(BF16)
            act_out[G * k + q] = act
            stacks.append(shifted(act, edge_act, q, lane))
            g = ga[G * k + q] * (slope * mask)
            acc[0] += g * uc
            acc[1] += g
            here_lane = lane == G * k + q
            acc[2] += jnp.where(here_lane, jnp.sum(g * u_row, axis=1, keepdims=True), 0.0)
            acc[3] += jnp.where(here_lane, jnp.sum(g, axis=1, keepdims=True), 0.0)
        acts = jnp.concatenate(stacks, axis=1)
        cots = jnp.concatenate(
            [jnp.concatenate([cot[G * (k - b) + q] for q in range(G)], axis=1) for b in taps], axis=0
        )
        gk[:, C * taps[0] : C * (taps[-1] + 1)] += dot_lanes(acts, cots)

    group(0, [0], (ids[1] > 0).astype(F32))
    group(1, [0, 1], 1.0)

    @pl.loop(2, 8)
    def _(k):
        group(k, [0, 1, 2], 1.0)

    group(8, [1, 2], 1.0)
    group(9, [2], (ids[1] < COLS - 1).astype(F32))

    def fold(x):
        x = x + pltpu.roll(x, 64, 1)
        x = x + pltpu.roll(x, 32, 1)
        return x + pltpu.roll(x, 16, 1)

    big_lane = lax.broadcasted_iota(jnp.int32, (2 * C, I), 1)
    ends = pltpu.roll(fold(jnp.concatenate([acc[4], acc[5]], axis=0)), 80, 1)
    sums = jnp.concatenate([acc[2], acc[3]], axis=0)
    total = gk[...]
    rest = jnp.concatenate([total[: 2 * C, 128:160]] * 4, axis=1)
    misc = jnp.where(big_lane < 80, sums, jnp.where(big_lane < 96, ends, rest))
    tail = jnp.concatenate([total[128:, 128:], total[:64, 160:], total[64:128, 160:]], axis=1)
    rows = jnp.concatenate([acc[0], acc[1]], axis=0)
    for t in range(32):
        if t < 24:
            out[t, :8] = total[8 * t : 8 * t + 8, :128]
        else:
            out[t, :8] = tail[8 * (t - 24) : 8 * (t - 24) + 8]
        out[t, 8:12] = rows[4 * t : 4 * t + 4]
        out[t, 12:16] = misc[4 * t : 4 * t + 4]


def whole(shape, dtype):
    return jax.ShapeDtypeStruct(shape, dtype)


VMEM = pl.BlockSpec(memory_space=pltpu.VMEM)
SMEM = pl.BlockSpec(memory_space=pltpu.SMEM)


def run_main(cot, w, row_wide, col_wide, ids):
    return pl.pallas_call(
        main_kernel,
        out_shape=(whole((32, 16, I), F32), whole((80, C, I), BF16), whole((10, C, I), BF16)),
        in_specs=[VMEM] * 4 + [SMEM],
        out_specs=(VMEM, VMEM, VMEM),
        scratch_shapes=[
            pltpu.VMEM((80, C, I), F32),
            pltpu.VMEM((10, C, I), F32),
            pltpu.VMEM((192, 192), F32),
            pltpu.VMEM((6, C, I), F32),
        ],
        compiler_params=pltpu.CompilerParams(vmem_limit_bytes=40 * 2**20),
        cost_estimate=pl.CostEstimate(flops=1_300_000_000, bytes_accessed=3_500_000, transcendentals=700_000),
        name="tile_gradients",
    )(cot, w, row_wide, col_wide, ids)


def forward_kernel(act, edge, w, out):
    lane = lanes()
    weights = w[...]

    def group(k, taps):
        edge_act = edge[k].astype(F32)
        for p in range(0, G, 2):
            stack = jnp.concatenate(
                [shifted(act[G * k + q], edge_act, q, lane) for q in (p, p + 1)], axis=1
            )
            part = dot(weights[C * taps[0] : C * (taps[-1] + 1)], stack)
            for n, b in enumerate(taps):
                for h, q in enumerate((p, p + 1)):
                    value = part[C * n : C * n + C, I * h : I * h + I]
                    place = G * (k - b) + q
                    out[place] = value if b == 0 else out[place] + value

    group(0, [0])
    group(1, [0, 1])

    @pl.loop(2, 8)
    def _(k):
        group(k, [0, 1, 2])

    group(8, [1, 2])
    group(9, [2])


def run_forward(act, edge, w):
    return pl.pallas_call(
        forward_kernel,
        out_shape=whole((J, C, I), F32),
        in_specs=[VMEM] * 3,
        out_specs=VMEM,
        compiler_params=pltpu.CompilerParams(vmem_limit_bytes=40 * 2**20),
        cost_estimate=pl.CostEstimate(flops=700_000_000, bytes_accessed=3_500_000, transcendentals=0),
        name="tile_forward",
    )(act, edge, w)


def reduce_all(parts, z_hi):
    got = exchange(parts, PLANE_GROUPS)
    kernel_sum = jnp.sum(got[:, :8], axis=0)
    rest_sum = jnp.sum(got[:, 12:, 96:], axis=0)
    by_row = got.reshape(8, 4, 16, 128)
    row_main = jnp.sum(by_row[:, :, 8:12], axis=1).reshape(32, 128)
    row_edge = jnp.sum(by_row[:, :, 12:, 80:96], axis=1).reshape(32, 16)
    col_wide = jnp.sum(by_row[:, :, 12:, :80], axis=0).reshape(16, 80)
    tail = jnp.concatenate(
        [col_wide, row_edge[:16], row_edge[16:], rest_sum.reshape(16, 8), jnp.zeros((16, 8), F32)], axis=1
    )
    share = jnp.concatenate([kernel_sum, row_main, tail], axis=0).astype(BF16)
    got = exchange(jnp.broadcast_to(share[None], (16, 56, 128)), LINE_GROUPS).astype(F32)
    kernel_sum = jnp.sum(got[:, :8], axis=0)
    rest_sum = jnp.sum(got[:, 40:, 112:120], axis=0).reshape(4, 32)
    halves = got.reshape(2, 8, 56, 128)
    mine = lax.dynamic_index_in_dim(halves, z_hi, 0, keepdims=False)
    total = jnp.sum(mine[:, 8:40], axis=0).reshape(4, 2, 4, 128)
    edges = jnp.sum(halves[:, :, 40:, 80:112], axis=1)
    edges = jnp.concatenate([edges[:, :, :16], edges[:, :, 16:]], axis=1).reshape(2, 4, 2, 4, 16)
    edges = edges.transpose(1, 0, 2, 3, 4).reshape(16, 4, 16)
    none = jnp.zeros((1, 4, 8), F32)
    from_left = jnp.concatenate([none, edges[:-1, :, :8]], axis=0)
    from_right = jnp.concatenate([edges[1:, :, 8:], none], axis=0)
    cols = jnp.sum(halves[:, :, 40:, :80], axis=0).reshape(8, 4, 4, 80)
    cols = cols.transpose(1, 0, 2, 3).reshape(32, 4, 80)
    low = jnp.concatenate([none, cols[:-1, :, 72:]], axis=0)
    high = jnp.concatenate([cols[1:, :, :8], none], axis=0)
    inner = cols[:, :, 8:72]
    inner = jnp.concatenate([inner[:, :, :8] + low, inner[:, :, 8:56], inner[:, :, 56:] + high], axis=2)
    inner = inner.reshape(16, 2, 4, 64).transpose(0, 2, 1, 3).reshape(16, 4, 128)
    inner = jnp.concatenate(
        [inner[:, :, :8] + from_left, inner[:, :, 8:120], inner[:, :, 120:] + from_right], axis=2
    )
    inner = lax.dynamic_index_in_dim(inner.reshape(4, 2, 2, 4, 128), z_hi, 1, keepdims=False)
    total = (total + inner).reshape(8, 1, 4, 128)
    total = jnp.broadcast_to(total, (8, 4, 4, 128)).reshape(32, 4, 128)
    rest_sum = jnp.pad(rest_sum, ((0, 0), (0, 96)))
    done = jnp.concatenate([kernel_sum, rest_sum], axis=0)
    done = jnp.broadcast_to(done[None], (32, 12, 128))
    got = exchange(jnp.concatenate([done, total], axis=1), PLANE_GROUPS)
    main = got[:, :8].reshape(256, 128)
    rest = got[:, 8:12, :32].reshape(128, 32)
    right = jnp.concatenate([rest, jnp.concatenate([main[192:, 64:96], main[192:, 96:]], axis=0)], axis=1)
    right = jnp.concatenate([right, main[192:, :64]], axis=0)
    gk = jnp.concatenate([main[:192], right], axis=1)
    return gk, got[:, 12:].reshape(128, 128)


def on_device(embedding, kernel, cotangent):
    rows_local = embedding.shape[0]
    bin_count = rows_local * ROWS
    row_id = lax.axis_index("row")
    col_id = lax.axis_index("col")
    everyone = exchange(jnp.broadcast_to(embedding[None], (ROWS,) + embedding.shape), ROW_GROUPS)
    everyone = jnp.pad(everyone.reshape(bin_count, 2 * C), ((G, I), (0, 0)))
    row_wide = lax.dynamic_slice_in_dim(everyone, row_id * rows_local, rows_local + 2 * G, 0)
    col_wide = lax.dynamic_slice_in_dim(everyone, col_id * J, I, 0)
    ids = jnp.stack([row_id, col_id])
    parts, act, edge = run_main(
        cotangent.transpose(1, 2, 0), kernel.reshape(9, C, C), row_wide, col_wide, ids
    )
    taps = kernel.transpose(1, 3, 0, 2).reshape(192, 192)
    prediction = run_forward(act, edge, taps).transpose(2, 0, 1)
    gk, ge = reduce_all(parts, row_id // 2 % 2)
    gk = gk.reshape(3, C, 3, C).transpose(0, 2, 1, 3)
    return prediction, gk / bin_count, ge.T * float(bin_count) ** (-0.5)


def solution(mesh):
    in_specs = (P("row", None), P(), P("row", "col", None))
    out_specs = (P("row", "col", None), P(), P("row", None))
    return jax.shard_map(
        on_device, mesh=mesh, in_specs=in_specs, out_specs=out_specs, check_vma=False
    )
```

time: 1510 us -> 120 us (0.08)
  waiting for transfers between devices: 1150 us -> 40.7 us
  blocking collectives: 239 us -> 16.3 us
  matrix products: 41.3 us -> 0 us
  Pallas kernels: 0 us -> 19.7 us
    psum x3 -> x0, waiting for transfers between devices: 1140 us -> none  [the longest x1 419 us: on_device(): row_total = lax.psum(row_part, 'col')]
    psum x2 -> x0, blocking collectives: 239 us -> none  [the longest x1 127 us: from_root(): return lax.psum(jnp.where(mine, shard, jnp.zeros_like(shard)), axis)]
    dot_general x27 -> x0, matrix products: 41.3 us -> none  [the longest x9 23.3 us: on_device(): jnp.einsum('ijc,cd->ijd', shifted_pairs, kernel[kernel_tap_row, kernel_ta...]
    all_to_all x0 -> x3, waiting for transfers between devices: none -> 40.7 us  [exchange(): return lax.all_to_all(parts, ('row', 'col'), 0, 0, axis_index_groups=groups)]
    ppermute x8 -> x0, starting transfers between devices: 38.9 us -> none  [the longest x4 30.2 us: padded(): lax.ppermute(tail, axis, [(i, (i + 1) % count) for i in range(ends)])]
    all_to_all x0 -> x3, starting transfers between devices: none -> 34.8 us  [exchange(): return lax.all_to_all(parts, ('row', 'col'), 0, 0, axis_index_groups=groups)]
    pallas_call x0 -> x2, Pallas kernels: none -> 19.7 us  [the longest x1 15.3 us: run_main(): pl.pallas_call(main_kernel, out_shape=(whole((32, 16, I), F32), whole((80...]
    all_to_all x0 -> x1, blocking collectives: none -> 16.3 us  [exchange(): return lax.all_to_all(parts, ('row', 'col'), 0, 0, axis_index_groups=groups)]
  transfers between devices with their start and end apart: 11 -> 3, of which waited for: 5 -> 3; matrix products, arithmetic and copies ran while one was open for 4% -> 0% of each run, Pallas kernels for 0% -> 4%
where the time goes in v1:
time: 120 us
  waiting for transfers between devices  40.7 us (34%)
  starting transfers between devices  34.8 us (29%)
  Pallas kernels  19.7 us (16%)
  blocking collectives  16.3 us (14%)
  local copies, waits for them, and re-layouts  5.58 us (5%)
  other arithmetic  1.93 us (2%)
    all_to_all x3, waiting for transfers between devices, exchange(): return lax.all_to_all(parts, ('row', 'col'), 0, 0, axis_index_groups=groups)  40.7 us
    all_to_all x3, starting transfers between devices, exchange(): return lax.all_to_all(parts, ('row', 'col'), 0, 0, axis_index_groups=groups)  34.8 us
    all_to_all x1, blocking collectives, exchange(): return lax.all_to_all(parts, ('row', 'col'), 0, 0, axis_index_groups=groups)  16.3 us
    pallas_call x1, Pallas kernels, run_main(): pl.pallas_call(main_kernel, out_shape=(whole((32, 16, I), F32), whole((80...  15.3 us
    pallas_call x1, Pallas kernels, run_forward(): pl.pallas_call(forward_kernel, out_shape=whole((J, C, I), F32), in_specs=...  4.36 us
  transfers between devices with their start and end apart: 3, of which 3 were waited for; matrix products, arithmetic and copies ran while one was open for 0% of the time, Pallas kernels for 4%

profile of v1, /device:TPU:1, one launch (start us, length us, event | category | flops | bytes accessed | tf_op | source)
XLA Modules:
  0.0 120.0 jit_solution(11794853505661466967)
XLA Ops:
  0.6 0.0 copy-start.1
  0.6 0.0 copy-start
  0.7 1.7 %broadcast_in_dim.10 = bf16[16,128,128]{2,1,0:T(8,128)(2,1)} broadcast(bf16[128,128]{1,0:T(8,128)(2,1)} %param.3), dimensions={1,2} | broadcast | bytes 557056 | tf_op jit(solution)/shard_map/broadcast_in_dim | solution.py:328
  2.4 16.2 %all-to-all-start = ((bf16[16,128,128]{2,1,0:T(8,128)(2,1)}), bf16[16,128,128]{2,1,0:T(8,128)(2,1)S(1)}, u32[]{:S(2)}, u32[]{:S(2)}) async-start(bf16[16,128,128]{2,1,0:T(8,128)(2,1)} %broadcast_in_dim.10), calls=%async_computation | async-start | bytes 1048576 | tf_op jit(solution)/shard_map/all_to_all | solution.py:40
  18.6 0.1 pad_add_fusion.ids
  18.7 23.0 %all-to-all-done = bf16[16,128,128]{2,1,0:T(8,128)(2,1)S(1)} async-done(((bf16[16,128,128]{2,1,0:T(8,128)(2,1)}), bf16[16,128,128]{2,1,0:T(8,128)(2,1)S(1)}, u32[]{:S(2)}, u32[]{:S(2)}) %all-to-all-start) | async-done | bytes 524320 | tf_op jit(solution)/shard_map/all_to_all | solution.py:40
  41.7 0.1 pad_dynamic-slice_fusion.1.row_wide
  41.8 0.1 pad_dynamic-slice_fusion.col_wide
  41.9 0.0 copy-done.1
  41.9 0.0 copy-done
  41.9 15.3 %tile_gradients.1 = (f32[32,16,128]{2,1,0:T(8,128)S(1)}, bf16[80,64,128]{2,1,0:T(8,128)(2,1)S(1)}, bf16[10,64,128]{2,1,0:T(8,128)(2,1)S(1)}) custom-call(bf16[64,64,128]{2,1,0:T(8,128)(2,1)S(1)} %bitcast.46, bf16[9,64,64]{2,1,0:T(8,128)(2,1)S(1)} %bitcast.44, bf16[144,128]{1,0:T(8,128)(2,1)S(1)} %pad_dynamic-slice_fusion.1.row_wide, ...), custom_call_target="tpu_custom_call" | custom-call | flops 1300000000 | bytes 3500000 | tf_op jit(solution)/shard_map/tile_gradients/pallas_call | solution.py:217
  57.3 16.3 %all_to_all.20 = f32[32,16,128]{2,1,0:T(8,128)S(1)} all-to-all(f32[32,16,128]{2,1,0:T(8,128)S(1)} %get-tuple-element.8), channel_id=1, replica_groups={{0,8,16,24,32,40,48,56,128,136,144,152,160,168,176,184,256,264,272,280,..., dimensions={0} | all-to-all | bytes 524288 | tf_op jit(solution)/shard_map/all_to_all | solution.py:40
  73.7 0.1 slice_reduce_fusion.7
  73.8 0.1 slice_reduce_fusion.6
  73.9 0.1 reshape.119
  74.0 0.1 concatenate.54
  74.2 0.7 broadcast_in_dim.12
  74.9 10.4 %all-to-all-start.2 = ((bf16[16,56,128]{2,1,0:T(8,128)(2,1)}), bf16[16,56,128]{2,1,0:T(8,128)(2,1)S(1)}, u32[]{:S(2)}, u32[]{:S(2)}) async-start(bf16[16,56,128]{2,1,0:T(8,128)(2,1)} %broadcast_in_dim.12), calls=%async_computation.2 | async-start | bytes 458752 | tf_op jit(solution)/shard_map/all_to_all | solution.py:40
  85.3 13.5 %all-to-all-done.2 = bf16[16,56,128]{2,1,0:T(8,128)(2,1)S(1)} async-done(((bf16[16,56,128]{2,1,0:T(8,128)(2,1)}), bf16[16,56,128]{2,1,0:T(8,128)(2,1)S(1)}, u32[]{:S(2)}, u32[]{:S(2)}) %all-to-all-start.2) | async-done | bytes 229408 | tf_op jit(solution)/shard_map/all_to_all | solution.py:40
  98.9 0.1 fusion.1
  99.0 0.1 slice.156
  99.1 0.1 slice_reduce_fusion
  99.2 0.1 slice_reduce_fusion.3
  99.4 0.1 slice_add_fusion.1
  99.5 0.1 pad_maximum_fusion.1
  99.6 0.1 reshape.126
  99.7 0.1 fusion.3
  99.8 0.1 fusion.2
  99.9 0.1 slice.164
  100.0 0.1 slice_add_fusion.3
  100.0 0.1 pad_maximum_fusion.3
  100.2 0.1 reshape.120
  100.3 0.7 pad_maximum_fusion
  101.1 8.1 %all-to-all-start.3 = ((f32[32,16,128]{2,1,0:T(8,128)}), f32[32,16,128]{2,1,0:T(8,128)S(1)}, u32[]{:S(2)}, u32[]{:S(2)}) async-start(f32[32,16,128]{2,1,0:T(8,128)} %pad_maximum_fusion), calls=%async_computation.3 | async-start | bytes 524288 | tf_op jit(solution)/shard_map/all_to_all | solution.py:40
  109.2 0.2 copy.50
  109.4 0.2 reshape.116.w
  109.5 4.4 %tile_forward.1 = f32[64,64,128]{2,1,0:T(8,128)} custom-call(bf16[80,64,128]{2,1,0:T(8,128)(2,1)S(1)} %get-tuple-element.6.act, bf16[10,64,128]{2,1,0:T(8,128)(2,1)S(1)} %get-tuple-element.7.edge, bf16[192,192]{1,0:T(8,128)(2,1)S(1)} %reshape.116.w), custom_call_target="tpu_custom_call" | custom-call | flops 700000000 | bytes 3500000 | tf_op jit(solution)/shard_map/tile_forward/pallas_call | solution.py:263
  113.9 4.2 %all-to-all-done.3 = f32[32,16,128]{2,1,0:T(8,128)S(1)} async-done(((f32[32,16,128]{2,1,0:T(8,128)}), f32[32,16,128]{2,1,0:T(8,128)S(1)}, u32[]{:S(2)}, u32[]{:S(2)}) %all-to-all-start.3) | async-done | bytes 262176 | tf_op jit(solution)/shard_map/all_to_all | solution.py:40
  118.1 0.1 fusion
  118.2 0.1 maximum_multiply_fusion
  118.3 0.2 div.23
  118.5 0.7 copy.57
  119.2 0.7 copy.58
  (26 shorter events, 0.4 us)
Async XLA Ops:
  0.6 41.3 %copy-start.1 = (bf16[128,64,64]{0,2,1:T(8,128)(2,1)S(1)}, bf16[128,64,64]{0,2,1:T(8,128)(2,1)}, u32[]{:S(2)}) copy-start(bf16[128,64,64]{0,2,1:T(8,128)(2,1)} %param.5) | copy-start | bytes 3145732
  0.6 41.3 %copy-start = (bf16[3,3,64,64]{3,2,1,0:T(8,128)(2,1)S(1)}, bf16[3,3,64,64]{3,2,1,0:T(8,128)(2,1)}, u32[]{:S(2)}) copy-start(bf16[3,3,64,64]{3,2,1,0:T(8,128)(2,1)} %param.4) | copy-start | bytes 221188
  2.4 39.3 %all-to-all-start = ((bf16[16,128,128]{2,1,0:T(8,128)(2,1)}), bf16[16,128,128]{2,1,0:T(8,128)(2,1)S(1)}, u32[]{:S(2)}, u32[]{:S(2)}) async-start(bf16[16,128,128]{2,1,0:T(8,128)(2,1)} %broadcast_in_dim.10), calls=%async_computation | async-start | bytes 1048576 | tf_op jit(solution)/shard_map/all_to_all | solution.py:40
  74.9 23.9 %all-to-all-start.2 = ((bf16[16,56,128]{2,1,0:T(8,128)(2,1)}), bf16[16,56,128]{2,1,0:T(8,128)(2,1)S(1)}, u32[]{:S(2)}, u32[]{:S(2)}) async-start(bf16[16,56,128]{2,1,0:T(8,128)(2,1)} %broadcast_in_dim.12), calls=%async_computation.2 | async-start | bytes 458752 | tf_op jit(solution)/shard_map/all_to_all | solution.py:40
  101.1 17.0 %all-to-all-start.3 = ((f32[32,16,128]{2,1,0:T(8,128)}), f32[32,16,128]{2,1,0:T(8,128)S(1)}, u32[]{:S(2)}, u32[]{:S(2)}) async-start(f32[32,16,128]{2,1,0:T(8,128)} %pad_maximum_fusion), calls=%async_computation.3 | async-start | bytes 524288 | tf_op jit(solution)/shard_map/all_to_all | solution.py:40

commit v2 on v1

--- a/solution.py
+++ b/solution.py
@@ -36,6 +36,21 @@
 ]
 
 
+def window_pairs():
+    pairs = []
+    for row in range(ROWS):
+        for col in range(COLS):
+            x, z_lo = col // 8, col % 8
+            place = row // 2 % 2 * 4 + col % 2 * 2 + row % 2
+            source_row = col // 2
+            source_col = (row // 4 + 2) % 4 * 8 + (place - TURN[z_lo // 2]) % 8
+            pairs.append((source_row * COLS + source_col, row * COLS + col))
+    return pairs
+
+
+TURN = (0, 7, 1, 0)
+
+
 def exchange(parts, groups):
     return lax.all_to_all(parts, ("row", "col"), 0, 0, axis_index_groups=groups)
 
@@ -46,14 +61,6 @@
 G = 8
 
 
-def lanes():
-    return lax.broadcasted_iota(jnp.int32, (C, I), 1)
-
-
-def turn(x, shift):
-    return pltpu.roll(x.astype(F32), shift % I, 1).astype(x.dtype)
-
-
 def dot(a, b):
     return lax.dot_general(a, b, (((1,), (0,)), ((), ())), preferred_element_type=F32)
 
@@ -68,16 +75,14 @@
     return dot(high, picks) + dot(low, picks)
 
 
-def shifted(act, edge, jj, lane):
-    ends = turn(edge, -(16 * jj + 8))
-    wide = act.astype(F32)
-    before = jnp.where(lane < 8, ends.astype(F32), pltpu.roll(wide, 8, 1)).astype(BF16)
-    after = jnp.where(lane >= 120, ends.astype(F32), pltpu.roll(wide, I - 8, 1)).astype(BF16)
-    return jnp.concatenate([before, act, after], axis=0)
-
-
-def main_kernel(cot, w, row_wide, col_wide, ids, out, act_out, edge_out, ga, gae, gk, acc):
-    lane = lanes()
+def neighbours(value, ends, lane):
+    before = jnp.where(lane < 8, ends, pltpu.roll(value, 8, 1)).astype(BF16)
+    after = jnp.where(lane >= 120, ends, pltpu.roll(value, I - 8, 1)).astype(BF16)
+    return before, value.astype(BF16), after
+
+
+def back_kernel(cot, w, ga, gae):
+    lane = lax.broadcasted_iota(jnp.int32, (C, I), 1)
     slot = lane % 16
     weights = jnp.concatenate(
         [jnp.concatenate([w[3 * a + b] for a in range(3)], axis=1) for b in range(3)], axis=0
@@ -119,90 +124,132 @@
     def _(k):
         back(k, False)
 
-    acc[...] = jnp.zeros_like(acc)
-    gk[...] = jnp.zeros_like(gk)
-    wide = row_wide[...].astype(F32)
-    row = wide[G : G + I].T
-    ends = jnp.concatenate([wide[G + I :], wide[:G]], axis=0)
-    edge_row = jnp.concatenate([ends] * 8, axis=0).T
-    u_row, v_row = row[:C], row[C:]
-    u_edge, v_edge = edge_row[:C], edge_row[C:]
-    col_f = col_wide[...].astype(F32).T
-    col = col_f.astype(BF16)
-    has_low = (ids[0] > 0).astype(F32)
-    has_high = (ids[0] < ROWS - 1).astype(F32)
-    edge_mask = jnp.where(slot < 8, has_high, has_low)
+
+def fold8(tiles, lane):
+    for step in (16, 32, 64):
+        low = lane & step == 0
+        tiles = [
+            jnp.where(low, x, y) + pltpu.roll(jnp.where(low, y, x), step, 1)
+            for x, y in zip(tiles[::2], tiles[1::2])
+        ]
+    return tiles[0]
+
+
+def main_kernel(cot, ga, gae, own, ends, window, ids, out, act_out, edge_out, gk, acc, half, col_t):
+    step = pl.program_id(0)
+    lane = lax.broadcasted_iota(jnp.int32, (C, I), 1)
+    thin = lax.broadcasted_iota(jnp.int32, (16, I), 1)
     m0 = lax.broadcasted_iota(jnp.int32, (I, I), 0)
     m1 = lax.broadcasted_iota(jnp.int32, (I, I), 1)
 
-    def gate(x):
-        s = 0.5 + 0.5 * jnp.tanh(0.5 * x)
-        y = x * s
-        return y, s + y * (1.0 - s)
+    @pl.when(step == 0)
+    def _():
+        acc[...] = jnp.zeros_like(acc)
+        gk[...] = jnp.zeros_like(gk)
+        row, col = ids[0], ids[1]
+        block = col // 2
+        low = ends[jnp.maximum(row - 1, 0)].astype(F32)[G:]
+        high = ends[jnp.minimum(row + 1, ROWS - 1)].astype(F32)[:G]
+        edge = jnp.concatenate([high, low], axis=0)
+        half[:, :I] = own[...].astype(F32).T * 0.5
+        half[:, I:] = jnp.concatenate([edge] * 8, axis=0).T * 0.5
+        inner = window[...].astype(F32)
+        low = ends[jnp.maximum(block - 1, 0)].astype(F32)[G:]
+        high = ends[jnp.minimum(block + 1, ROWS - 1)].astype(F32)[:G]
+        wide = jnp.where(
+            col % 2 == 0, jnp.concatenate([low, inner], axis=0), jnp.concatenate([inner, high], axis=0)
+        )
+        col_t[...] = jnp.concatenate([wide, jnp.zeros((I - 80, I), F32)], axis=0).T
+
+    def gate(h):
+        t = jnp.tanh(h)
+        p = 1.0 + t
+        y = h * p
+        return y, p + y * (1.0 - t)
 
     def group(k, taps, mask):
         spread = (m0 == G * k + m1 // 16).astype(BF16)
         gather = (m1 == G * k + m0 // 16).astype(BF16)
-        here = dot(col, spread)
-        edge_on = edge_mask * mask
-        y, slope = gate(u_edge * here[:C] + (v_edge + here[C:]))
+        wide = col_t[...]
+        here = dot(wide.astype(BF16), spread)
+        edge_on = jnp.where(
+            lane % 16 < 8, (ids[0] < ROWS - 1).astype(F32), (ids[0] > 0).astype(F32)
+        )
+        if mask is not None:
+            edge_on = edge_on * mask
+        y, slope = gate(half[:C, I:] * here[:C] + (half[C:, I:] + 0.5 * here[C:]))
         edge_act = y * edge_on
-        edge_out[k] = edge_act.astype(BF16)
-        g = gae[k] * (slope * edge_on)
-        acc[4] += g * here[:C]
-        acc[5] += g
-        acc[2] += split_dot(g * u_edge, gather)
-        acc[3] += split_dot(g, gather)
-        near = pltpu.roll(col_f, (I - G * k) % I, 1)
-        stacks = []
-        for q in range(G):
-            uc, vc = near[:C, q : q + 1], near[C:, q : q + 1]
-            y, slope = gate(u_row * uc + (v_row + vc))
-            act = (y * mask).astype(BF16)
-            act_out[G * k + q] = act
-            stacks.append(shifted(act, edge_act, q, lane))
-            g = ga[G * k + q] * (slope * mask)
-            acc[0] += g * uc
-            acc[1] += g
-            here_lane = lane == G * k + q
-            acc[2] += jnp.where(here_lane, jnp.sum(g * u_row, axis=1, keepdims=True), 0.0)
-            acc[3] += jnp.where(here_lane, jnp.sum(g, axis=1, keepdims=True), 0.0)
-        acts = jnp.concatenate(stacks, axis=1)
+        edge_out[0] = edge_act.astype(BF16)
+        g_edge = gae[k] * (slope * edge_on)
+        acc[4] += g_edge * here[:C]
+        acc[5] += g_edge
+        near = pltpu.roll(wide, (I - G * k) % I, 1)
+        ends_q = [pltpu.roll(edge_act, (I - 16 * q - 8) % I, 1) for q in range(G)]
+        pieces = [[[None] * 4 for _ in range(3)] for _ in range(G)]
+        sums = []
+        for n in range(4):
+            part = slice(16 * n, 16 * n + 16)
+            u_half, v_half = half[part, :I], half[C + 16 * n : C + 16 * n + 16, :I]
+            row_u = row_v = 0.0
+            g_u, g_v = [], []
+            for q in range(G):
+                uc = near[part, q : q + 1]
+                vc = near[C + 16 * n : C + 16 * n + 16, q : q + 1] * 0.5
+                y, slope = gate(u_half * uc + (v_half + vc))
+                g = ga[q, part] * slope
+                if mask is not None:
+                    y, g = y * mask, g * mask
+                three = neighbours(y, ends_q[q][part], thin)
+                for a in range(3):
+                    pieces[q][a][n] = three[a]
+                act_out[q, part] = three[1]
+                row_u += g * uc
+                row_v += g
+                g_u.append(g * u_half)
+                g_v.append(g)
+            acc[0, part] += row_u
+            acc[1, part] += row_v
+            sums.append((fold8(g_u, thin), fold8(g_v, thin)))
+        for m, g in ((0, g_edge * half[:C, I:]), (1, g_edge)):
+            folded = jnp.concatenate([x[m] for x in sums], axis=0) + g
+            acc[2 + m] += split_dot(folded, gather)
+        acts = jnp.concatenate(
+            [jnp.concatenate([t for a in range(3) for t in pieces[q][a]], axis=0) for q in range(G)],
+            axis=1,
+        )
         cots = jnp.concatenate(
             [jnp.concatenate([cot[G * (k - b) + q] for q in range(G)], axis=1) for b in taps], axis=0
         )
         gk[:, C * taps[0] : C * (taps[-1] + 1)] += dot_lanes(acts, cots)
 
-    group(0, [0], (ids[1] > 0).astype(F32))
-    group(1, [0, 1], 1.0)
-
-    @pl.loop(2, 8)
-    def _(k):
-        group(k, [0, 1, 2], 1.0)
-
-    group(8, [1, 2], 1.0)
-    group(9, [2], (ids[1] < COLS - 1).astype(F32))
-
-    def fold(x):
+    pl.when(step == 0)(lambda: group(0, [0], (ids[1] > 0).astype(F32)))
+    pl.when(step == 1)(lambda: group(1, [0, 1], None))
+    pl.when((step > 1) & (step < 8))(lambda: group(step, [0, 1, 2], None))
+    pl.when(step == 8)(lambda: group(8, [1, 2], None))
+    pl.when(step == 9)(lambda: group(9, [2], (ids[1] < COLS - 1).astype(F32)))
+
+    def folded(x):
         x = x + pltpu.roll(x, 64, 1)
         x = x + pltpu.roll(x, 32, 1)
         return x + pltpu.roll(x, 16, 1)
 
-    big_lane = lax.broadcasted_iota(jnp.int32, (2 * C, I), 1)
-    ends = pltpu.roll(fold(jnp.concatenate([acc[4], acc[5]], axis=0)), 80, 1)
-    sums = jnp.concatenate([acc[2], acc[3]], axis=0)
-    total = gk[...]
-    rest = jnp.concatenate([total[: 2 * C, 128:160]] * 4, axis=1)
-    misc = jnp.where(big_lane < 80, sums, jnp.where(big_lane < 96, ends, rest))
-    tail = jnp.concatenate([total[128:, 128:], total[:64, 160:], total[64:128, 160:]], axis=1)
-    rows = jnp.concatenate([acc[0], acc[1]], axis=0)
-    for t in range(32):
-        if t < 24:
-            out[t, :8] = total[8 * t : 8 * t + 8, :128]
-        else:
-            out[t, :8] = tail[8 * (t - 24) : 8 * (t - 24) + 8]
-        out[t, 8:12] = rows[4 * t : 4 * t + 4]
-        out[t, 12:16] = misc[4 * t : 4 * t + 4]
+    @pl.when(step == 9)
+    def _():
+        big_lane = lax.broadcasted_iota(jnp.int32, (2 * C, I), 1)
+        outer = pltpu.roll(folded(jnp.concatenate([acc[4], acc[5]], axis=0)), 80, 1) * 0.5
+        sums = jnp.concatenate([acc[2], acc[3] * 0.5], axis=0)
+        total = gk[...]
+        rest = jnp.concatenate([total[: 2 * C, 128:160]] * 4, axis=1)
+        misc = jnp.where(big_lane < 80, sums, jnp.where(big_lane < 96, outer, rest))
+        tail = jnp.concatenate([total[128:, 128:], total[:64, 160:], total[64:128, 160:]], axis=1)
+        rows = jnp.concatenate([acc[0], acc[1]], axis=0) * 0.5
+        for t in range(32):
+            if t < 24:
+                out[t, :8] = total[8 * t : 8 * t + 8, :128]
+            else:
+                out[t, :8] = tail[8 * (t - 24) : 8 * (t - 24) + 8]
+            out[t, 8:12] = rows[4 * t : 4 * t + 4]
+            out[t, 12:16] = misc[4 * t : 4 * t + 4]
 
 
 def whole(shape, dtype):
@@ -213,34 +260,52 @@
 SMEM = pl.BlockSpec(memory_space=pltpu.SMEM)
 
 
-def run_main(cot, w, row_wide, col_wide, ids):
+def run_back(cot, w):
+    return pl.pallas_call(
+        back_kernel,
+        out_shape=(whole((80, C, I), F32), whole((10, C, I), F32)),
+        in_specs=[VMEM] * 2,
+        out_specs=(VMEM, VMEM),
+        compiler_params=pltpu.CompilerParams(vmem_limit_bytes=40 * 2**20),
+        cost_estimate=pl.CostEstimate(flops=2_400_000_000, bytes_accessed=4_000_000, transcendentals=0),
+        name="tile_back",
+    )(cot, w)
+
+
+def run_main(cot, ga, gae, own, ends, window, ids):
+    def group(shape):
+        return pl.BlockSpec((shape, C, I), lambda k: (k, 0, 0))
+
     return pl.pallas_call(
         main_kernel,
+        grid=(10,),
         out_shape=(whole((32, 16, I), F32), whole((80, C, I), BF16), whole((10, C, I), BF16)),
-        in_specs=[VMEM] * 4 + [SMEM],
-        out_specs=(VMEM, VMEM, VMEM),
+        in_specs=[VMEM, group(G), VMEM, VMEM, VMEM, VMEM, SMEM],
+        out_specs=(VMEM, group(G), group(1)),
         scratch_shapes=[
-            pltpu.VMEM((80, C, I), F32),
-            pltpu.VMEM((10, C, I), F32),
             pltpu.VMEM((192, 192), F32),
             pltpu.VMEM((6, C, I), F32),
+            pltpu.VMEM((2 * C, 2 * I), F32),
+            pltpu.VMEM((2 * C, I), F32),
         ],
         compiler_params=pltpu.CompilerParams(vmem_limit_bytes=40 * 2**20),
-        cost_estimate=pl.CostEstimate(flops=1_300_000_000, bytes_accessed=3_500_000, transcendentals=700_000),
+        cost_estimate=pl.CostEstimate(flops=1_300_000_000, bytes_accessed=6_000_000, transcendentals=700_000),
         name="tile_gradients",
-    )(cot, w, row_wide, col_wide, ids)
+    )(cot, ga, gae, own, ends, window, ids)
 
 
 def forward_kernel(act, edge, w, out):
-    lane = lanes()
+    lane = lax.broadcasted_iota(jnp.int32, (C, I), 1)
     weights = w[...]
 
     def group(k, taps):
         edge_act = edge[k].astype(F32)
         for p in range(0, G, 2):
-            stack = jnp.concatenate(
-                [shifted(act[G * k + q], edge_act, q, lane) for q in (p, p + 1)], axis=1
-            )
+            stacks = []
+            for q in (p, p + 1):
+                ends = pltpu.roll(edge_act, (I - 16 * q - 8) % I, 1)
+                stacks.append(jnp.concatenate(neighbours(act[G * k + q].astype(F32), ends, lane), axis=0))
+            stack = jnp.concatenate(stacks, axis=1)
             part = dot(weights[C * taps[0] : C * (taps[-1] + 1)], stack)
             for n, b in enumerate(taps):
                 for h, q in enumerate((p, p + 1)):
@@ -325,14 +390,15 @@
     bin_count = rows_local * ROWS
     row_id = lax.axis_index("row")
     col_id = lax.axis_index("col")
-    everyone = exchange(jnp.broadcast_to(embedding[None], (ROWS,) + embedding.shape), ROW_GROUPS)
-    everyone = jnp.pad(everyone.reshape(bin_count, 2 * C), ((G, I), (0, 0)))
-    row_wide = lax.dynamic_slice_in_dim(everyone, row_id * rows_local, rows_local + 2 * G, 0)
-    col_wide = lax.dynamic_slice_in_dim(everyone, col_id * J, I, 0)
+    place = (col_id % 8 + sum(jnp.where(row_id % 4 == n, turn, 0) for n, turn in enumerate(TURN))) % 8
+    mine = lax.dynamic_slice_in_dim(embedding, place // 2 % 2 * (J - G), J + G, 0)
+    window = lax.ppermute(mine, ("row", "col"), window_pairs())
+    ends = jnp.concatenate([embedding[:G], embedding[rows_local - G :]], axis=0)
+    ends = exchange(jnp.broadcast_to(ends[None], (ROWS,) + ends.shape), ROW_GROUPS)
     ids = jnp.stack([row_id, col_id])
-    parts, act, edge = run_main(
-        cotangent.transpose(1, 2, 0), kernel.reshape(9, C, C), row_wide, col_wide, ids
-    )
+    cot = cotangent.transpose(1, 2, 0)
+    ga, gae = run_back(cot, kernel.reshape(9, C, C))
+    parts, act, edge = run_main(cot, ga, gae, embedding, ends, window, ids)
     taps = kernel.transpose(1, 3, 0, 2).reshape(192, 192)
     prediction = run_forward(act, edge, taps).transpose(2, 0, 1)
     gk, ge = reduce_all(parts, row_id // 2 % 2)

time: 120 us -> 103 us (0.86)
  waiting for transfers between devices: 40.7 us -> 20.8 us
  local copies, waits for them, and re-layouts: 5.58 us -> 11.1 us
  blocking collectives: 16.3 us -> 12.1 us
  starting transfers between devices: 34.8 us -> 37.5 us
  Pallas kernels: 19.7 us -> 17.7 us
    all_to_all x3, waiting for transfers between devices: 40.7 us -> 20.8 us  [exchange(): return lax.all_to_all(parts, ('row', 'col'), 0, 0, axis_index_groups=groups)]
    ppermute x0 -> x1, starting transfers between devices: none -> 17.6 us  [on_device(): window = lax.ppermute(mine, ('row', 'col'), window_pairs())]
    all_to_all x3, starting transfers between devices: 34.8 us -> 19.9 us  [exchange(): return lax.all_to_all(parts, ('row', 'col'), 0, 0, axis_index_groups=groups)]
    unnamed x6 -> x16, local copies, waits for them, and re-layouts: 1.48 us -> 6.85 us
    all_to_all x1, blocking collectives: 16.3 us -> 12.1 us  [exchange(): return lax.all_to_all(parts, ('row', 'col'), 0, 0, axis_index_groups=groups)]
    pallas_call x1 -> x2, Pallas kernels: 15.3 us -> 13.4 us  [the longest x1 10.4 us: run_main(): pl.pallas_call(main_kernel, grid=(10,), out_shape=(whole((32, 16, I), F32...]
  transfers between devices with their start and end apart: 3 -> 4, of which waited for: 3 -> 3; matrix products, arithmetic and copies ran while one was open for 0% -> 2% of each run, Pallas kernels for 4% -> 7%
where the time goes in v2:
time: 103 us; the launch traced here: 102 us
  starting transfers between devices  37.5 us (36%)
  waiting for transfers between devices  20.8 us (20%)
  Pallas kernels  17.7 us (17%)
  blocking collectives  12.1 us (12%)
  local copies, waits for them, and re-layouts  11.1 us (11%)
  other arithmetic  1.92 us (2%)
  between operations  1.03 us (1%)
    all_to_all x3, waiting for transfers between devices, exchange(): return lax.all_to_all(parts, ('row', 'col'), 0, 0, axis_index_groups=groups)  20.8 us
    all_to_all x3, starting transfers between devices, exchange(): return lax.all_to_all(parts, ('row', 'col'), 0, 0, axis_index_groups=groups)  19.9 us
    ppermute x1, starting transfers between devices, on_device(): window = lax.ppermute(mine, ('row', 'col'), window_pairs())  17.6 us
    all_to_all x1, blocking collectives, exchange(): return lax.all_to_all(parts, ('row', 'col'), 0, 0, axis_index_groups=groups)  12.1 us
    pallas_call x1, Pallas kernels, run_main(): pl.pallas_call(main_kernel, grid=(10,), out_shape=(whole((32, 16, I), F32...  10.4 us
    unnamed x16, local copies, waits for them, and re-layouts  6.85 us
    pallas_call x1, Pallas kernels, run_forward(): pl.pallas_call(forward_kernel, out_shape=whole((J, C, I), F32), in_specs=...  4.35 us
    pallas_call x1, Pallas kernels, run_back(): pl.pallas_call(back_kernel, out_shape=(whole((80, C, I), F32), whole((10,...  2.94 us
  transfers between devices with their start and end apart: 4, of which 3 were waited for; matrix products, arithmetic and copies ran while one was open for 2% of the time, Pallas kernels for 7%

profile of v2, /device:TPU:1, one launch (start us, length us, event | category | flops | bytes accessed | tf_op | source)
XLA Modules:
  0.0 102.2 jit_solution(12360523087031984580)
XLA Ops:
  0.7 0.7 constant_dynamic-slice_fusion.1
  1.4 17.6 %collective-permute-start = (bf16[72,128]{1,0:T(8,128)(2,1)S(1)}, bf16[72,128]{1,0:T(8,128)(2,1)S(1)}, u32[]{:S(2)}, u32[]{:S(2)}) collective-permute-start(bf16[72,128]{1,0:T(8,128)(2,1)S(1)} %constant_dynamic-slice_fusion.1), channel_id=1, source_target_pairs={{16,0},{18,1},{49,2},{51,3},{87,4},{81,5},{112,6},{114,7},{144,8},... | collective-permute-start | bytes 55304 | tf_op jit(solution)/shard_map/ppermute | solution.py:395
  19.0 0.7 fusion.3
  19.7 0.6 broadcast_in_dim.10
  20.4 4.4 %all-to-all-start = ((bf16[16,16,128]{2,1,0:T(8,128)(2,1)}), bf16[16,16,128]{2,1,0:T(8,128)(2,1)S(1)}, u32[]{:S(2)}, u32[]{:S(2)}) async-start(bf16[16,16,128]{2,1,0:T(8,128)(2,1)} %broadcast_in_dim.10), calls=%async_computation | async-start | bytes 131072 | tf_op jit(solution)/shard_map/all_to_all | solution.py:55
  24.8 0.0 copy-start
  24.8 0.9 copy-done
  25.7 0.0 copy-start.3
  25.7 1.2 %copy-done.3 = bf16[128,64,64]{0,2,1:T(8,128)(2,1)S(1)} copy-done((bf16[128,64,64]{0,2,1:T(8,128)(2,1)S(1)}, bf16[128,64,64]{0,2,1:T(8,128)(2,1)}, u32[]{:S(2)}) %copy-start.3) | copy-done | bytes 1048600
  26.9 0.0 copy-start.2
  26.9 0.0 copy-start.4
  26.9 2.9 %tile_back.1 = (f32[80,64,128]{2,1,0:T(8,128)S(1)}, f32[10,64,128]{2,1,0:T(8,128)S(1)}) custom-call(bf16[64,64,128]{2,1,0:T(8,128)(2,1)S(1)} %bitcast.45, bf16[9,64,64]{2,1,0:T(8,128)(2,1)S(1)} %bitcast.43), custom_call_target="tpu_custom_call" | custom-call | flops 2400000000 | bytes 4000000 | tf_op jit(solution)/shard_map/tile_back/pallas_call | solution.py:264
  29.9 0.0 copy-start.5
  29.9 1.5 %copy-done.5 = f32[80,64,128]{2,1,0:T(8,128)} copy-done((f32[80,64,128]{2,1,0:T(8,128)}, f32[80,64,128]{2,1,0:T(8,128)S(1)}, u32[]{:S(2)}) %copy-start.5) | copy-done | bytes 2621464
  31.4 0.1 pad_add_fusion.ids
  31.5 0.0 collective-permute-done.window
  31.5 3.1 %all-to-all-done.ends = bf16[16,16,128]{2,1,0:T(8,128)(2,1)S(1)} async-done(((bf16[16,16,128]{2,1,0:T(8,128)(2,1)}), bf16[16,16,128]{2,1,0:T(8,128)(2,1)S(1)}, u32[]{:S(2)}, u32[]{:S(2)}) %all-to-all-start) | async-done | bytes 65568 | tf_op jit(solution)/shard_map/all_to_all | solution.py:55
  34.5 0.0 copy-done.2
  34.5 0.0 copy-done.4
  34.5 0.0 copy-start.6
  34.5 1.7 %copy-done.6 = f32[80,64,128]{2,1,0:T(8,128)S(1)} copy-done((f32[80,64,128]{2,1,0:T(8,128)S(1)}, f32[80,64,128]{2,1,0:T(8,128)}, u32[]{:S(2)}) %copy-start.6) | copy-done | bytes 2621464
  36.3 10.4 %tile_gradients.1 = (f32[32,16,128]{2,1,0:T(8,128)S(1)}, bf16[80,64,128]{2,1,0:T(8,128)(2,1)S(1)}, bf16[10,64,128]{2,1,0:T(8,128)(2,1)S(1)}) custom-call(bf16[64,64,128]{2,1,0:T(8,128)(2,1)S(1)} %bitcast.46, f32[80,64,128]{2,1,0:T(8,128)S(1)} %copy-done.6, f32[10,64,128]{2,1,0:T(8,128)S(1)} %get-tuple-element.9.gae, bf16[128,128]{1,0:T(8,128)(2,1)S(1)} %copy-done.2, ...), custom_call_target="tpu_custom_call" | custom-call | flops 1300000000 | bytes 6000000 | tf_op jit(solution)/shard_map/tile_gradients/pallas_call | solution.py:279
  46.7 12.1 %all_to_all.20 = f32[32,16,128]{2,1,0:T(8,128)S(1)} all-to-all(f32[32,16,128]{2,1,0:T(8,128)S(1)} %get-tuple-element.12), channel_id=1, replica_groups={{0,8,16,24,32,40,48,56,128,136,144,152,160,168,176,184,256,264,272,280,..., dimensions={0} | all-to-all | bytes 524288 | tf_op jit(solution)/shard_map/all_to_all | solution.py:55
  58.8 0.1 slice_reduce_fusion.7
  59.0 0.1 slice_reduce_fusion.6
  59.1 0.1 reshape.115
  59.2 0.1 concatenate.58
  59.3 0.7 broadcast_in_dim.12
  60.1 7.4 %all-to-all-start.2 = ((bf16[16,56,128]{2,1,0:T(8,128)(2,1)}), bf16[16,56,128]{2,1,0:T(8,128)(2,1)S(1)}, u32[]{:S(2)}, u32[]{:S(2)}) async-start(bf16[16,56,128]{2,1,0:T(8,128)(2,1)} %broadcast_in_dim.12), calls=%async_computation.2 | async-start | bytes 458752 | tf_op jit(solution)/shard_map/all_to_all | solution.py:55
  67.5 13.5 %all-to-all-done.2 = bf16[16,56,128]{2,1,0:T(8,128)(2,1)S(1)} async-done(((bf16[16,56,128]{2,1,0:T(8,128)(2,1)}), bf16[16,56,128]{2,1,0:T(8,128)(2,1)S(1)}, u32[]{:S(2)}, u32[]{:S(2)}) %all-to-all-start.2) | async-done | bytes 229408 | tf_op jit(solution)/shard_map/all_to_all | solution.py:55
  81.0 0.1 slice_reduce_fusion.3
  81.2 0.1 slice_reduce_fusion
  81.3 0.0 copy-start.1
  81.4 0.1 fusion.1
  81.4 0.1 slice.164
  81.5 0.1 reshape.116
  81.6 0.1 fusion.4
  81.7 0.1 fusion.2
  81.8 0.1 slice_add_fusion.1
  81.9 0.1 pad_maximum_fusion.1
  82.0 0.1 reshape.122
  82.1 0.1 slice.172
  82.2 0.1 slice_add_fusion.3
  82.3 0.1 pad_maximum_fusion.3
  82.5 0.7 pad_maximum_fusion
  83.3 8.1 %all-to-all-start.3 = ((f32[32,16,128]{2,1,0:T(8,128)}), f32[32,16,128]{2,1,0:T(8,128)S(1)}, u32[]{:S(2)}, u32[]{:S(2)}) async-start(f32[32,16,128]{2,1,0:T(8,128)} %pad_maximum_fusion), calls=%async_computation.3 | async-start | bytes 524288 | tf_op jit(solution)/shard_map/all_to_all | solution.py:55
  91.4 0.0 copy-done.1
  91.4 0.2 copy.50
  91.6 0.2 reshape.112.w
  91.7 4.4 %tile_forward.1 = f32[64,64,128]{2,1,0:T(8,128)} custom-call(bf16[80,64,128]{2,1,0:T(8,128)(2,1)S(1)} %get-tuple-element.10.act, bf16[10,64,128]{2,1,0:T(8,128)(2,1)S(1)} %get-tuple-element.11.edge, bf16[192,192]{1,0:T(8,128)(2,1)S(1)} %reshape.112.w), custom_call_target="tpu_custom_call" | custom-call | flops 700000000 | bytes 3500000 | tf_op jit(solution)/shard_map/tile_forward/pallas_call | solution.py:328
  96.1 4.2 %all-to-all-done.3 = f32[32,16,128]{2,1,0:T(8,128)S(1)} async-done(((f32[32,16,128]{2,1,0:T(8,128)}), f32[32,16,128]{2,1,0:T(8,128)S(1)}, u32[]{:S(2)}, u32[]{:S(2)}) %all-to-all-start.3) | async-done | bytes 262176 | tf_op jit(solution)/shard_map/all_to_all | solution.py:55
  100.3 0.1 fusion
  100.4 0.1 maximum_multiply_fusion
  100.5 0.2 div.33
  100.7 0.7 copy.57
  101.4 0.7 copy.58
  (27 shorter events, 0.4 us)
Async XLA Ops:
  1.4 30.0 %collective-permute-start = (bf16[72,128]{1,0:T(8,128)(2,1)S(1)}, bf16[72,128]{1,0:T(8,128)(2,1)S(1)}, u32[]{:S(2)}, u32[]{:S(2)}) collective-permute-start(bf16[72,128]{1,0:T(8,128)(2,1)S(1)} %constant_dynamic-slice_fusion.1), channel_id=1, source_target_pairs={{16,0},{18,1},{49,2},{51,3},{87,4},{81,5},{112,6},{114,7},{144,8},... | collective-permute-start | bytes 55304 | tf_op jit(solution)/shard_map/ppermute | solution.py:395
  20.4 14.2 %all-to-all-start = ((bf16[16,16,128]{2,1,0:T(8,128)(2,1)}), bf16[16,16,128]{2,1,0:T(8,128)(2,1)S(1)}, u32[]{:S(2)}, u32[]{:S(2)}) async-start(bf16[16,16,128]{2,1,0:T(8,128)(2,1)} %broadcast_in_dim.10), calls=%async_computation | async-start | bytes 131072 | tf_op jit(solution)/shard_map/all_to_all | solution.py:55
  24.8 0.9 copy-start
  25.7 1.2 %copy-start.3 = (bf16[128,64,64]{0,2,1:T(8,128)(2,1)S(1)}, bf16[128,64,64]{0,2,1:T(8,128)(2,1)}, u32[]{:S(2)}) copy-start(bf16[128,64,64]{0,2,1:T(8,128)(2,1)} %param.5) | copy-start | bytes 3145732
  26.9 7.6 %copy-start.2 = (bf16[128,128]{1,0:T(8,128)(2,1)S(1)}, bf16[128,128]{1,0:T(8,128)(2,1)}, u32[]{:S(2)}) copy-start(bf16[128,128]{1,0:T(8,128)(2,1)} %own.1) | copy-start | bytes 98308
  26.9 7.6 %copy-start.4 = (bf16[128,64,64]{0,2,1:T(8,128)(2,1)S(1)}, bf16[128,64,64]{0,2,1:T(8,128)(2,1)}, u32[]{:S(2)}) copy-start(bf16[128,64,64]{0,2,1:T(8,128)(2,1)} %param.5) | copy-start | bytes 3145732
  29.9 1.5 %copy-start.5 = (f32[80,64,128]{2,1,0:T(8,128)}, f32[80,64,128]{2,1,0:T(8,128)S(1)}, u32[]{:S(2)}) copy-start(f32[80,64,128]{2,1,0:T(8,128)S(1)} %get-tuple-element.8.ga) | copy-start | bytes 7864324
  34.5 1.7 %copy-start.6 = (f32[80,64,128]{2,1,0:T(8,128)S(1)}, f32[80,64,128]{2,1,0:T(8,128)}, u32[]{:S(2)}) copy-start(f32[80,64,128]{2,1,0:T(8,128)} %copy-done.5) | copy-start | bytes 7864324
  60.1 21.0 %all-to-all-start.2 = ((bf16[16,56,128]{2,1,0:T(8,128)(2,1)}), bf16[16,56,128]{2,1,0:T(8,128)(2,1)S(1)}, u32[]{:S(2)}, u32[]{:S(2)}) async-start(bf16[16,56,128]{2,1,0:T(8,128)(2,1)} %broadcast_in_dim.12), calls=%async_computation.2 | async-start | bytes 458752 | tf_op jit(solution)/shard_map/all_to_all | solution.py:55
  81.3 10.1 %copy-start.1 = (bf16[3,3,64,64]{3,2,1,0:T(8,128)(2,1)S(1)}, bf16[3,3,64,64]{3,2,1,0:T(8,128)(2,1)}, u32[]{:S(2)}) copy-start(bf16[3,3,64,64]{3,2,1,0:T(8,128)(2,1)} %param.4) | copy-start | bytes 221188
  83.3 17.0 %all-to-all-start.3 = ((f32[32,16,128]{2,1,0:T(8,128)}), f32[32,16,128]{2,1,0:T(8,128)S(1)}, u32[]{:S(2)}, u32[]{:S(2)}) async-start(f32[32,16,128]{2,1,0:T(8,128)} %pad_maximum_fusion), calls=%async_computation.3 | async-start | bytes 524288 | tf_op jit(solution)/shard_map/all_to_all | solution.py:55

commit v3 on v2

v3 whole, which is shorter than its diff:
```python
import jax
import jax.numpy as jnp
from jax import lax
from jax.experimental import pallas as pl
from jax.experimental.pallas import tpu as pltpu
from jax.sharding import PartitionSpec as P

BF16 = jnp.bfloat16
F32 = jnp.float32

ROWS, COLS = 16, 32


def device_id(y, z_hi, core, x, z_lo):
    return (y * 4 + z_hi * 2 + core) * COLS + x * 8 + z_lo


PLANE_GROUPS = [
    [device_id(y, zh, k, x, zl) for k in range(2) for y in range(4) for x in range(4)]
    for zh in range(2)
    for zl in range(8)
]
LINE_GROUPS = [
    [device_id(y, zh, k, x, zl) for zh in range(2) for zl in range(8)]
    for y in range(4)
    for k in range(2)
    for x in range(4)
]
ROW_GROUPS = [
    [
        device_id(r // 4, r // 2 % 2, r % 2, x, (zl + 4 * (r // 2 % 2)) % 8)
        for r in range(ROWS)
    ]
    for x in range(4)
    for zl in range(8)
]


def window_pairs():
    pairs = []
    for row in range(ROWS):
        for col in range(COLS):
            x, z_lo = col // 8, col % 8
            place = row // 2 % 2 * 4 + col % 2 * 2 + row % 2
            source_row = col // 2
            source_col = (row // 4 + 2) % 4 * 8 + (place - TURN[z_lo // 2]) % 8
            pairs.append((source_row * COLS + source_col, row * COLS + col))
    return pairs


TURN = (0, 7, 1, 0)


def exchange(parts, groups):
    return lax.all_to_all(parts, ("row", "col"), 0, 0, axis_index_groups=groups)


C = 64
I = 128
J = 64
G = 8


def dot(a, b):
    return lax.dot_general(a, b, (((1,), (0,)), ((), ())), preferred_element_type=F32)


def dot_lanes(a, b):
    return lax.dot_general(a, b, (((1,), (1,)), ((), ())), preferred_element_type=F32)


def split_dot(x, picks):
    high = x.astype(BF16)
    low = (x - high.astype(F32)).astype(BF16)
    return dot(high, picks) + dot(low, picks)


def neighbours(value, ends, lane):
    before = jnp.where(lane < 8, ends, pltpu.roll(value, 8, 1))
    after = jnp.where(lane >= 120, ends, pltpu.roll(value, I - 8, 1))
    return before, value, after


def back_kernel(cot, w, ga, gae):
    lane = lax.broadcasted_iota(jnp.int32, (C, I), 1)
    slot = lane % 16
    weights = jnp.concatenate(
        [jnp.concatenate([w[3 * a + b] for a in range(3)], axis=1) for b in range(3)], axis=0
    )
    edge_weights = jnp.concatenate(
        [jnp.concatenate([w[b], w[6 + b]], axis=1) for b in range(3)], axis=0
    )

    def put(ref, place, value, fresh):
        ref[place] = value if fresh else ref[place] + value

    def back(k, first):
        fresh = [first, first, True]
        packed = jnp.zeros((C, I), F32)
        for p in range(0, G, 2):
            stacks = []
            for q in (p, p + 1):
                x = cot[G * k + q]
                wide = x.astype(F32)
                later = jnp.where(lane < 120, pltpu.roll(wide, I - 8, 1), 0.0).astype(BF16)
                earlier = jnp.where(lane >= 8, pltpu.roll(wide, 8, 1), 0.0).astype(BF16)
                stacks.append(jnp.concatenate([later, x, earlier], axis=0))
                packed = jnp.where(lane // 16 == q, pltpu.roll(wide, (16 * q + 8) % I, 1), packed)
            part = dot(weights, jnp.concatenate(stacks, axis=1))
            for b in range(3):
                for n, q in enumerate((p, p + 1)):
                    value = part[C * b : C * b + C, I * n : I * n + I]
                    put(ga, G * (k + b) + q, value, fresh[b])
        both = jnp.concatenate(
            [jnp.where(slot >= 8, packed, 0.0), jnp.where(slot < 8, packed, 0.0)], axis=0
        ).astype(BF16)
        part = dot(edge_weights, both)
        for b in range(3):
            put(gae, k + b, part[C * b : C * b + C], fresh[b])

    back(0, True)

    @pl.loop(1, 8)
    def _(k):
        back(k, False)


def fold8(tiles, lane):
    for step in (16, 32, 64):
        low = lane & step == 0
        tiles = [
            jnp.where(low, x, y) + pltpu.roll(jnp.where(low, y, x), step, 1)
            for x, y in zip(tiles[::2], tiles[1::2])
        ]
    return tiles[0]


def main_kernel(
    cot, ga, gae, own, ends, window, ids, out, act_out, edge_out, gk, acc, half, col_t, expand
):
    lane = lax.broadcasted_iota(jnp.int32, (C, I), 1)
    thin = lax.broadcasted_iota(jnp.int32, (16, I), 1)
    m0 = lax.broadcasted_iota(jnp.int32, (I, I), 0)
    m1 = lax.broadcasted_iota(jnp.int32, (I, I), 1)
    acc[...] = jnp.zeros_like(acc)
    gk[...] = jnp.zeros_like(gk)
    for q in range(G):
        expand[:, I * q : I * q + I] = (m0 == q).astype(BF16)
    row, col = ids[0], ids[1]
    block = col // 2
    low = ends[jnp.maximum(row - 1, 0)].astype(F32)[G:]
    high = ends[jnp.minimum(row + 1, ROWS - 1)].astype(F32)[:G]
    edge = jnp.concatenate([high, low], axis=0)
    half[:, :I] = own[...].astype(F32).T * 0.5
    half[:, I:] = jnp.concatenate([edge] * 8, axis=0).T * 0.5
    inner = window[...].astype(F32)
    low = ends[jnp.maximum(block - 1, 0)].astype(F32)[G:]
    high = ends[jnp.minimum(block + 1, ROWS - 1)].astype(F32)[:G]
    wide = jnp.where(
        col % 2 == 0, jnp.concatenate([low, inner], axis=0), jnp.concatenate([inner, high], axis=0)
    )
    col_t[...] = jnp.concatenate([wide, jnp.zeros((I - 80, I), F32)], axis=0).T

    def gate(h):
        t = jnp.tanh(h)
        p = 1.0 + t
        y = h * p
        return y, p + y * (1.0 - t)

    def group(k, taps, mask):
        spread = (m0 == G * k + m1 // 16).astype(BF16)
        gather = (m1 == G * k + m0 // 16).astype(BF16)
        wide = col_t[...]
        here = dot(wide.astype(BF16), spread)
        edge_on = jnp.where(
            lane % 16 < 8, (ids[0] < ROWS - 1).astype(F32), (ids[0] > 0).astype(F32)
        )
        if mask is not None:
            edge_on = edge_on * mask
        y, slope = gate(half[:C, I:] * here[:C] + (half[C:, I:] + 0.5 * here[C:]))
        edge_act = y * edge_on
        edge_act = edge_act.astype(BF16)
        edge_out[k] = edge_act
        g_edge = gae[k] * (slope * edge_on)
        acc[4] += g_edge * here[:C]
        acc[5] += g_edge
        near = pltpu.roll(wide, (I - G * k) % I, 1)
        near = jnp.concatenate([near[:C], near[C:] * 0.5], axis=0).astype(BF16)
        near = dot(near, expand[...])
        ends_q = [pltpu.roll(edge_act, (I - 16 * q - 8) % I, 1) for q in range(G)]
        pieces = [[[None] * 4 for _ in range(3)] for _ in range(G)]
        sums = []
        for n in range(4):
            part = slice(16 * n, 16 * n + 16)
            u_half, v_half = half[part, :I], half[C + 16 * n : C + 16 * n + 16, :I]
            row_u = row_v = 0.0
            g_u, g_v = [], []
            for q in range(G):
                uc = near[part, I * q : I * q + I]
                vc = near[C + 16 * n : C + 16 * n + 16, I * q : I * q + I]
                y, slope = gate(u_half * uc + (v_half + vc))
                g = ga[G * k + q, part] * slope
                if mask is not None:
                    y, g = y * mask, g * mask
                three = neighbours(y.astype(BF16), ends_q[q][part], thin)
                for a in range(3):
                    pieces[q][a][n] = three[a]
                act_out[G * k + q, part] = three[1]
                row_u += g * uc
                row_v += g
                g_u.append(g * u_half)
                g_v.append(g)
            acc[0, part] += row_u
            acc[1, part] += row_v
            sums.append((fold8(g_u, thin), fold8(g_v, thin)))
        for m, g in ((0, g_edge * half[:C, I:]), (1, g_edge)):
            folded = jnp.concatenate([x[m] for x in sums], axis=0) + g
            acc[2 + m] += split_dot(folded, gather)
        acts = jnp.concatenate(
            [jnp.concatenate([t for a in range(3) for t in pieces[q][a]], axis=0) for q in range(G)],
            axis=1,
        )
        cots = jnp.concatenate(
            [jnp.concatenate([cot[G * (k - b) + q] for q in range(G)], axis=1) for b in taps], axis=0
        )
        gk[:, C * taps[0] : C * (taps[-1] + 1)] += dot_lanes(acts, cots)

    group(0, [0], (col > 0).astype(F32))
    group(1, [0, 1], None)

    @pl.loop(2, 8)
    def _(k):
        group(k, [0, 1, 2], None)

    group(8, [1, 2], None)
    group(9, [2], (col < COLS - 1).astype(F32))

    def folded(x):
        x = x + pltpu.roll(x, 64, 1)
        x = x + pltpu.roll(x, 32, 1)
        return x + pltpu.roll(x, 16, 1)

    big_lane = lax.broadcasted_iota(jnp.int32, (2 * C, I), 1)
    outer = pltpu.roll(folded(jnp.concatenate([acc[4], acc[5]], axis=0)), 80, 1) * 0.5
    sums = jnp.concatenate([acc[2], acc[3] * 0.5], axis=0)
    total = gk[...]
    rest = jnp.concatenate([total[: 2 * C, 128:160]] * 4, axis=1)
    misc = jnp.where(big_lane < 80, sums, jnp.where(big_lane < 96, outer, rest))
    tail = jnp.concatenate([total[128:, 128:], total[:64, 160:], total[64:128, 160:]], axis=1)
    rows = jnp.concatenate([acc[0], acc[1]], axis=0) * 0.5
    for t in range(32):
        if t < 24:
            out[t, :8] = total[8 * t : 8 * t + 8, :128]
        else:
            out[t, :8] = tail[8 * (t - 24) : 8 * (t - 24) + 8]
        out[t, 8:12] = rows[4 * t : 4 * t + 4]
        out[t, 12:16] = misc[4 * t : 4 * t + 4]


def whole(shape, dtype):
    return jax.ShapeDtypeStruct(shape, dtype)


VMEM = pl.BlockSpec(memory_space=pltpu.VMEM)
SMEM = pl.BlockSpec(memory_space=pltpu.SMEM)


def run_back(cot, w):
    return pl.pallas_call(
        back_kernel,
        out_shape=(whole((80, C, I), F32), whole((10, C, I), F32)),
        in_specs=[VMEM, VMEM],
        out_specs=(VMEM, VMEM),
        compiler_params=pltpu.CompilerParams(vmem_limit_bytes=12 * 2**20),
        cost_estimate=pl.CostEstimate(flops=2_400_000_000, bytes_accessed=4_000_000, transcendentals=0),
        name="tile_back",
    )(cot, w)


def run_main(cot, ga, gae, own, ends, window, ids):
    return pl.pallas_call(
        main_kernel,
        out_shape=(whole((32, 16, I), F32), whole((80, C, I), BF16), whole((10, C, I), BF16)),
        in_specs=[VMEM] * 6 + [SMEM],
        out_specs=(VMEM, VMEM, VMEM),
        scratch_shapes=[
            pltpu.VMEM((192, 192), F32),
            pltpu.VMEM((6, C, I), F32),
            pltpu.VMEM((2 * C, 2 * I), F32),
            pltpu.VMEM((2 * C, I), F32),
            pltpu.VMEM((I, G * I), BF16),
        ],
        compiler_params=pltpu.CompilerParams(vmem_limit_bytes=12 * 2**20),
        cost_estimate=pl.CostEstimate(flops=1_300_000_000, bytes_accessed=6_000_000, transcendentals=700_000),
        name="tile_gradients",
    )(cot, ga, gae, own, ends, window, ids)


def forward_kernel(act, edge, w, out):
    lane = lax.broadcasted_iota(jnp.int32, (C, I), 1)
    weights = w[...]

    def group(k, taps):
        edge_act = edge[k]
        for p in range(0, G, 2):
            stacks = []
            for q in (p, p + 1):
                ends = pltpu.roll(edge_act, (I - 16 * q - 8) % I, 1)
                stacks.append(jnp.concatenate(neighbours(act[G * k + q], ends, lane), axis=0))
            stack = jnp.concatenate(stacks, axis=1)
            part = dot(weights[C * taps[0] : C * (taps[-1] + 1)], stack)
            for n, b in enumerate(taps):
                for h, q in enumerate((p, p + 1)):
                    value = part[C * n : C * n + C, I * h : I * h + I]
                    place = G * (k - b) + q
                    out[place] = value if b == 0 else out[place] + value

    group(0, [0])
    group(1, [0, 1])

    @pl.loop(2, 8)
    def _(k):
        group(k, [0, 1, 2])

    group(8, [1, 2])
    group(9, [2])


def run_forward(act, edge, w):
    return pl.pallas_call(
        forward_kernel,
        out_shape=whole((J, C, I), F32),
        in_specs=[VMEM] * 3,
        out_specs=VMEM,
        compiler_params=pltpu.CompilerParams(vmem_limit_bytes=40 * 2**20),
        cost_estimate=pl.CostEstimate(flops=700_000_000, bytes_accessed=3_500_000, transcendentals=0),
        name="tile_forward",
    )(act, edge, w)


def swap_rows(x):
    return pltpu.roll(x, 4, 0)


def share_kernel(got, out):
    lane = lax.broadcasted_iota(jnp.int32, (8, I), 1)
    low = lax.broadcasted_iota(jnp.int32, (8, I), 0) < 4
    by_row = [sum(got[4 * m + x, 8:16] for x in range(4)) for m in range(8)]
    by_col = [sum(got[4 * m + x, 8:16] for m in range(8)) for x in range(4)]
    weights = sum(got[t, :8] for t in range(32))
    rest = sum(by_col)
    tails = []
    for x in range(4):
        tail = jnp.where(lane < 80, by_col[x], by_row[x])
        tail = jnp.where(lane < 96, tail, pltpu.roll(by_row[4 + x], 16, 1))
        tails.append(jnp.where(lane < 112, tail, pltpu.roll(rest, 16, 1) if x == 0 else rest))
    rows = [jnp.where(low, by_row[m], swap_rows(by_row[m + 1])) for m in range(0, 8, 2)]
    rows += [jnp.where(low, swap_rows(tails[x]), tails[x + 1]) for x in (0, 2)]
    share = jnp.concatenate(rows + [weights], axis=0).astype(BF16)
    for z in range(16):
        out[z] = share


def finish_kernel(got, ids, out):
    lane = lax.broadcasted_iota(jnp.int32, (16, I), 1)
    part = lax.broadcasted_iota(jnp.int32, (16, I), 0)
    first, last = lane < 8, lane >= 120
    z_hi = ids[0] // 2 % 2
    parts = [got[z].astype(F32) for z in range(16)]
    weights = sum(p[48:] for p in parts)
    tails = [p[32:48] for p in parts]
    edges = [sum(tails[8 * h : 8 * h + 8]) for h in range(2)]
    cols = [jnp.where(lane < 80, tails[n] + tails[8 + n], 0.0) for n in range(8)]
    body, from_low, from_high = {}, {}, {}
    for h in range(2):
        for core in range(2):
            n = 4 * h + 2 * core
            left = pltpu.roll(cols[n], I - 8, 1)
            right = pltpu.roll(cols[n + 1], 56, 1)
            body[h, core] = jnp.where(last, 0.0, left) + jnp.where(first, 0.0, right)
            from_low[h, core] = jnp.where(first, pltpu.roll(edges[h], 48 - 16 * core, 1) + right, 0.0)
            from_high[h, core] = jnp.where(last, pltpu.roll(edges[h], 32 - 16 * core, 1) + left, 0.0)
    above = jnp.where(part >= 4, pltpu.roll(from_low[1, 1], 4, 0), 0.0)
    below = jnp.where(part < 12, pltpu.roll(from_high[0, 0], 12, 0), 0.0)
    sums = {
        (0, 0): above + from_high[0, 1],
        (0, 1): from_low[0, 0] + from_high[1, 0],
        (1, 0): from_low[0, 1] + from_high[1, 1],
        (1, 1): from_low[1, 0] + below,
    }
    rest = edges[0] + edges[1]
    small = lax.broadcasted_iota(jnp.int32, (8, I), 1)
    low = lax.broadcasted_iota(jnp.int32, (8, I), 0) < 4
    rest = jnp.where(small < 112, pltpu.roll(swap_rows(rest[:8]), I - 16, 1), rest[:8])
    for core in range(2):
        rows = slice(16 * core, 16 * core + 16)
        main = [sum(p[rows] for p in parts[8 * h : 8 * h + 8]) for h in range(2)]
        total = jnp.where(
            z_hi == 0, main[0] + body[0, core] + sums[0, core], main[1] + body[1, core] + sums[1, core]
        )
        for y in range(4):
            tile = total[8 * (y // 2) : 8 * (y // 2) + 8]
            tile = jnp.where(low, tile if y % 2 == 0 else swap_rows(tile), rest)
            message = jnp.concatenate([weights, tile], axis=0).astype(BF16)
            for x in range(4):
                out[16 * core + 4 * y + x] = message


def unpack_kernel(got, gk, ge):
    parts = [got[t].astype(F32) for t in range(32)]
    main = jnp.concatenate([p[:8] for p in parts], axis=0) * (1.0 / (ROWS * I))
    low = lax.broadcasted_iota(jnp.int32, (8, I), 0) < 4
    pairs = list(zip(parts[::2], parts[1::2]))
    rest = jnp.concatenate([jnp.where(low, swap_rows(p[8:]), q[8:]) for p, q in pairs], axis=0)
    sums = jnp.concatenate([jnp.where(low, p[8:], swap_rows(q[8:])) for p, q in pairs], axis=0)
    rest = rest * (1.0 / (ROWS * I))
    ge[...] = sums.T * float(ROWS * I) ** (-0.5)
    tail = main[192:]
    for a in range(3):
        rows = slice(C * a, C * a + C)
        gk[3 * a] = main[rows, :C]
        gk[3 * a + 1] = main[rows, C:]
        if a == 2:
            gk[3 * a + 2] = tail[:, :C]
        else:
            gk[3 * a + 2] = jnp.concatenate([rest[rows, 96:], tail[:, 64 + 32 * a : 96 + 32 * a]], axis=1)


def small_call(kernel, out_shape, ids, name, **options):
    return pl.pallas_call(
        kernel,
        out_shape=out_shape,
        in_specs=[VMEM] + [SMEM] * ids,
        out_specs=jax.tree.map(lambda _: VMEM, out_shape),
        cost_estimate=pl.CostEstimate(flops=1_000_000, bytes_accessed=500_000, transcendentals=0),
        name=name,
        **options,
    )


def reduce_all(parts, ids, **options):
    got = exchange(parts, PLANE_GROUPS)
    share = small_call(share_kernel, whole((16, 56, I), BF16), 0, "plane_sums", **options)(got)
    got = exchange(share, LINE_GROUPS)
    done = small_call(finish_kernel, whole((32, 16, I), BF16), 1, "line_sums", **options)(got, ids)
    got = exchange(done, PLANE_GROUPS)
    shapes = (whole((9, C, C), F32), whole((2 * C, I), F32))
    return small_call(unpack_kernel, shapes, 0, "unpack", **options)(got)


def on_device(embedding, kernel, cotangent):
    rows_local = embedding.shape[0]
    row_id = lax.axis_index("row")
    col_id = lax.axis_index("col")
    place = (col_id % 8 + sum(jnp.where(row_id % 4 == n, turn, 0) for n, turn in enumerate(TURN))) % 8
    mine = lax.dynamic_slice_in_dim(embedding, place // 2 % 2 * (J - G), J + G, 0)
    window = lax.ppermute(mine, ("row", "col"), window_pairs())
    ends = jnp.concatenate([embedding[:G], embedding[rows_local - G :]], axis=0)
    ends = exchange(jnp.broadcast_to(ends[None], (ROWS,) + ends.shape), ROW_GROUPS)
    ids = jnp.stack([row_id, col_id])
    cot = cotangent.transpose(1, 2, 0)
    ga, gae = run_back(cot, kernel.reshape(9, C, C))
    parts, act, edge = run_main(cot, ga, gae, embedding, ends, window, ids)
    taps = kernel.transpose(1, 3, 0, 2).reshape(192, 192)
    prediction = run_forward(act, edge, taps).transpose(2, 0, 1)
    gk, ge = reduce_all(parts, ids)
    return prediction, gk.reshape(kernel.shape), ge


def solution(mesh):
    in_specs = (P("row", None), P(), P("row", "col", None))
    out_specs = (P("row", "col", None), P(), P("row", None))
    return jax.shard_map(
        on_device, mesh=mesh, in_specs=in_specs, out_specs=out_specs, check_vma=False
    )
```

time: 103 us -> 101 us (0.981)
  blocking collectives: 12.1 us -> 31.8 us
  waiting for transfers between devices: 20.8 us -> 5.89 us
  starting transfers between devices: 37.5 us -> 31.4 us
  Pallas kernels: 17.7 us -> 21.5 us
  local copies, waits for them, and re-layouts: 11.1 us -> 8.43 us
  other arithmetic: 1.92 us -> 0.08 us
    all_to_all x1 -> x2, blocking collectives: 12.1 us -> 31.8 us  [exchange(): return lax.all_to_all(parts, ('row', 'col'), 0, 0, axis_index_groups=groups)]
    all_to_all x3 -> x2, waiting for transfers between devices: 20.8 us -> 5.89 us  [exchange(): return lax.all_to_all(parts, ('row', 'col'), 0, 0, axis_index_groups=groups)]
    all_to_all x3 -> x2, starting transfers between devices: 19.9 us -> 13.9 us  [exchange(): return lax.all_to_all(parts, ('row', 'col'), 0, 0, axis_index_groups=groups)]
    pallas_call x1 -> x4, Pallas kernels: 10.4 us -> 14.2 us  [the longest x1 9.03 us: run_main(): pl.pallas_call(main_kernel, out_shape=(whole((32, 16, I), F32), whole((80...]
    unnamed x16 -> x18, local copies, waits for them, and re-layouts: 6.85 us -> 6.03 us
  transfers between devices with their start and end apart: 4 -> 3, of which waited for: 3 -> 2; matrix products, arithmetic and copies ran while one was open for 2% -> 2% of each run, Pallas kernels for 7% -> 7%
where the time goes in v3:
time: 101 us; the launch traced here: 100 us
  blocking collectives  31.8 us (31%)
  starting transfers between devices  31.4 us (31%)
  Pallas kernels  21.5 us (21%)
  local copies, waits for them, and re-layouts  8.43 us (8%)
  waiting for transfers between devices  5.89 us (6%)
    all_to_all x2, blocking collectives, exchange(): return lax.all_to_all(parts, ('row', 'col'), 0, 0, axis_index_groups=groups)  31.8 us
    ppermute x1, starting transfers between devices, on_device(): window = lax.ppermute(mine, ('row', 'col'), window_pairs())  17.6 us
    all_to_all x2, starting transfers between devices, exchange(): return lax.all_to_all(parts, ('row', 'col'), 0, 0, axis_index_groups=groups)  13.9 us
    pallas_call x1, Pallas kernels, run_main(): pl.pallas_call(main_kernel, out_shape=(whole((32, 16, I), F32), whole((80...  9.03 us
    unnamed x18, local copies, waits for them, and re-layouts  6.03 us
    all_to_all x2, waiting for transfers between devices, exchange(): return lax.all_to_all(parts, ('row', 'col'), 0, 0, axis_index_groups=groups)  5.89 us
    pallas_call x1, Pallas kernels, run_forward(): pl.pallas_call(forward_kernel, out_shape=whole((J, C, I), F32), in_specs=...  4.37 us
    pallas_call x1, Pallas kernels, run_back(): pl.pallas_call(back_kernel, out_shape=(whole((80, C, I), F32), whole((10,...  2.94 us
  transfers between devices with their start and end apart: 3, of which 2 were waited for; matrix products, arithmetic and copies ran while one was open for 2% of the time, Pallas kernels for 7%

profile of v3, /device:TPU:1, one launch (start us, length us, event | category | flops | bytes accessed | tf_op | source)
XLA Modules:
  0.0 100.0 jit_solution(18056208810742841769)
XLA Ops:
  0.7 0.7 constant_dynamic-slice_fusion
  1.4 17.6 %collective-permute-start = (bf16[72,128]{1,0:T(8,128)(2,1)S(1)}, bf16[72,128]{1,0:T(8,128)(2,1)S(1)}, u32[]{:S(2)}, u32[]{:S(2)}) collective-permute-start(bf16[72,128]{1,0:T(8,128)(2,1)S(1)} %constant_dynamic-slice_fusion), channel_id=1, source_target_pairs={{16,0},{18,1},{49,2},{51,3},{87,4},{81,5},{112,6},{114,7},{144,8},... | collective-permute-start | bytes 55304 | tf_op jit(solution)/shard_map/ppermute | solution.py:457
  19.0 0.7 fusion
  19.7 0.6 broadcast_in_dim.2
  20.4 4.4 %all-to-all-start = ((bf16[16,16,128]{2,1,0:T(8,128)(2,1)}), bf16[16,16,128]{2,1,0:T(8,128)(2,1)S(1)}, u32[]{:S(2)}, u32[]{:S(2)}) async-start(bf16[16,16,128]{2,1,0:T(8,128)(2,1)} %broadcast_in_dim.2), calls=%async_computation | async-start | bytes 131072 | tf_op jit(solution)/shard_map/all_to_all | solution.py:55
  24.8 0.0 copy-start
  24.8 0.9 copy-done
  25.7 0.0 copy-start.4
  25.7 1.2 %copy-done.4 = bf16[128,64,64]{0,2,1:T(8,128)(2,1)S(1)} copy-done((bf16[128,64,64]{0,2,1:T(8,128)(2,1)S(1)}, bf16[128,64,64]{0,2,1:T(8,128)(2,1)}, u32[]{:S(2)}) %copy-start.4) | copy-done | bytes 1048600
  26.9 0.0 copy-start.2
  26.9 0.0 copy-start.5
  26.9 2.9 %tile_back.1 = (f32[80,64,128]{2,1,0:T(8,128)S(1)}, f32[10,64,128]{2,1,0:T(8,128)S(1)}) custom-call(bf16[64,64,128]{2,1,0:T(8,128)(2,1)S(1)} %bitcast.9, bf16[9,64,64]{2,1,0:T(8,128)(2,1)S(1)} %bitcast.7), custom_call_target="tpu_custom_call" | custom-call | flops 2400000000 | bytes 4000000 | tf_op jit(solution)/shard_map/tile_back/pallas_call | solution.py:269
  29.9 0.0 copy-start.6
  29.9 1.5 %copy-done.6 = f32[80,64,128]{2,1,0:T(8,128)} copy-done((f32[80,64,128]{2,1,0:T(8,128)}, f32[80,64,128]{2,1,0:T(8,128)S(1)}, u32[]{:S(2)}) %copy-start.6) | copy-done | bytes 2621464
  31.4 0.1 pad_add_fusion.ids
  31.4 0.0 copy-start.3
  31.5 0.0 collective-permute-done.window
  31.5 3.1 %all-to-all-done.ends = bf16[16,16,128]{2,1,0:T(8,128)(2,1)S(1)} async-done(((bf16[16,16,128]{2,1,0:T(8,128)(2,1)}), bf16[16,16,128]{2,1,0:T(8,128)(2,1)S(1)}, u32[]{:S(2)}, u32[]{:S(2)}) %all-to-all-start) | async-done | bytes 65568 | tf_op jit(solution)/shard_map/all_to_all | solution.py:55
  34.5 0.0 copy-done.2
  34.5 0.0 copy-done.5
  34.5 0.0 copy-start.7
  34.5 1.7 %copy-done.7 = f32[80,64,128]{2,1,0:T(8,128)S(1)} copy-done((f32[80,64,128]{2,1,0:T(8,128)S(1)}, f32[80,64,128]{2,1,0:T(8,128)}, u32[]{:S(2)}) %copy-start.7) | copy-done | bytes 2621464
  36.3 9.0 %tile_gradients.1 = (f32[32,16,128]{2,1,0:T(8,128)S(1)}, bf16[80,64,128]{2,1,0:T(8,128)(2,1)S(1)}, bf16[10,64,128]{2,1,0:T(8,128)(2,1)S(1)}) custom-call(bf16[64,64,128]{2,1,0:T(8,128)(2,1)S(1)} %bitcast.10, f32[80,64,128]{2,1,0:T(8,128)S(1)} %copy-done.7, f32[10,64,128]{2,1,0:T(8,128)S(1)} %get-tuple-element.11.gae, bf16[128,128]{1,0:T(8,128)(2,1)S(1)} %copy-done.2, ...), custom_call_target="tpu_custom_call" | custom-call | flops 1300000000 | bytes 6000000 | tf_op jit(solution)/shard_map/tile_gradients/pallas_call | solution.py:281
  45.3 0.0 copy-done.3
  45.3 0.0 copy-start.1
  45.3 12.3 %all_to_all.20.got = f32[32,16,128]{2,1,0:T(8,128)} all-to-all(f32[32,16,128]{2,1,0:T(8,128)S(1)} %get-tuple-element.14), channel_id=1, replica_groups={{0,8,16,24,128,136,144,152,256,264,272,280,384,392,400,408,32,40,48,56,..., dimensions={0} | all-to-all | bytes 524288 | tf_op jit(solution)/shard_map/all_to_all | solution.py:55
  57.6 1.7 %plane_sums.1 = bf16[16,56,128]{2,1,0:T(8,128)(2,1)} custom-call(f32[32,16,128]{2,1,0:T(8,128)} %all_to_all.20.got), custom_call_target="tpu_custom_call" | custom-call | flops 1000000 | bytes 500000 | tf_op jit(solution)/shard_map/plane_sums/pallas_call | solution.py:443
  59.3 19.6 %all_to_all.21.got = bf16[16,56,128]{2,1,0:T(8,128)(2,1)} all-to-all(bf16[16,56,128]{2,1,0:T(8,128)(2,1)} %plane_sums.1), channel_id=1, replica_groups={{0,1,2,3,4,5,6,7,64,65,66,67,68,69,70,71},{8,9,10,11,12,13,14,15,72,73,..., dimensions={0} | all-to-all | bytes 458752 | tf_op jit(solution)/shard_map/all_to_all | solution.py:55
  78.9 1.7 %line_sums.1 = bf16[32,16,128]{2,1,0:T(8,128)(2,1)} custom-call(bf16[16,56,128]{2,1,0:T(8,128)(2,1)} %all_to_all.21.got, s32[2]{0:T(128)} %copy-done.3), custom_call_target="tpu_custom_call" | custom-call | flops 1000000 | bytes 500000 | tf_op jit(solution)/shard_map/line_sums/pallas_call | solution.py:445
  80.6 9.5 %all-to-all-start.3 = ((bf16[32,16,128]{2,1,0:T(8,128)(2,1)}), bf16[32,16,128]{2,1,0:T(8,128)(2,1)S(1)}, u32[]{:S(2)}, u32[]{:S(2)}) async-start(bf16[32,16,128]{2,1,0:T(8,128)(2,1)} %line_sums.1), calls=%async_computation.3 | async-start | bytes 262144 | tf_op jit(solution)/shard_map/all_to_all | solution.py:55
  90.1 0.0 copy-done.1
  90.1 0.2 copy.7
  90.2 0.2 reshape.17.w
  90.4 4.4 %tile_forward.1 = f32[64,64,128]{2,1,0:T(8,128)} custom-call(bf16[80,64,128]{2,1,0:T(8,128)(2,1)S(1)} %get-tuple-element.12.act, bf16[10,64,128]{2,1,0:T(8,128)(2,1)S(1)} %get-tuple-element.13.edge, bf16[192,192]{1,0:T(8,128)(2,1)S(1)} %reshape.17.w), custom_call_target="tpu_custom_call" | custom-call | flops 700000000 | bytes 3500000 | tf_op jit(solution)/shard_map/tile_forward/pallas_call | solution.py:330
  94.8 2.8 %all-to-all-done.3.got = bf16[32,16,128]{2,1,0:T(8,128)(2,1)S(1)} async-done(((bf16[32,16,128]{2,1,0:T(8,128)(2,1)}), bf16[32,16,128]{2,1,0:T(8,128)(2,1)S(1)}, u32[]{:S(2)}, u32[]{:S(2)}) %all-to-all-start.3) | async-done | bytes 131104 | tf_op jit(solution)/shard_map/all_to_all | solution.py:55
  97.6 0.0 copy-start.8
  97.6 0.7 copy-done.8
  98.3 1.8 %unpack.1 = (f32[9,64,64]{2,1,0:T(8,128)}, f32[128,128]{1,0:T(8,128)}) custom-call(bf16[32,16,128]{2,1,0:T(8,128)(2,1)} %copy-done.8), custom_call_target="tpu_custom_call" | custom-call | flops 1000000 | bytes 500000 | tf_op jit(solution)/shard_map/unpack/pallas_call | solution.py:448
  (1 shorter events, 0.0 us)
Async XLA Ops:
  1.4 30.0 %collective-permute-start = (bf16[72,128]{1,0:T(8,128)(2,1)S(1)}, bf16[72,128]{1,0:T(8,128)(2,1)S(1)}, u32[]{:S(2)}, u32[]{:S(2)}) collective-permute-start(bf16[72,128]{1,0:T(8,128)(2,1)S(1)} %constant_dynamic-slice_fusion), channel_id=1, source_target_pairs={{16,0},{18,1},{49,2},{51,3},{87,4},{81,5},{112,6},{114,7},{144,8},... | collective-permute-start | bytes 55304 | tf_op jit(solution)/shard_map/ppermute | solution.py:457
  20.4 14.2 %all-to-all-start = ((bf16[16,16,128]{2,1,0:T(8,128)(2,1)}), bf16[16,16,128]{2,1,0:T(8,128)(2,1)S(1)}, u32[]{:S(2)}, u32[]{:S(2)}) async-start(bf16[16,16,128]{2,1,0:T(8,128)(2,1)} %broadcast_in_dim.2), calls=%async_computation | async-start | bytes 131072 | tf_op jit(solution)/shard_map/all_to_all | solution.py:55
  24.8 0.9 copy-start
  25.7 1.2 %copy-start.4 = (bf16[128,64,64]{0,2,1:T(8,128)(2,1)S(1)}, bf16[128,64,64]{0,2,1:T(8,128)(2,1)}, u32[]{:S(2)}) copy-start(bf16[128,64,64]{0,2,1:T(8,128)(2,1)} %param.5) | copy-start | bytes 3145732
  26.9 7.6 %copy-start.2 = (bf16[128,128]{1,0:T(8,128)(2,1)S(1)}, bf16[128,128]{1,0:T(8,128)(2,1)}, u32[]{:S(2)}) copy-start(bf16[128,128]{1,0:T(8,128)(2,1)} %own.1) | copy-start | bytes 98308
  26.9 7.6 %copy-start.5 = (bf16[128,64,64]{0,2,1:T(8,128)(2,1)S(1)}, bf16[128,64,64]{0,2,1:T(8,128)(2,1)}, u32[]{:S(2)}) copy-start(bf16[128,64,64]{0,2,1:T(8,128)(2,1)} %param.5) | copy-start | bytes 3145732
  29.9 1.5 %copy-start.6 = (f32[80,64,128]{2,1,0:T(8,128)}, f32[80,64,128]{2,1,0:T(8,128)S(1)}, u32[]{:S(2)}) copy-start(f32[80,64,128]{2,1,0:T(8,128)S(1)} %get-tuple-element.10.ga) | copy-start | bytes 7864324
  31.4 13.9 %copy-start.3 = (s32[2]{0:T(128)}, s32[2]{0:T(128)S(1)}, u32[]{:S(2)}) copy-start(s32[2]{0:T(128)S(1)} %pad_add_fusion.ids) | copy-start | bytes 28
  34.5 1.7 %copy-start.7 = (f32[80,64,128]{2,1,0:T(8,128)S(1)}, f32[80,64,128]{2,1,0:T(8,128)}, u32[]{:S(2)}) copy-start(f32[80,64,128]{2,1,0:T(8,128)} %copy-done.6) | copy-start | bytes 7864324
  45.3 44.8 %copy-start.1 = (bf16[3,3,64,64]{3,2,1,0:T(8,128)(2,1)S(1)}, bf16[3,3,64,64]{3,2,1,0:T(8,128)(2,1)}, u32[]{:S(2)}) copy-start(bf16[3,3,64,64]{3,2,1,0:T(8,128)(2,1)} %param.4) | copy-start | bytes 221188
  80.6 17.0 %all-to-all-start.3 = ((bf16[32,16,128]{2,1,0:T(8,128)(2,1)}), bf16[32,16,128]{2,1,0:T(8,128)(2,1)S(1)}, u32[]{:S(2)}, u32[]{:S(2)}) async-start(bf16[32,16,128]{2,1,0:T(8,128)(2,1)} %line_sums.1), calls=%async_computation.3 | async-start | bytes 262144 | tf_op jit(solution)/shard_map/all_to_all | solution.py:55
  97.6 0.7 copy-start.8

commit v4 on v3

--- a/solution.py
+++ b/solution.py
@@ -81,9 +81,39 @@
     return before, value, after
 
 
-def back_kernel(cot, w, ga, gae):
+class Stream:
+    def __init__(self, source, target, sems, count):
+        self.source, self.target, self.sems, self.count = source, target, sems, count
+
+    def copy(self, k):
+        size = self.source.shape[0] // self.count
+        place = pl.ds(k * size, size)
+        return pltpu.make_async_copy(self.source.at[place], self.target.at[place], self.sems.at[k])
+
+    def start(self, k):
+        if isinstance(k, int):
+            if k < self.count:
+                self.copy(k).start()
+        else:
+            pl.when(k < self.count)(lambda: self.copy(k).start())
+
+    def wait(self, k):
+        self.copy(k).wait()
+
+
+AHEAD = 3
+
+
+def back_kernel(cot_hbm, w_hbm, ga_hbm, gae, cot, w, ga, cot_sems, w_sem, ga_sems):
+    w_copy = pltpu.make_async_copy(w_hbm, w, w_sem)
+    w_copy.start()
+    come = Stream(cot_hbm, cot, cot_sems, 8)
+    leave = Stream(ga, ga_hbm, ga_sems, 10)
+    for k in range(AHEAD):
+        come.start(k)
     lane = lax.broadcasted_iota(jnp.int32, (C, I), 1)
     slot = lane % 16
+    w_copy.wait()
     weights = jnp.concatenate(
         [jnp.concatenate([w[3 * a + b] for a in range(3)], axis=1) for b in range(3)], axis=0
     )
@@ -95,6 +125,8 @@
         ref[place] = value if fresh else ref[place] + value
 
     def back(k, first):
+        come.wait(k)
+        come.start(k + AHEAD)
         fresh = [first, first, True]
         packed = jnp.zeros((C, I), F32)
         for p in range(0, G, 2):
@@ -117,12 +149,18 @@
         part = dot(edge_weights, both)
         for b in range(3):
             put(gae, k + b, part[C * b : C * b + C], fresh[b])
+        leave.start(k)
 
     back(0, True)
 
     @pl.loop(1, 8)
     def _(k):
         back(k, False)
+
+    leave.start(8)
+    leave.start(9)
+    for k in range(10):
+        leave.wait(k)
 
 
 def fold8(tiles, lane):
@@ -136,12 +174,16 @@
 
 
 def main_kernel(
-    cot, ga, gae, own, ends, window, ids, out, act_out, edge_out, gk, acc, half, col_t, expand
+    cot, ga_hbm, gae, own, ends, window, ids, out, act_out, edge_out,
+    gk, acc, half, col_t, expand, ga, ga_sems,
 ):
     lane = lax.broadcasted_iota(jnp.int32, (C, I), 1)
     thin = lax.broadcasted_iota(jnp.int32, (16, I), 1)
     m0 = lax.broadcasted_iota(jnp.int32, (I, I), 0)
     m1 = lax.broadcasted_iota(jnp.int32, (I, I), 1)
+    come = Stream(ga_hbm, ga, ga_sems, 10)
+    for k in range(AHEAD):
+        come.start(k)
     acc[...] = jnp.zeros_like(acc)
     gk[...] = jnp.zeros_like(gk)
     for q in range(G):
@@ -168,6 +210,8 @@
         return y, p + y * (1.0 - t)
 
     def group(k, taps, mask):
+        come.wait(k)
+        come.start(k + AHEAD)
         spread = (m0 == G * k + m1 // 16).astype(BF16)
         gather = (m1 == G * k + m0 // 16).astype(BF16)
         wide = col_t[...]
@@ -262,6 +306,7 @@
 
 
 VMEM = pl.BlockSpec(memory_space=pltpu.VMEM)
+HBM = pl.BlockSpec(memory_space=pltpu.HBM)
 SMEM = pl.BlockSpec(memory_space=pltpu.SMEM)
 
 
@@ -269,9 +314,17 @@
     return pl.pallas_call(
         back_kernel,
         out_shape=(whole((80, C, I), F32), whole((10, C, I), F32)),
-        in_specs=[VMEM, VMEM],
-        out_specs=(VMEM, VMEM),
-        compiler_params=pltpu.CompilerParams(vmem_limit_bytes=12 * 2**20),
+        in_specs=[HBM, HBM],
+        out_specs=(HBM, VMEM),
+        scratch_shapes=[
+            pltpu.VMEM((J, C, I), BF16),
+            pltpu.VMEM((9, C, C), BF16),
+            pltpu.VMEM((80, C, I), F32),
+            pltpu.SemaphoreType.DMA((8,)),
+            pltpu.SemaphoreType.DMA,
+            pltpu.SemaphoreType.DMA((10,)),
+        ],
+        compiler_params=pltpu.CompilerParams(vmem_limit_bytes=16 * 2**20),
         cost_estimate=pl.CostEstimate(flops=2_400_000_000, bytes_accessed=4_000_000, transcendentals=0),
         name="tile_back",
     )(cot, w)
@@ -281,7 +334,7 @@
     return pl.pallas_call(
         main_kernel,
         out_shape=(whole((32, 16, I), F32), whole((80, C, I), BF16), whole((10, C, I), BF16)),
-        in_specs=[VMEM] * 6 + [SMEM],
+        in_specs=[VMEM, HBM] + [VMEM] * 4 + [SMEM],
         out_specs=(VMEM, VMEM, VMEM),
         scratch_shapes=[
             pltpu.VMEM((192, 192), F32),
@@ -289,8 +342,10 @@
             pltpu.VMEM((2 * C, 2 * I), F32),
             pltpu.VMEM((2 * C, I), F32),
             pltpu.VMEM((I, G * I), BF16),
+            pltpu.VMEM((80, C, I), F32),
+            pltpu.SemaphoreType.DMA((10,)),
         ],
-        compiler_params=pltpu.CompilerParams(vmem_limit_bytes=12 * 2**20),
+        compiler_params=pltpu.CompilerParams(vmem_limit_bytes=16 * 2**20),
         cost_estimate=pl.CostEstimate(flops=1_300_000_000, bytes_accessed=6_000_000, transcendentals=700_000),
         name="tile_gradients",
     )(cot, ga, gae, own, ends, window, ids)
@@ -332,10 +387,20 @@
         out_shape=whole((J, C, I), F32),
         in_specs=[VMEM] * 3,
         out_specs=VMEM,
-        compiler_params=pltpu.CompilerParams(vmem_limit_bytes=40 * 2**20),
+        compiler_params=pltpu.CompilerParams(vmem_limit_bytes=16 * 2**20),
         cost_estimate=pl.CostEstimate(flops=700_000_000, bytes_accessed=3_500_000, transcendentals=0),
         name="tile_forward",
     )(act, edge, w)
+
+
+def cut_kernel(own, ids, window, ends):
+    turn = sum(jnp.where(ids[0] % 4 == n, turn, 0) for n, turn in enumerate(TURN))
+    odd = (ids[1] + turn) % 8 // 2 % 2
+    wide = own[...].astype(F32)
+    window[...] = jnp.where(odd == 1, wide[J - G :], wide[: J + G]).astype(BF16)
+    both = jnp.concatenate([wide[:G], wide[I - G :]], axis=0).astype(BF16)
+    for n in range(ROWS):
+        ends[n] = both
 
 
 def swap_rows(x):
@@ -432,6 +497,7 @@
         out_shape=out_shape,
         in_specs=[VMEM] + [SMEM] * ids,
         out_specs=jax.tree.map(lambda _: VMEM, out_shape),
+        compiler_params=pltpu.CompilerParams(vmem_limit_bytes=6 * 2**20),
         cost_estimate=pl.CostEstimate(flops=1_000_000, bytes_accessed=500_000, transcendentals=0),
         name=name,
         **options,
@@ -449,15 +515,13 @@
 
 
 def on_device(embedding, kernel, cotangent):
-    rows_local = embedding.shape[0]
     row_id = lax.axis_index("row")
     col_id = lax.axis_index("col")
-    place = (col_id % 8 + sum(jnp.where(row_id % 4 == n, turn, 0) for n, turn in enumerate(TURN))) % 8
-    mine = lax.dynamic_slice_in_dim(embedding, place // 2 % 2 * (J - G), J + G, 0)
+    ids = jnp.stack([row_id, col_id])
+    shapes = (whole((J + G, 2 * C), BF16), whole((ROWS, 2 * G, 2 * C), BF16))
+    mine, ends = small_call(cut_kernel, shapes, 1, "cut_embedding")(embedding, ids)
     window = lax.ppermute(mine, ("row", "col"), window_pairs())
-    ends = jnp.concatenate([embedding[:G], embedding[rows_local - G :]], axis=0)
-    ends = exchange(jnp.broadcast_to(ends[None], (ROWS,) + ends.shape), ROW_GROUPS)
-    ids = jnp.stack([row_id, col_id])
+    ends = exchange(ends, ROW_GROUPS)
     cot = cotangent.transpose(1, 2, 0)
     ga, gae = run_back(cot, kernel.reshape(9, C, C))
     parts, act, edge = run_main(cot, ga, gae, embedding, ends, window, ids)

time: 101 us -> 100 us (0.990)
  starting transfers between devices: 31.4 us -> 37 us
  waiting for transfers between devices: 5.89 us -> 2.83 us
  local copies, waits for them, and re-layouts: 8.43 us -> 6.45 us
  blocking collectives: 31.8 us -> 30.2 us
  Pallas kernels: 21.5 us -> 22.7 us
    all_to_all x2, starting transfers between devices: 13.9 us -> 25.7 us  [exchange(): return lax.all_to_all(parts, ('row', 'col'), 0, 0, axis_index_groups=groups)]
    ppermute x1, starting transfers between devices: 17.6 us -> 11.3 us  [on_device(): window = lax.ppermute(mine, ('row', 'col'), window_pairs())]
    all_to_all x2, waiting for transfers between devices: 5.89 us -> 2.83 us  [exchange(): return lax.all_to_all(parts, ('row', 'col'), 0, 0, axis_index_groups=groups)]
    pallas_call x1, Pallas kernels: 2.94 us -> 4.98 us  [run_back(): pl.pallas_call(back_kernel, out_shape=(whole((80, C, I), F32), whole((10,...]
    all_to_all x2, blocking collectives: 31.8 us -> 30.2 us  [exchange(): return lax.all_to_all(parts, ('row', 'col'), 0, 0, axis_index_groups=groups)]
    pallas_call x1, Pallas kernels: 1.73 us -> 0.09 us  [reduce_all(): small_call(share_kernel, whole((16, 56, I), BF16), 0, 'plane_sums', **opt...]
    pallas_call x0 -> x1, Pallas kernels: none -> 1.18 us  [on_device(): small_call(cut_kernel, shapes, 1, 'cut_embedding')(embedding, ids)]
    unnamed x18 -> x16, local copies, waits for them, and re-layouts: 6.03 us -> 6.12 us
  transfers between devices with their start and end apart: 3 -> 3, of which waited for: 2 -> 1; matrix products, arithmetic and copies ran while one was open for 2% -> 0% of each run, Pallas kernels for 7% -> 9%
where the time goes in v4:
time: 100 us; the launch traced here: 99.9 us
  starting transfers between devices  37 us (37%)
  blocking collectives  30.2 us (30%)
  Pallas kernels  22.7 us (23%)
  local copies, waits for them, and re-layouts  6.45 us (6%)
  waiting for transfers between devices  2.83 us (3%)
    all_to_all x2, blocking collectives, exchange(): return lax.all_to_all(parts, ('row', 'col'), 0, 0, axis_index_groups=groups)  30.2 us
    all_to_all x2, starting transfers between devices, exchange(): return lax.all_to_all(parts, ('row', 'col'), 0, 0, axis_index_groups=groups)  25.7 us
    ppermute x1, starting transfers between devices, on_device(): window = lax.ppermute(mine, ('row', 'col'), window_pairs())  11.3 us
    pallas_call x1, Pallas kernels, run_main(): pl.pallas_call(main_kernel, out_shape=(whole((32, 16, I), F32), whole((80...  9.89 us
    unnamed x16, local copies, waits for them, and re-layouts  6.12 us
    pallas_call x1, Pallas kernels, run_back(): pl.pallas_call(back_kernel, out_shape=(whole((80, C, I), F32), whole((10,...  4.98 us
    pallas_call x1, Pallas kernels, run_forward(): pl.pallas_call(forward_kernel, out_shape=whole((J, C, I), F32), in_specs=...  4.36 us
    all_to_all x2, waiting for transfers between devices, exchange(): return lax.all_to_all(parts, ('row', 'col'), 0, 0, axis_index_groups=groups)  2.83 us
  transfers between devices with their start and end apart: 3, of which 1 were waited for; matrix products, arithmetic and copies ran while one was open for 0% of the time, Pallas kernels for 9%

profile of v4, /device:TPU:1, one launch (start us, length us, event | category | flops | bytes accessed | tf_op | source)
XLA Modules:
  0.0 99.9 jit_solution(15653181604029182767)
XLA Ops:
  0.6 0.1 pad_add_fusion.ids
  0.7 0.0 copy-start.2
  0.7 0.8 copy-done.2
  1.5 1.2 %cut_embedding.1 = (bf16[72,128]{1,0:T(8,128)(2,1)S(1)}, bf16[16,16,128]{2,1,0:T(8,128)(2,1)}) custom-call(bf16[128,128]{1,0:T(8,128)(2,1)S(1)} %copy-done.2, s32[2]{0:T(128)S(1)} %pad_add_fusion.ids), custom_call_target="tpu_custom_call" | custom-call | flops 1000000 | bytes 500000 | tf_op jit(solution)/shard_map/cut_embedding/pallas_call | solution.py:522
  2.6 16.2 %all-to-all-start = ((bf16[16,16,128]{2,1,0:T(8,128)(2,1)}), bf16[16,16,128]{2,1,0:T(8,128)(2,1)S(1)}, u32[]{:S(2)}, u32[]{:S(2)}) async-start(bf16[16,16,128]{2,1,0:T(8,128)(2,1)} %get-tuple-element.14), calls=%async_computation | async-start | bytes 131072 | tf_op jit(solution)/shard_map/all_to_all | solution.py:55
  18.9 11.3 %collective-permute-start = (bf16[72,128]{1,0:T(8,128)(2,1)S(1)}, bf16[72,128]{1,0:T(8,128)(2,1)S(1)}, u32[]{:S(2)}, u32[]{:S(2)}) collective-permute-start(bf16[72,128]{1,0:T(8,128)(2,1)S(1)} %get-tuple-element.15), channel_id=1, source_target_pairs={{16,0},{18,1},{49,2},{51,3},{87,4},{81,5},{112,6},{114,7},{144,8},... | collective-permute-start | bytes 55304 | tf_op jit(solution)/shard_map/ppermute | solution.py:523
  30.2 0.0 copy-start
  30.2 0.9 copy-done
  31.1 0.0 copy-start.4
  31.1 1.2 %copy-done.4 = bf16[128,64,64]{0,2,1:T(8,128)(2,1)S(1)} copy-done((bf16[128,64,64]{0,2,1:T(8,128)(2,1)S(1)}, bf16[128,64,64]{0,2,1:T(8,128)(2,1)}, u32[]{:S(2)}) %copy-start.4) | copy-done | bytes 1048600
  32.3 0.0 copy-start.3
  32.3 0.0 copy-start.5
  32.3 5.0 %tile_back.1 = (f32[80,64,128]{2,1,0:T(8,128)S(1)}, f32[10,64,128]{2,1,0:T(8,128)S(1)}) custom-call(bf16[64,64,128]{2,1,0:T(8,128)(2,1)S(1)} %bitcast.9, bf16[9,64,64]{2,1,0:T(8,128)(2,1)S(1)} %bitcast.7), custom_call_target="tpu_custom_call" | custom-call | flops 2400000000 | bytes 4000000 | tf_op jit(solution)/shard_map/tile_back/pallas_call | solution.py:314
  37.3 0.0 copy-start.6
  37.3 1.5 %copy-done.6 = f32[80,64,128]{2,1,0:T(8,128)} copy-done((f32[80,64,128]{2,1,0:T(8,128)}, f32[80,64,128]{2,1,0:T(8,128)S(1)}, u32[]{:S(2)}) %copy-start.6) | copy-done | bytes 2621464
  38.8 0.0 collective-permute-done.window
  38.8 0.0 all-to-all-done.ends
  38.8 0.0 copy-done.3
  38.8 0.0 copy-done.5
  38.8 0.0 copy-start.7
  38.8 1.7 %copy-done.7 = f32[80,64,128]{2,1,0:T(8,128)S(1)} copy-done((f32[80,64,128]{2,1,0:T(8,128)S(1)}, f32[80,64,128]{2,1,0:T(8,128)}, u32[]{:S(2)}) %copy-start.7) | copy-done | bytes 2621464
  40.5 9.9 %tile_gradients.1 = (f32[32,16,128]{2,1,0:T(8,128)S(1)}, bf16[80,64,128]{2,1,0:T(8,128)(2,1)S(1)}, bf16[10,64,128]{2,1,0:T(8,128)(2,1)S(1)}) custom-call(bf16[64,64,128]{2,1,0:T(8,128)(2,1)S(1)} %bitcast.10, f32[80,64,128]{2,1,0:T(8,128)S(1)} %copy-done.7, f32[10,64,128]{2,1,0:T(8,128)S(1)} %get-tuple-element.13.gae, bf16[128,128]{1,0:T(8,128)(2,1)S(1)} %copy-done.3, ...), custom_call_target="tpu_custom_call" | custom-call | flops 1300000000 | bytes 6000000 | tf_op jit(solution)/shard_map/tile_gradients/pallas_call | solution.py:334
  50.4 0.0 copy-start.1
  50.5 13.2 %all_to_all.20.got = f32[32,16,128]{2,1,0:T(8,128)S(1)} all-to-all(f32[32,16,128]{2,1,0:T(8,128)S(1)} %get-tuple-element.18), channel_id=1, replica_groups={{0,8,16,24,128,136,144,152,256,264,272,280,384,392,400,408,32,40,48,56,..., dimensions={0} | all-to-all | bytes 524288 | tf_op jit(solution)/shard_map/all_to_all | solution.py:55
  63.6 0.1 plane_sums.1
  63.7 17.0 %all_to_all.21.got = bf16[16,56,128]{2,1,0:T(8,128)(2,1)S(1)} all-to-all(bf16[16,56,128]{2,1,0:T(8,128)(2,1)S(1)} %plane_sums.1), channel_id=1, replica_groups={{0,1,2,3,4,5,6,7,64,65,66,67,68,69,70,71},{8,9,10,11,12,13,14,15,72,73,..., dimensions={0} | all-to-all | bytes 458752 | tf_op jit(solution)/shard_map/all_to_all | solution.py:55
  80.7 1.3 %line_sums.1 = bf16[32,16,128]{2,1,0:T(8,128)(2,1)} custom-call(bf16[16,56,128]{2,1,0:T(8,128)(2,1)S(1)} %all_to_all.21.got, s32[2]{0:T(128)S(1)} %pad_add_fusion.ids), custom_call_target="tpu_custom_call" | custom-call | flops 1000000 | bytes 500000 | tf_op jit(solution)/shard_map/line_sums/pallas_call | solution.py:511
  82.0 9.5 %all-to-all-start.3 = ((bf16[32,16,128]{2,1,0:T(8,128)(2,1)}), bf16[32,16,128]{2,1,0:T(8,128)(2,1)S(1)}, u32[]{:S(2)}, u32[]{:S(2)}) async-start(bf16[32,16,128]{2,1,0:T(8,128)(2,1)} %line_sums.1), calls=%async_computation.3 | async-start | bytes 262144 | tf_op jit(solution)/shard_map/all_to_all | solution.py:55
  91.5 0.0 copy-done.1
  91.5 0.2 copy.7
  91.7 0.2 reshape.16.w
  91.8 4.4 %tile_forward.1 = f32[64,64,128]{2,1,0:T(8,128)} custom-call(bf16[80,64,128]{2,1,0:T(8,128)(2,1)S(1)} %get-tuple-element.16.act, bf16[10,64,128]{2,1,0:T(8,128)(2,1)S(1)} %get-tuple-element.17.edge, bf16[192,192]{1,0:T(8,128)(2,1)S(1)} %reshape.16.w), custom_call_target="tpu_custom_call" | custom-call | flops 700000000 | bytes 3500000 | tf_op jit(solution)/shard_map/tile_forward/pallas_call | solution.py:385
  96.2 2.8 %all-to-all-done.3.got = bf16[32,16,128]{2,1,0:T(8,128)(2,1)S(1)} async-done(((bf16[32,16,128]{2,1,0:T(8,128)(2,1)}), bf16[32,16,128]{2,1,0:T(8,128)(2,1)S(1)}, u32[]{:S(2)}, u32[]{:S(2)}) %all-to-all-start.3) | async-done | bytes 131104 | tf_op jit(solution)/shard_map/all_to_all | solution.py:55
  99.0 0.9 unpack.1
Async XLA Ops:
  0.7 0.8 copy-start.2
  2.6 36.1 %all-to-all-start = ((bf16[16,16,128]{2,1,0:T(8,128)(2,1)}), bf16[16,16,128]{2,1,0:T(8,128)(2,1)S(1)}, u32[]{:S(2)}, u32[]{:S(2)}) async-start(bf16[16,16,128]{2,1,0:T(8,128)(2,1)} %get-tuple-element.14), calls=%async_computation | async-start | bytes 131072 | tf_op jit(solution)/shard_map/all_to_all | solution.py:55
  18.9 19.9 %collective-permute-start = (bf16[72,128]{1,0:T(8,128)(2,1)S(1)}, bf16[72,128]{1,0:T(8,128)(2,1)S(1)}, u32[]{:S(2)}, u32[]{:S(2)}) collective-permute-start(bf16[72,128]{1,0:T(8,128)(2,1)S(1)} %get-tuple-element.15), channel_id=1, source_target_pairs={{16,0},{18,1},{49,2},{51,3},{87,4},{81,5},{112,6},{114,7},{144,8},... | collective-permute-start | bytes 55304 | tf_op jit(solution)/shard_map/ppermute | solution.py:523
  30.2 0.9 copy-start
  31.1 1.2 %copy-start.4 = (bf16[128,64,64]{0,2,1:T(8,128)(2,1)S(1)}, bf16[128,64,64]{0,2,1:T(8,128)(2,1)}, u32[]{:S(2)}) copy-start(bf16[128,64,64]{0,2,1:T(8,128)(2,1)} %param.5) | copy-start | bytes 3145732
  32.3 6.5 %copy-start.3 = (bf16[128,128]{1,0:T(8,128)(2,1)S(1)}, bf16[128,128]{1,0:T(8,128)(2,1)}, u32[]{:S(2)}) copy-start(bf16[128,128]{1,0:T(8,128)(2,1)} %own.3) | copy-start | bytes 98308
  32.3 6.5 %copy-start.5 = (bf16[128,64,64]{0,2,1:T(8,128)(2,1)S(1)}, bf16[128,64,64]{0,2,1:T(8,128)(2,1)}, u32[]{:S(2)}) copy-start(bf16[128,64,64]{0,2,1:T(8,128)(2,1)} %param.5) | copy-start | bytes 3145732
  37.3 1.5 %copy-start.6 = (f32[80,64,128]{2,1,0:T(8,128)}, f32[80,64,128]{2,1,0:T(8,128)S(1)}, u32[]{:S(2)}) copy-start(f32[80,64,128]{2,1,0:T(8,128)S(1)} %get-tuple-element.12.ga_hbm) | copy-start | bytes 7864324
  38.8 1.7 %copy-start.7 = (f32[80,64,128]{2,1,0:T(8,128)S(1)}, f32[80,64,128]{2,1,0:T(8,128)}, u32[]{:S(2)}) copy-start(f32[80,64,128]{2,1,0:T(8,128)} %copy-done.6) | copy-start | bytes 7864324
  50.4 41.1 %copy-start.1 = (bf16[3,3,64,64]{3,2,1,0:T(8,128)(2,1)S(1)}, bf16[3,3,64,64]{3,2,1,0:T(8,128)(2,1)}, u32[]{:S(2)}) copy-start(bf16[3,3,64,64]{3,2,1,0:T(8,128)(2,1)} %param.4) | copy-start | bytes 221188
  82.0 17.0 %all-to-all-start.3 = ((bf16[32,16,128]{2,1,0:T(8,128)(2,1)}), bf16[32,16,128]{2,1,0:T(8,128)(2,1)S(1)}, u32[]{:S(2)}, u32[]{:S(2)}) async-start(bf16[32,16,128]{2,1,0:T(8,128)(2,1)} %line_sums.1), calls=%async_computation.3 | async-start | bytes 262144 | tf_op jit(solution)/shard_map/all_to_all | solution.py:55

commit v5 on v3

--- a/solution.py
+++ b/solution.py
@@ -81,7 +81,7 @@
     return before, value, after
 
 
-def back_kernel(cot, w, ga, gae):
+def back(cot, w, ga, gae):
     lane = lax.broadcasted_iota(jnp.int32, (C, I), 1)
     slot = lane % 16
     weights = jnp.concatenate(
@@ -94,7 +94,7 @@
     def put(ref, place, value, fresh):
         ref[place] = value if fresh else ref[place] + value
 
-    def back(k, first):
+    def group(k, first):
         fresh = [first, first, True]
         packed = jnp.zeros((C, I), F32)
         for p in range(0, G, 2):
@@ -118,11 +118,11 @@
         for b in range(3):
             put(gae, k + b, part[C * b : C * b + C], fresh[b])
 
-    back(0, True)
+    group(0, True)
 
     @pl.loop(1, 8)
     def _(k):
-        back(k, False)
+        group(k, False)
 
 
 def fold8(tiles, lane):
@@ -136,12 +136,13 @@
 
 
 def main_kernel(
-    cot, ga, gae, own, ends, window, ids, out, act_out, edge_out, gk, acc, half, col_t, expand
+    cot, w, own, ends, window, ids, out, act_out, edge_out, gk, acc, half, col_t, expand, ga, gae
 ):
     lane = lax.broadcasted_iota(jnp.int32, (C, I), 1)
     thin = lax.broadcasted_iota(jnp.int32, (16, I), 1)
     m0 = lax.broadcasted_iota(jnp.int32, (I, I), 0)
     m1 = lax.broadcasted_iota(jnp.int32, (I, I), 1)
+    back(cot, w, ga, gae)
     acc[...] = jnp.zeros_like(acc)
     gk[...] = jnp.zeros_like(gk)
     for q in range(G):
@@ -265,23 +266,11 @@
 SMEM = pl.BlockSpec(memory_space=pltpu.SMEM)
 
 
-def run_back(cot, w):
-    return pl.pallas_call(
-        back_kernel,
-        out_shape=(whole((80, C, I), F32), whole((10, C, I), F32)),
-        in_specs=[VMEM, VMEM],
-        out_specs=(VMEM, VMEM),
-        compiler_params=pltpu.CompilerParams(vmem_limit_bytes=12 * 2**20),
-        cost_estimate=pl.CostEstimate(flops=2_400_000_000, bytes_accessed=4_000_000, transcendentals=0),
-        name="tile_back",
-    )(cot, w)
-
-
-def run_main(cot, ga, gae, own, ends, window, ids):
+def run_main(cot, w, own, ends, window, ids):
     return pl.pallas_call(
         main_kernel,
         out_shape=(whole((32, 16, I), F32), whole((80, C, I), BF16), whole((10, C, I), BF16)),
-        in_specs=[VMEM] * 6 + [SMEM],
+        in_specs=[VMEM] * 5 + [SMEM],
         out_specs=(VMEM, VMEM, VMEM),
         scratch_shapes=[
             pltpu.VMEM((192, 192), F32),
@@ -289,11 +278,13 @@
             pltpu.VMEM((2 * C, 2 * I), F32),
             pltpu.VMEM((2 * C, I), F32),
             pltpu.VMEM((I, G * I), BF16),
+            pltpu.VMEM((80, C, I), F32),
+            pltpu.VMEM((10, C, I), F32),
         ],
         compiler_params=pltpu.CompilerParams(vmem_limit_bytes=12 * 2**20),
-        cost_estimate=pl.CostEstimate(flops=1_300_000_000, bytes_accessed=6_000_000, transcendentals=700_000),
+        cost_estimate=pl.CostEstimate(flops=3_700_000_000, bytes_accessed=4_000_000, transcendentals=700_000),
         name="tile_gradients",
-    )(cot, ga, gae, own, ends, window, ids)
+    )(cot, w, own, ends, window, ids)
 
 
 def forward_kernel(act, edge, w, out):
@@ -332,7 +323,7 @@
         out_shape=whole((J, C, I), F32),
         in_specs=[VMEM] * 3,
         out_specs=VMEM,
-        compiler_params=pltpu.CompilerParams(vmem_limit_bytes=40 * 2**20),
+        compiler_params=pltpu.CompilerParams(vmem_limit_bytes=12 * 2**20),
         cost_estimate=pl.CostEstimate(flops=700_000_000, bytes_accessed=3_500_000, transcendentals=0),
         name="tile_forward",
     )(act, edge, w)
@@ -432,6 +423,7 @@
         out_shape=out_shape,
         in_specs=[VMEM] + [SMEM] * ids,
         out_specs=jax.tree.map(lambda _: VMEM, out_shape),
+        compiler_params=pltpu.CompilerParams(vmem_limit_bytes=6 * 2**20),
         cost_estimate=pl.CostEstimate(flops=1_000_000, bytes_accessed=500_000, transcendentals=0),
         name=name,
         **options,
@@ -455,12 +447,13 @@
     place = (col_id % 8 + sum(jnp.where(row_id % 4 == n, turn, 0) for n, turn in enumerate(TURN))) % 8
     mine = lax.dynamic_slice_in_dim(embedding, place // 2 % 2 * (J - G), J + G, 0)
     window = lax.ppermute(mine, ("row", "col"), window_pairs())
-    ends = jnp.concatenate([embedding[:G], embedding[rows_local - G :]], axis=0)
+    ends = embedding.reshape(I // G, G, 2 * C)[:: I // G - 1].reshape(2 * G, 2 * C)
     ends = exchange(jnp.broadcast_to(ends[None], (ROWS,) + ends.shape), ROW_GROUPS)
     ids = jnp.stack([row_id, col_id])
     cot = cotangent.transpose(1, 2, 0)
-    ga, gae = run_back(cot, kernel.reshape(9, C, C))
-    parts, act, edge = run_main(cot, ga, gae, embedding, ends, window, ids)
+    parts, act, edge = run_main(
+        cot, kernel.reshape(9, C, C), embedding, ends, window, ids
+    )
     taps = kernel.transpose(1, 3, 0, 2).reshape(192, 192)
     prediction = run_forward(act, edge, taps).transpose(2, 0, 1)
     gk, ge = reduce_all(parts, ids)

time: 101 us -> 104 us (1.030)
  blocking collectives: 31.8 us -> 37.9 us
  starting transfers between devices: 31.4 us -> 37 us
  local copies, waits for them, and re-layouts: 8.43 us -> 5.28 us
  Pallas kernels: 21.5 us -> 18.6 us
  waiting for transfers between devices: 5.89 us -> 3.62 us
    all_to_all x2, starting transfers between devices: 13.9 us -> 25.7 us  [exchange(): return lax.all_to_all(parts, ('row', 'col'), 0, 0, axis_index_groups=groups)]
    ppermute x1, starting transfers between devices: 17.6 us -> 11.3 us  [on_device(): window = lax.ppermute(mine, ('row', 'col'), window_pairs())]
    all_to_all x2, blocking collectives: 31.8 us -> 37.9 us  [exchange(): return lax.all_to_all(parts, ('row', 'col'), 0, 0, axis_index_groups=groups)]
    unnamed x18 -> x8, local copies, waits for them, and re-layouts: 6.03 us -> 2.9 us
    all_to_all x2, waiting for transfers between devices: 5.89 us -> 2.83 us  [exchange(): return lax.all_to_all(parts, ('row', 'col'), 0, 0, axis_index_groups=groups)]
    pallas_call x1 -> x0, Pallas kernels: 2.94 us -> none  [run_back(): pl.pallas_call(back_kernel, out_shape=(whole((80, C, I), F32), whole((10,...]
    pallas_call x1, Pallas kernels: 9.03 us -> 11.9 us  [run_main(): pl.pallas_call(main_kernel, out_shape=(whole((32, 16, I), F32), whole((80...]
    pallas_call x1, Pallas kernels: 1.73 us -> 0.09 us  [reduce_all(): small_call(share_kernel, whole((16, 56, I), BF16), 0, 'plane_sums', **opt...]
  transfers between devices with their start and end apart: 3 -> 3, of which waited for: 2 -> 2; matrix products, arithmetic and copies ran while one was open for 2% -> 1% of each run, Pallas kernels for 7% -> 4%
where the time goes in v5:
time: 104 us; the launch traced here: 103 us
  blocking collectives  37.9 us (36%)
  starting transfers between devices  37 us (36%)
  Pallas kernels  18.6 us (18%)
  local copies, waits for them, and re-layouts  5.28 us (5%)
  waiting for transfers between devices  3.62 us (3%)
    all_to_all x2, blocking collectives, exchange(): return lax.all_to_all(parts, ('row', 'col'), 0, 0, axis_index_groups=groups)  37.9 us
    all_to_all x2, starting transfers between devices, exchange(): return lax.all_to_all(parts, ('row', 'col'), 0, 0, axis_index_groups=groups)  25.7 us
    pallas_call x1, Pallas kernels, run_main(): pl.pallas_call(main_kernel, out_shape=(whole((32, 16, I), F32), whole((80...  11.9 us
    ppermute x1, starting transfers between devices, on_device(): window = lax.ppermute(mine, ('row', 'col'), window_pairs())  11.3 us
    pallas_call x1, Pallas kernels, run_forward(): pl.pallas_call(forward_kernel, out_shape=whole((J, C, I), F32), in_specs=...  4.36 us
    unnamed x8, local copies, waits for them, and re-layouts  2.9 us
    all_to_all x2, waiting for transfers between devices, exchange(): return lax.all_to_all(parts, ('row', 'col'), 0, 0, axis_index_groups=groups)  2.83 us
  transfers between devices with their start and end apart: 3, of which 2 were waited for; matrix products, arithmetic and copies ran while one was open for 1% of the time, Pallas kernels for 4%

profile of v5, /device:TPU:1, one launch (start us, length us, event | category | flops | bytes accessed | tf_op | source)
XLA Modules:
  0.0 103.1 jit_solution(16296918526260570483)
XLA Ops:
  0.6 0.7 slice_bitcast_fusion
  1.3 0.6 broadcast_in_dim.8
  2.0 16.2 %all-to-all-start = ((bf16[16,16,128]{2,1,0:T(8,128)(2,1)}), bf16[16,16,128]{2,1,0:T(8,128)(2,1)S(1)}, u32[]{:S(2)}, u32[]{:S(2)}) async-start(bf16[16,16,128]{2,1,0:T(8,128)(2,1)} %broadcast_in_dim.8), calls=%async_computation | async-start | bytes 131072 | tf_op jit(solution)/shard_map/all_to_all | solution.py:55
  18.2 0.7 constant_dynamic-slice_fusion
  18.9 11.3 %collective-permute-start = (bf16[72,128]{1,0:T(8,128)(2,1)S(1)}, bf16[72,128]{1,0:T(8,128)(2,1)S(1)}, u32[]{:S(2)}, u32[]{:S(2)}) collective-permute-start(bf16[72,128]{1,0:T(8,128)(2,1)S(1)} %constant_dynamic-slice_fusion), channel_id=1, source_target_pairs={{16,0},{18,1},{49,2},{51,3},{87,4},{81,5},{112,6},{114,7},{144,8},... | collective-permute-start | bytes 55304 | tf_op jit(solution)/shard_map/ppermute | solution.py:449
  30.2 0.1 pad_add_fusion.ids
  30.3 0.8 collective-permute-done.window
  31.1 0.0 all-to-all-done.ends
  31.1 0.0 copy-start
  31.1 0.9 copy-done
  32.0 0.0 copy-start.2
  32.0 0.8 copy-done.2
  32.7 0.0 copy-start.3
  32.7 1.2 %copy-done.3 = bf16[128,64,64]{0,2,1:T(8,128)(2,1)S(1)} copy-done((bf16[128,64,64]{0,2,1:T(8,128)(2,1)S(1)}, bf16[128,64,64]{0,2,1:T(8,128)(2,1)}, u32[]{:S(2)}) %copy-start.3) | copy-done | bytes 1048600
  34.0 11.9 %tile_gradients.1 = (f32[32,16,128]{2,1,0:T(8,128)S(1)}, bf16[80,64,128]{2,1,0:T(8,128)(2,1)S(1)}, bf16[10,64,128]{2,1,0:T(8,128)(2,1)S(1)}) custom-call(bf16[64,64,128]{2,1,0:T(8,128)(2,1)S(1)} %bitcast.13, bf16[9,64,64]{2,1,0:T(8,128)(2,1)S(1)} %bitcast.10, bf16[128,128]{1,0:T(8,128)(2,1)S(1)} %copy-done.2, bf16[16,16,128]{2,1,0:T(8,128)(2,1)S(1)} %all-to-all-done.ends, ...), custom_call_target="tpu_custom_call" | custom-call | flops 3700000000 | bytes 4000000 | tf_op jit(solution)/shard_map/tile_gradients/pallas_call | solution.py:270
  45.9 0.0 copy-start.1
  45.9 13.1 %all_to_all.20.got = f32[32,16,128]{2,1,0:T(8,128)S(1)} all-to-all(f32[32,16,128]{2,1,0:T(8,128)S(1)} %get-tuple-element.10), channel_id=1, replica_groups={{0,8,16,24,128,136,144,152,256,264,272,280,384,392,400,408,32,40,48,56,..., dimensions={0} | all-to-all | bytes 524288 | tf_op jit(solution)/shard_map/all_to_all | solution.py:55
  59.1 0.1 plane_sums.1
  59.2 24.7 %all_to_all.21.got = bf16[16,56,128]{2,1,0:T(8,128)(2,1)S(1)} all-to-all(bf16[16,56,128]{2,1,0:T(8,128)(2,1)S(1)} %plane_sums.1), channel_id=1, replica_groups={{0,1,2,3,4,5,6,7,64,65,66,67,68,69,70,71},{8,9,10,11,12,13,14,15,72,73,..., dimensions={0} | all-to-all | bytes 458752 | tf_op jit(solution)/shard_map/all_to_all | solution.py:55
  83.9 1.3 %line_sums.1 = bf16[32,16,128]{2,1,0:T(8,128)(2,1)} custom-call(bf16[16,56,128]{2,1,0:T(8,128)(2,1)S(1)} %all_to_all.21.got, s32[2]{0:T(128)S(1)} %pad_add_fusion.ids), custom_call_target="tpu_custom_call" | custom-call | flops 1000000 | bytes 500000 | tf_op jit(solution)/shard_map/line_sums/pallas_call | solution.py:437
  85.2 9.5 %all-to-all-start.3 = ((bf16[32,16,128]{2,1,0:T(8,128)(2,1)}), bf16[32,16,128]{2,1,0:T(8,128)(2,1)S(1)}, u32[]{:S(2)}, u32[]{:S(2)}) async-start(bf16[32,16,128]{2,1,0:T(8,128)(2,1)} %line_sums.1), calls=%async_computation.3 | async-start | bytes 262144 | tf_op jit(solution)/shard_map/all_to_all | solution.py:55
  94.7 0.0 copy-done.1
  94.7 0.2 copy.7
  94.9 0.2 reshape.21.w
  95.0 4.4 %tile_forward.1 = f32[64,64,128]{2,1,0:T(8,128)} custom-call(bf16[80,64,128]{2,1,0:T(8,128)(2,1)S(1)} %get-tuple-element.8.act, bf16[10,64,128]{2,1,0:T(8,128)(2,1)S(1)} %get-tuple-element.9.edge, bf16[192,192]{1,0:T(8,128)(2,1)S(1)} %reshape.21.w), custom_call_target="tpu_custom_call" | custom-call | flops 700000000 | bytes 3500000 | tf_op jit(solution)/shard_map/tile_forward/pallas_call | solution.py:321
  99.4 2.8 %all-to-all-done.3.got = bf16[32,16,128]{2,1,0:T(8,128)(2,1)S(1)} async-done(((bf16[32,16,128]{2,1,0:T(8,128)(2,1)}), bf16[32,16,128]{2,1,0:T(8,128)(2,1)S(1)}, u32[]{:S(2)}, u32[]{:S(2)}) %all-to-all-start.3) | async-done | bytes 131104 | tf_op jit(solution)/shard_map/all_to_all | solution.py:55
  102.2 0.9 unpack.1
Async XLA Ops:
  2.0 29.1 %all-to-all-start = ((bf16[16,16,128]{2,1,0:T(8,128)(2,1)}), bf16[16,16,128]{2,1,0:T(8,128)(2,1)S(1)}, u32[]{:S(2)}, u32[]{:S(2)}) async-start(bf16[16,16,128]{2,1,0:T(8,128)(2,1)} %broadcast_in_dim.8), calls=%async_computation | async-start | bytes 131072 | tf_op jit(solution)/shard_map/all_to_all | solution.py:55
  18.9 12.1 %collective-permute-start = (bf16[72,128]{1,0:T(8,128)(2,1)S(1)}, bf16[72,128]{1,0:T(8,128)(2,1)S(1)}, u32[]{:S(2)}, u32[]{:S(2)}) collective-permute-start(bf16[72,128]{1,0:T(8,128)(2,1)S(1)} %constant_dynamic-slice_fusion), channel_id=1, source_target_pairs={{16,0},{18,1},{49,2},{51,3},{87,4},{81,5},{112,6},{114,7},{144,8},... | collective-permute-start | bytes 55304 | tf_op jit(solution)/shard_map/ppermute | solution.py:449
  31.1 0.9 copy-start
  32.0 0.8 copy-start.2
  32.7 1.2 %copy-start.3 = (bf16[128,64,64]{0,2,1:T(8,128)(2,1)S(1)}, bf16[128,64,64]{0,2,1:T(8,128)(2,1)}, u32[]{:S(2)}) copy-start(bf16[128,64,64]{0,2,1:T(8,128)(2,1)} %param.5) | copy-start | bytes 3145732
  45.9 48.8 %copy-start.1 = (bf16[3,3,64,64]{3,2,1,0:T(8,128)(2,1)S(1)}, bf16[3,3,64,64]{3,2,1,0:T(8,128)(2,1)}, u32[]{:S(2)}) copy-start(bf16[3,3,64,64]{3,2,1,0:T(8,128)(2,1)} %param.4) | copy-start | bytes 221188
  85.2 17.0 %all-to-all-start.3 = ((bf16[32,16,128]{2,1,0:T(8,128)(2,1)}), bf16[32,16,128]{2,1,0:T(8,128)(2,1)S(1)}, u32[]{:S(2)}, u32[]{:S(2)}) async-start(bf16[32,16,128]{2,1,0:T(8,128)(2,1)} %line_sums.1), calls=%async_computation.3 | async-start | bytes 262144 | tf_op jit(solution)/shard_map/all_to_all | solution.py:55

commit v6 on v3

--- a/solution.py
+++ b/solution.py
@@ -332,7 +332,7 @@
         out_shape=whole((J, C, I), F32),
         in_specs=[VMEM] * 3,
         out_specs=VMEM,
-        compiler_params=pltpu.CompilerParams(vmem_limit_bytes=40 * 2**20),
+        compiler_params=pltpu.CompilerParams(vmem_limit_bytes=12 * 2**20),
         cost_estimate=pl.CostEstimate(flops=700_000_000, bytes_accessed=3_500_000, transcendentals=0),
         name="tile_forward",
     )(act, edge, w)
@@ -432,6 +432,7 @@
         out_shape=out_shape,
         in_specs=[VMEM] + [SMEM] * ids,
         out_specs=jax.tree.map(lambda _: VMEM, out_shape),
+        compiler_params=pltpu.CompilerParams(vmem_limit_bytes=6 * 2**20),
         cost_estimate=pl.CostEstimate(flops=1_000_000, bytes_accessed=500_000, transcendentals=0),
         name=name,
         **options,

time: 101 us -> 96.5 us (0.955)
  Pallas kernels: 21.5 us -> 18.6 us
    pallas_call x1, Pallas kernels: 1.73 us -> 0.09 us  [reduce_all(): small_call(share_kernel, whole((16, 56, I), BF16), 0, 'plane_sums', **opt...]
    unnamed x18 -> x14, local copies, waits for them, and re-layouts: 6.03 us -> 5.37 us
  transfers between devices with their start and end apart: 3 -> 3, of which waited for: 2 -> 2; matrix products, arithmetic and copies ran while one was open for 2% -> 2% of each run, Pallas kernels for 7% -> 8%
where the time goes in v6:
time: 96.5 us; the launch traced here: 96 us
  starting transfers between devices  31.4 us (33%)
  blocking collectives  31.4 us (33%)
  Pallas kernels  18.6 us (19%)
  local copies, waits for them, and re-layouts  7.78 us (8%)
  waiting for transfers between devices  5.9 us (6%)
    all_to_all x2, blocking collectives, exchange(): return lax.all_to_all(parts, ('row', 'col'), 0, 0, axis_index_groups=groups)  31.4 us
    ppermute x1, starting transfers between devices, on_device(): window = lax.ppermute(mine, ('row', 'col'), window_pairs())  17.6 us
    all_to_all x2, starting transfers between devices, exchange(): return lax.all_to_all(parts, ('row', 'col'), 0, 0, axis_index_groups=groups)  13.9 us
    pallas_call x1, Pallas kernels, run_main(): pl.pallas_call(main_kernel, out_shape=(whole((32, 16, I), F32), whole((80...  9.02 us
    all_to_all x2, waiting for transfers between devices, exchange(): return lax.all_to_all(parts, ('row', 'col'), 0, 0, axis_index_groups=groups)  5.89 us
    unnamed x14, local copies, waits for them, and re-layouts  5.37 us
    pallas_call x1, Pallas kernels, run_forward(): pl.pallas_call(forward_kernel, out_shape=whole((J, C, I), F32), in_specs=...  4.37 us
    pallas_call x1, Pallas kernels, run_back(): pl.pallas_call(back_kernel, out_shape=(whole((80, C, I), F32), whole((10,...  2.94 us
  transfers between devices with their start and end apart: 3, of which 2 were waited for; matrix products, arithmetic and copies ran while one was open for 2% of the time, Pallas kernels for 8%

profile of v6, /device:TPU:1, one launch (start us, length us, event | category | flops | bytes accessed | tf_op | source)
XLA Modules:
  0.0 96.0 jit_solution(6035751570373973635)
XLA Ops:
  0.7 0.7 constant_dynamic-slice_fusion
  1.4 17.6 %collective-permute-start = (bf16[72,128]{1,0:T(8,128)(2,1)S(1)}, bf16[72,128]{1,0:T(8,128)(2,1)S(1)}, u32[]{:S(2)}, u32[]{:S(2)}) collective-permute-start(bf16[72,128]{1,0:T(8,128)(2,1)S(1)} %constant_dynamic-slice_fusion), channel_id=1, source_target_pairs={{16,0},{18,1},{49,2},{51,3},{87,4},{81,5},{112,6},{114,7},{144,8},... | collective-permute-start | bytes 55304 | tf_op jit(solution)/shard_map/ppermute | solution.py:458
  19.0 0.7 fusion
  19.7 0.6 broadcast_in_dim.2
  20.4 4.4 %all-to-all-start = ((bf16[16,16,128]{2,1,0:T(8,128)(2,1)}), bf16[16,16,128]{2,1,0:T(8,128)(2,1)S(1)}, u32[]{:S(2)}, u32[]{:S(2)}) async-start(bf16[16,16,128]{2,1,0:T(8,128)(2,1)} %broadcast_in_dim.2), calls=%async_computation | async-start | bytes 131072 | tf_op jit(solution)/shard_map/all_to_all | solution.py:55
  24.8 0.0 copy-start
  24.8 0.9 copy-done
  25.7 0.0 copy-start.3
  25.7 1.2 %copy-done.3 = bf16[128,64,64]{0,2,1:T(8,128)(2,1)S(1)} copy-done((bf16[128,64,64]{0,2,1:T(8,128)(2,1)S(1)}, bf16[128,64,64]{0,2,1:T(8,128)(2,1)}, u32[]{:S(2)}) %copy-start.3) | copy-done | bytes 1048600
  26.9 0.0 copy-start.2
  26.9 0.0 copy-start.4
  26.9 2.9 %tile_back.1 = (f32[80,64,128]{2,1,0:T(8,128)S(1)}, f32[10,64,128]{2,1,0:T(8,128)S(1)}) custom-call(bf16[64,64,128]{2,1,0:T(8,128)(2,1)S(1)} %bitcast.9, bf16[9,64,64]{2,1,0:T(8,128)(2,1)S(1)} %bitcast.7), custom_call_target="tpu_custom_call" | custom-call | flops 2400000000 | bytes 4000000 | tf_op jit(solution)/shard_map/tile_back/pallas_call | solution.py:269
  29.9 0.0 copy-start.5
  29.9 1.5 %copy-done.5 = f32[80,64,128]{2,1,0:T(8,128)} copy-done((f32[80,64,128]{2,1,0:T(8,128)}, f32[80,64,128]{2,1,0:T(8,128)S(1)}, u32[]{:S(2)}) %copy-start.5) | copy-done | bytes 2621464
  31.4 0.1 pad_add_fusion.ids
  31.4 0.0 collective-permute-done.window
  31.4 3.1 %all-to-all-done.ends = bf16[16,16,128]{2,1,0:T(8,128)(2,1)S(1)} async-done(((bf16[16,16,128]{2,1,0:T(8,128)(2,1)}), bf16[16,16,128]{2,1,0:T(8,128)(2,1)S(1)}, u32[]{:S(2)}, u32[]{:S(2)}) %all-to-all-start) | async-done | bytes 65568 | tf_op jit(solution)/shard_map/all_to_all | solution.py:55
  34.5 0.0 copy-done.2
  34.5 0.0 copy-done.4
  34.5 0.0 copy-start.6
  34.5 1.7 %copy-done.6 = f32[80,64,128]{2,1,0:T(8,128)S(1)} copy-done((f32[80,64,128]{2,1,0:T(8,128)S(1)}, f32[80,64,128]{2,1,0:T(8,128)}, u32[]{:S(2)}) %copy-start.6) | copy-done | bytes 2621464
  36.3 9.0 %tile_gradients.1 = (f32[32,16,128]{2,1,0:T(8,128)S(1)}, bf16[80,64,128]{2,1,0:T(8,128)(2,1)S(1)}, bf16[10,64,128]{2,1,0:T(8,128)(2,1)S(1)}) custom-call(bf16[64,64,128]{2,1,0:T(8,128)(2,1)S(1)} %bitcast.10, f32[80,64,128]{2,1,0:T(8,128)S(1)} %copy-done.6, f32[10,64,128]{2,1,0:T(8,128)S(1)} %get-tuple-element.11.gae, bf16[128,128]{1,0:T(8,128)(2,1)S(1)} %copy-done.2, ...), custom_call_target="tpu_custom_call" | custom-call | flops 1300000000 | bytes 6000000 | tf_op jit(solution)/shard_map/tile_gradients/pallas_call | solution.py:281
  45.3 0.0 copy-start.1
  45.3 11.6 %all_to_all.20.got = f32[32,16,128]{2,1,0:T(8,128)S(1)} all-to-all(f32[32,16,128]{2,1,0:T(8,128)S(1)} %get-tuple-element.14), channel_id=1, replica_groups={{0,8,16,24,128,136,144,152,256,264,272,280,384,392,400,408,32,40,48,56,..., dimensions={0} | all-to-all | bytes 524288 | tf_op jit(solution)/shard_map/all_to_all | solution.py:55
  56.9 0.1 plane_sums.1
  57.0 19.8 %all_to_all.21.got = bf16[16,56,128]{2,1,0:T(8,128)(2,1)S(1)} all-to-all(bf16[16,56,128]{2,1,0:T(8,128)(2,1)S(1)} %plane_sums.1), channel_id=1, replica_groups={{0,1,2,3,4,5,6,7,64,65,66,67,68,69,70,71},{8,9,10,11,12,13,14,15,72,73,..., dimensions={0} | all-to-all | bytes 458752 | tf_op jit(solution)/shard_map/all_to_all | solution.py:55
  76.8 1.3 %line_sums.1 = bf16[32,16,128]{2,1,0:T(8,128)(2,1)} custom-call(bf16[16,56,128]{2,1,0:T(8,128)(2,1)S(1)} %all_to_all.21.got, s32[2]{0:T(128)S(1)} %pad_add_fusion.ids), custom_call_target="tpu_custom_call" | custom-call | flops 1000000 | bytes 500000 | tf_op jit(solution)/shard_map/line_sums/pallas_call | solution.py:446
  78.1 9.5 %all-to-all-start.3 = ((bf16[32,16,128]{2,1,0:T(8,128)(2,1)}), bf16[32,16,128]{2,1,0:T(8,128)(2,1)S(1)}, u32[]{:S(2)}, u32[]{:S(2)}) async-start(bf16[32,16,128]{2,1,0:T(8,128)(2,1)} %line_sums.1), calls=%async_computation.3 | async-start | bytes 262144 | tf_op jit(solution)/shard_map/all_to_all | solution.py:55
  87.6 0.0 copy-done.1
  87.6 0.2 copy.7
  87.8 0.2 reshape.17.w
  87.9 4.4 %tile_forward.1 = f32[64,64,128]{2,1,0:T(8,128)} custom-call(bf16[80,64,128]{2,1,0:T(8,128)(2,1)S(1)} %get-tuple-element.12.act, bf16[10,64,128]{2,1,0:T(8,128)(2,1)S(1)} %get-tuple-element.13.edge, bf16[192,192]{1,0:T(8,128)(2,1)S(1)} %reshape.17.w), custom_call_target="tpu_custom_call" | custom-call | flops 700000000 | bytes 3500000 | tf_op jit(solution)/shard_map/tile_forward/pallas_call | solution.py:330
  92.3 2.8 %all-to-all-done.3.got = bf16[32,16,128]{2,1,0:T(8,128)(2,1)S(1)} async-done(((bf16[32,16,128]{2,1,0:T(8,128)(2,1)}), bf16[32,16,128]{2,1,0:T(8,128)(2,1)S(1)}, u32[]{:S(2)}, u32[]{:S(2)}) %all-to-all-start.3) | async-done | bytes 131104 | tf_op jit(solution)/shard_map/all_to_all | solution.py:55
  95.1 0.9 unpack.1
  (1 shorter events, 0.0 us)
Async XLA Ops:
  1.4 30.0 %collective-permute-start = (bf16[72,128]{1,0:T(8,128)(2,1)S(1)}, bf16[72,128]{1,0:T(8,128)(2,1)S(1)}, u32[]{:S(2)}, u32[]{:S(2)}) collective-permute-start(bf16[72,128]{1,0:T(8,128)(2,1)S(1)} %constant_dynamic-slice_fusion), channel_id=1, source_target_pairs={{16,0},{18,1},{49,2},{51,3},{87,4},{81,5},{112,6},{114,7},{144,8},... | collective-permute-start | bytes 55304 | tf_op jit(solution)/shard_map/ppermute | solution.py:458
  20.4 14.2 %all-to-all-start = ((bf16[16,16,128]{2,1,0:T(8,128)(2,1)}), bf16[16,16,128]{2,1,0:T(8,128)(2,1)S(1)}, u32[]{:S(2)}, u32[]{:S(2)}) async-start(bf16[16,16,128]{2,1,0:T(8,128)(2,1)} %broadcast_in_dim.2), calls=%async_computation | async-start | bytes 131072 | tf_op jit(solution)/shard_map/all_to_all | solution.py:55
  24.8 0.9 copy-start
  25.7 1.2 %copy-start.3 = (bf16[128,64,64]{0,2,1:T(8,128)(2,1)S(1)}, bf16[128,64,64]{0,2,1:T(8,128)(2,1)}, u32[]{:S(2)}) copy-start(bf16[128,64,64]{0,2,1:T(8,128)(2,1)} %param.5) | copy-start | bytes 3145732
  26.9 7.6 %copy-start.2 = (bf16[128,128]{1,0:T(8,128)(2,1)S(1)}, bf16[128,128]{1,0:T(8,128)(2,1)}, u32[]{:S(2)}) copy-start(bf16[128,128]{1,0:T(8,128)(2,1)} %own.1) | copy-start | bytes 98308
  26.9 7.6 %copy-start.4 = (bf16[128,64,64]{0,2,1:T(8,128)(2,1)S(1)}, bf16[128,64,64]{0,2,1:T(8,128)(2,1)}, u32[]{:S(2)}) copy-start(bf16[128,64,64]{0,2,1:T(8,128)(2,1)} %param.5) | copy-start | bytes 3145732
  29.9 1.5 %copy-start.5 = (f32[80,64,128]{2,1,0:T(8,128)}, f32[80,64,128]{2,1,0:T(8,128)S(1)}, u32[]{:S(2)}) copy-start(f32[80,64,128]{2,1,0:T(8,128)S(1)} %get-tuple-element.10.ga) | copy-start | bytes 7864324
  34.5 1.7 %copy-start.6 = (f32[80,64,128]{2,1,0:T(8,128)S(1)}, f32[80,64,128]{2,1,0:T(8,128)}, u32[]{:S(2)}) copy-start(f32[80,64,128]{2,1,0:T(8,128)} %copy-done.5) | copy-start | bytes 7864324
  45.3 42.3 %copy-start.1 = (bf16[3,3,64,64]{3,2,1,0:T(8,128)(2,1)S(1)}, bf16[3,3,64,64]{3,2,1,0:T(8,128)(2,1)}, u32[]{:S(2)}) copy-start(bf16[3,3,64,64]{3,2,1,0:T(8,128)(2,1)} %param.4) | copy-start | bytes 221188
  78.1 17.0 %all-to-all-start.3 = ((bf16[32,16,128]{2,1,0:T(8,128)(2,1)}), bf16[32,16,128]{2,1,0:T(8,128)(2,1)S(1)}, u32[]{:S(2)}, u32[]{:S(2)}) async-start(bf16[32,16,128]{2,1,0:T(8,128)(2,1)} %line_sums.1), calls=%async_computation.3 | async-start | bytes 262144 | tf_op jit(solution)/shard_map/all_to_all | solution.py:55

commit v7 on v6

--- a/solution.py
+++ b/solution.py
@@ -36,19 +36,40 @@
 ]
 
 
+def chip(device):
+    row, col = device // COLS, device % COLS
+    return col // 8, row // 4, row // 2 % 2 * 8 + col % 8
+
+
+def hops(one, other):
+    steps = [abs(a - b) for a, b in zip(chip(one), chip(other))]
+    return sum(min(n, size - n) for n, size in zip(steps, (4, 4, 16)))
+
+
+def match(sources, targets, most):
+    taken = {}
+
+    def place(target, seen):
+        for source in sorted(sources, key=lambda source: hops(source, target)):
+            if source in seen or hops(source, target) > most:
+                continue
+            seen.add(source)
+            if source not in taken or place(taken[source], seen):
+                taken[source] = target
+                return True
+        return False
+
+    return taken if all(place(target, set()) for target in targets) else None
+
+
 def window_pairs():
     pairs = []
-    for row in range(ROWS):
-        for col in range(COLS):
-            x, z_lo = col // 8, col % 8
-            place = row // 2 % 2 * 4 + col % 2 * 2 + row % 2
-            source_row = col // 2
-            source_col = (row // 4 + 2) % 4 * 8 + (place - TURN[z_lo // 2]) % 8
-            pairs.append((source_row * COLS + source_col, row * COLS + col))
+    for block in range(ROWS):
+        sources = [block * COLS + col for col in range(COLS)]
+        targets = [row * COLS + 2 * block + half for row in range(ROWS) for half in range(2)]
+        found = next(filter(None, (match(sources, targets, most) for most in range(13))))
+        pairs += sorted(found.items())
     return pairs
-
-
-TURN = (0, 7, 1, 0)
 
 
 def exchange(parts, groups):
@@ -154,6 +175,7 @@
     half[:, :I] = own[...].astype(F32).T * 0.5
     half[:, I:] = jnp.concatenate([edge] * 8, axis=0).T * 0.5
     inner = window[...].astype(F32)
+    inner = jnp.where(col % 2 == 0, inner[: J + G], inner[J - G :])
     low = ends[jnp.maximum(block - 1, 0)].astype(F32)[G:]
     high = ends[jnp.minimum(block + 1, ROWS - 1)].astype(F32)[:G]
     wide = jnp.where(
@@ -453,9 +475,7 @@
     rows_local = embedding.shape[0]
     row_id = lax.axis_index("row")
     col_id = lax.axis_index("col")
-    place = (col_id % 8 + sum(jnp.where(row_id % 4 == n, turn, 0) for n, turn in enumerate(TURN))) % 8
-    mine = lax.dynamic_slice_in_dim(embedding, place // 2 % 2 * (J - G), J + G, 0)
-    window = lax.ppermute(mine, ("row", "col"), window_pairs())
+    window = lax.ppermute(embedding, ("row", "col"), window_pairs())
     ends = jnp.concatenate([embedding[:G], embedding[rows_local - G :]], axis=0)
     ends = exchange(jnp.broadcast_to(ends[None], (ROWS,) + ends.shape), ROW_GROUPS)
     ids = jnp.stack([row_id, col_id])

time: 96.5 us -> 96.2 us (level)
    ppermute x1, starting transfers between devices: 17.6 us -> 16.5 us  [on_device(): window = lax.ppermute(embedding, ('row', 'col'), window_pairs())]
where the time goes in v7:
time: 96.2 us; the launch traced here: 95.7 us
  blocking collectives  32.1 us (33%)
  starting transfers between devices  31.2 us (32%)
  Pallas kernels  18.6 us (19%)
  local copies, waits for them, and re-layouts  7.08 us (7%)
  waiting for transfers between devices  5.9 us (6%)
    all_to_all x2, blocking collectives, exchange(): return lax.all_to_all(parts, ('row', 'col'), 0, 0, axis_index_groups=groups)  32.1 us
    ppermute x1, starting transfers between devices, on_device(): window = lax.ppermute(embedding, ('row', 'col'), window_pairs())  16.5 us
    all_to_all x2, starting transfers between devices, exchange(): return lax.all_to_all(parts, ('row', 'col'), 0, 0, axis_index_groups=groups)  14.7 us
    pallas_call x1, Pallas kernels, run_main(): pl.pallas_call(main_kernel, out_shape=(whole((32, 16, I), F32), whole((80...  9.06 us
    all_to_all x2, waiting for transfers between devices, exchange(): return lax.all_to_all(parts, ('row', 'col'), 0, 0, axis_index_groups=groups)  5.9 us
    unnamed x14, local copies, waits for them, and re-layouts  5.37 us
    pallas_call x1, Pallas kernels, run_forward(): pl.pallas_call(forward_kernel, out_shape=whole((J, C, I), F32), in_specs=...  4.36 us
    pallas_call x1, Pallas kernels, run_back(): pl.pallas_call(back_kernel, out_shape=(whole((80, C, I), F32), whole((10,...  2.94 us
  transfers between devices with their start and end apart: 3, of which 2 were waited for; matrix products, arithmetic and copies ran while one was open for 2% of the time, Pallas kernels for 8%

profile of v7, /device:TPU:1, one launch (start us, length us, event | category | flops | bytes accessed | tf_op | source)
XLA Modules:
  0.0 95.7 jit_solution(2467317366807606668)
XLA Ops:
  0.6 16.5 %collective-permute-start = (bf16[128,128]{1,0:T(8,128)(2,1)}, bf16[128,128]{1,0:T(8,128)(2,1)S(1)}, u32[]{:S(2)}, u32[]{:S(2)}) collective-permute-start(bf16[128,128]{1,0:T(8,128)(2,1)} %own.1), channel_id=1, source_target_pairs={{0,33},{1,1},{2,417},{3,64},{4,320},{5,97},{6,480},{7,481},{8,0},{... | collective-permute-start | bytes 98312 | tf_op jit(solution)/shard_map/ppermute | solution.py:478
  17.2 0.7 fusion
  17.9 0.6 broadcast_in_dim.2
  18.5 5.2 %all-to-all-start = ((bf16[16,16,128]{2,1,0:T(8,128)(2,1)}), bf16[16,16,128]{2,1,0:T(8,128)(2,1)S(1)}, u32[]{:S(2)}, u32[]{:S(2)}) async-start(bf16[16,16,128]{2,1,0:T(8,128)(2,1)} %broadcast_in_dim.2), calls=%async_computation | async-start | bytes 131072 | tf_op jit(solution)/shard_map/all_to_all | solution.py:76
  23.8 0.0 copy-start
  23.8 0.9 copy-done
  24.7 0.0 copy-start.3
  24.7 1.2 %copy-done.3 = bf16[128,64,64]{0,2,1:T(8,128)(2,1)S(1)} copy-done((bf16[128,64,64]{0,2,1:T(8,128)(2,1)S(1)}, bf16[128,64,64]{0,2,1:T(8,128)(2,1)}, u32[]{:S(2)}) %copy-start.3) | copy-done | bytes 1048600
  25.9 0.0 copy-start.2
  25.9 0.0 copy-start.4
  25.9 2.9 %tile_back.1 = (f32[80,64,128]{2,1,0:T(8,128)S(1)}, f32[10,64,128]{2,1,0:T(8,128)S(1)}) custom-call(bf16[64,64,128]{2,1,0:T(8,128)(2,1)S(1)} %bitcast.9, bf16[9,64,64]{2,1,0:T(8,128)(2,1)S(1)} %bitcast.7), custom_call_target="tpu_custom_call" | custom-call | flops 2400000000 | bytes 4000000 | tf_op jit(solution)/shard_map/tile_back/pallas_call | solution.py:291
  28.8 0.0 copy-start.5
  28.8 1.5 %copy-done.5 = f32[80,64,128]{2,1,0:T(8,128)} copy-done((f32[80,64,128]{2,1,0:T(8,128)}, f32[80,64,128]{2,1,0:T(8,128)S(1)}, u32[]{:S(2)}) %copy-start.5) | copy-done | bytes 2621464
  30.3 0.1 pad_add_fusion.ids
  30.4 0.0 collective-permute-done.window
  30.4 3.1 %all-to-all-done.ends = bf16[16,16,128]{2,1,0:T(8,128)(2,1)S(1)} async-done(((bf16[16,16,128]{2,1,0:T(8,128)(2,1)}), bf16[16,16,128]{2,1,0:T(8,128)(2,1)S(1)}, u32[]{:S(2)}, u32[]{:S(2)}) %all-to-all-start) | async-done | bytes 65568 | tf_op jit(solution)/shard_map/all_to_all | solution.py:76
  33.5 0.0 copy-done.2
  33.5 0.0 copy-done.4
  33.5 0.0 copy-start.6
  33.5 1.7 %copy-done.6 = f32[80,64,128]{2,1,0:T(8,128)S(1)} copy-done((f32[80,64,128]{2,1,0:T(8,128)S(1)}, f32[80,64,128]{2,1,0:T(8,128)}, u32[]{:S(2)}) %copy-start.6) | copy-done | bytes 2621464
  35.2 9.1 %tile_gradients.1 = (f32[32,16,128]{2,1,0:T(8,128)S(1)}, bf16[80,64,128]{2,1,0:T(8,128)(2,1)S(1)}, bf16[10,64,128]{2,1,0:T(8,128)(2,1)S(1)}) custom-call(bf16[64,64,128]{2,1,0:T(8,128)(2,1)S(1)} %bitcast.10, f32[80,64,128]{2,1,0:T(8,128)S(1)} %copy-done.6, f32[10,64,128]{2,1,0:T(8,128)S(1)} %get-tuple-element.11.gae, bf16[128,128]{1,0:T(8,128)(2,1)S(1)} %copy-done.2, ...), custom_call_target="tpu_custom_call" | custom-call | flops 1300000000 | bytes 6000000 | tf_op jit(solution)/shard_map/tile_gradients/pallas_call | solution.py:303
  44.3 0.0 copy-start.1
  44.3 13.0 %all_to_all.20.got = f32[32,16,128]{2,1,0:T(8,128)S(1)} all-to-all(f32[32,16,128]{2,1,0:T(8,128)S(1)} %get-tuple-element.14), channel_id=1, replica_groups={{0,8,16,24,128,136,144,152,256,264,272,280,384,392,400,408,32,40,48,56,..., dimensions={0} | all-to-all | bytes 524288 | tf_op jit(solution)/shard_map/all_to_all | solution.py:76
  57.3 0.1 plane_sums.1
  57.4 19.1 %all_to_all.21.got = bf16[16,56,128]{2,1,0:T(8,128)(2,1)S(1)} all-to-all(bf16[16,56,128]{2,1,0:T(8,128)(2,1)S(1)} %plane_sums.1), channel_id=1, replica_groups={{0,1,2,3,4,5,6,7,64,65,66,67,68,69,70,71},{8,9,10,11,12,13,14,15,72,73,..., dimensions={0} | all-to-all | bytes 458752 | tf_op jit(solution)/shard_map/all_to_all | solution.py:76
  76.5 1.3 %line_sums.1 = bf16[32,16,128]{2,1,0:T(8,128)(2,1)} custom-call(bf16[16,56,128]{2,1,0:T(8,128)(2,1)S(1)} %all_to_all.21.got, s32[2]{0:T(128)S(1)} %pad_add_fusion.ids), custom_call_target="tpu_custom_call" | custom-call | flops 1000000 | bytes 500000 | tf_op jit(solution)/shard_map/line_sums/pallas_call | solution.py:468
  77.8 9.5 %all-to-all-start.3 = ((bf16[32,16,128]{2,1,0:T(8,128)(2,1)}), bf16[32,16,128]{2,1,0:T(8,128)(2,1)S(1)}, u32[]{:S(2)}, u32[]{:S(2)}) async-start(bf16[32,16,128]{2,1,0:T(8,128)(2,1)} %line_sums.1), calls=%async_computation.3 | async-start | bytes 262144 | tf_op jit(solution)/shard_map/all_to_all | solution.py:76
  87.3 0.0 copy-done.1
  87.3 0.2 copy.7
  87.4 0.2 reshape.17.w
  87.6 4.4 %tile_forward.1 = f32[64,64,128]{2,1,0:T(8,128)} custom-call(bf16[80,64,128]{2,1,0:T(8,128)(2,1)S(1)} %get-tuple-element.12.act, bf16[10,64,128]{2,1,0:T(8,128)(2,1)S(1)} %get-tuple-element.13.edge, bf16[192,192]{1,0:T(8,128)(2,1)S(1)} %reshape.17.w), custom_call_target="tpu_custom_call" | custom-call | flops 700000000 | bytes 3500000 | tf_op jit(solution)/shard_map/tile_forward/pallas_call | solution.py:352
  92.0 2.8 %all-to-all-done.3.got = bf16[32,16,128]{2,1,0:T(8,128)(2,1)S(1)} async-done(((bf16[32,16,128]{2,1,0:T(8,128)(2,1)}), bf16[32,16,128]{2,1,0:T(8,128)(2,1)S(1)}, u32[]{:S(2)}, u32[]{:S(2)}) %all-to-all-start.3) | async-done | bytes 131104 | tf_op jit(solution)/shard_map/all_to_all | solution.py:76
  94.8 0.9 unpack.1
  (1 shorter events, 0.0 us)
Async XLA Ops:
  0.6 29.8 %collective-permute-start = (bf16[128,128]{1,0:T(8,128)(2,1)}, bf16[128,128]{1,0:T(8,128)(2,1)S(1)}, u32[]{:S(2)}, u32[]{:S(2)}) collective-permute-start(bf16[128,128]{1,0:T(8,128)(2,1)} %own.1), channel_id=1, source_target_pairs={{0,33},{1,1},{2,417},{3,64},{4,320},{5,97},{6,480},{7,481},{8,0},{... | collective-permute-start | bytes 98312 | tf_op jit(solution)/shard_map/ppermute | solution.py:478
  18.5 14.9 %all-to-all-start = ((bf16[16,16,128]{2,1,0:T(8,128)(2,1)}), bf16[16,16,128]{2,1,0:T(8,128)(2,1)S(1)}, u32[]{:S(2)}, u32[]{:S(2)}) async-start(bf16[16,16,128]{2,1,0:T(8,128)(2,1)} %broadcast_in_dim.2), calls=%async_computation | async-start | bytes 131072 | tf_op jit(solution)/shard_map/all_to_all | solution.py:76
  23.8 0.9 copy-start
  24.7 1.2 %copy-start.3 = (bf16[128,64,64]{0,2,1:T(8,128)(2,1)S(1)}, bf16[128,64,64]{0,2,1:T(8,128)(2,1)}, u32[]{:S(2)}) copy-start(bf16[128,64,64]{0,2,1:T(8,128)(2,1)} %param.5) | copy-start | bytes 3145732
  25.9 7.6 %copy-start.2 = (bf16[128,128]{1,0:T(8,128)(2,1)S(1)}, bf16[128,128]{1,0:T(8,128)(2,1)}, u32[]{:S(2)}) copy-start(bf16[128,128]{1,0:T(8,128)(2,1)} %own.1) | copy-start | bytes 98308
  25.9 7.6 %copy-start.4 = (bf16[128,64,64]{0,2,1:T(8,128)(2,1)S(1)}, bf16[128,64,64]{0,2,1:T(8,128)(2,1)}, u32[]{:S(2)}) copy-start(bf16[128,64,64]{0,2,1:T(8,128)(2,1)} %param.5) | copy-start | bytes 3145732
  28.8 1.5 %copy-start.5 = (f32[80,64,128]{2,1,0:T(8,128)}, f32[80,64,128]{2,1,0:T(8,128)S(1)}, u32[]{:S(2)}) copy-start(f32[80,64,128]{2,1,0:T(8,128)S(1)} %get-tuple-element.10.ga) | copy-start | bytes 7864324
  33.5 1.7 %copy-start.6 = (f32[80,64,128]{2,1,0:T(8,128)S(1)}, f32[80,64,128]{2,1,0:T(8,128)}, u32[]{:S(2)}) copy-start(f32[80,64,128]{2,1,0:T(8,128)} %copy-done.5) | copy-start | bytes 7864324
  44.3 43.0 %copy-start.1 = (bf16[3,3,64,64]{3,2,1,0:T(8,128)(2,1)S(1)}, bf16[3,3,64,64]{3,2,1,0:T(8,128)(2,1)}, u32[]{:S(2)}) copy-start(bf16[3,3,64,64]{3,2,1,0:T(8,128)(2,1)} %param.4) | copy-start | bytes 221188
  77.8 17.0 %all-to-all-start.3 = ((bf16[32,16,128]{2,1,0:T(8,128)(2,1)}), bf16[32,16,128]{2,1,0:T(8,128)(2,1)S(1)}, u32[]{:S(2)}, u32[]{:S(2)}) async-start(bf16[32,16,128]{2,1,0:T(8,128)(2,1)} %line_sums.1), calls=%async_computation.3 | async-start | bytes 262144 | tf_op jit(solution)/shard_map/all_to_all | solution.py:76

commit v8 on v6

--- a/solution.py
+++ b/solution.py
@@ -439,14 +439,16 @@
     )
 
 
-def reduce_all(parts, ids, **options):
+def reduce_all(parts, ids, prediction, **options):
     got = exchange(parts, PLANE_GROUPS)
     share = small_call(share_kernel, whole((16, 56, I), BF16), 0, "plane_sums", **options)(got)
     got = exchange(share, LINE_GROUPS)
     done = small_call(finish_kernel, whole((32, 16, I), BF16), 1, "line_sums", **options)(got, ids)
+    done, prediction = lax.optimization_barrier((done, prediction))
     got = exchange(done, PLANE_GROUPS)
     shapes = (whole((9, C, C), F32), whole((2 * C, I), F32))
-    return small_call(unpack_kernel, shapes, 0, "unpack", **options)(got)
+    gk, ge = small_call(unpack_kernel, shapes, 0, "unpack", **options)(got)
+    return prediction, gk, ge
 
 
 def on_device(embedding, kernel, cotangent):
@@ -463,9 +465,8 @@
     ga, gae = run_back(cot, kernel.reshape(9, C, C))
     parts, act, edge = run_main(cot, ga, gae, embedding, ends, window, ids)
     taps = kernel.transpose(1, 3, 0, 2).reshape(192, 192)
-    prediction = run_forward(act, edge, taps).transpose(2, 0, 1)
-    gk, ge = reduce_all(parts, ids)
-    return prediction, gk.reshape(kernel.shape), ge
+    prediction, gk, ge = reduce_all(parts, ids, run_forward(act, edge, taps))
+    return prediction.transpose(2, 0, 1), gk.reshape(kernel.shape), ge
 
 
 def solution(mesh):

time: 96.5 us -> 96.1 us (level)
  waiting for transfers between devices: 5.9 us -> 11 us
  blocking collectives: 31.4 us -> 27.9 us
  starting transfers between devices: 31.4 us -> 29.4 us
    all_to_all x2, waiting for transfers between devices: 5.89 us -> 11 us  [exchange(): return lax.all_to_all(parts, ('row', 'col'), 0, 0, axis_index_groups=groups)]
    all_to_all x2, blocking collectives: 31.4 us -> 27.9 us  [exchange(): return lax.all_to_all(parts, ('row', 'col'), 0, 0, axis_index_groups=groups)]
    all_to_all x2, starting transfers between devices: 13.9 us -> 11.8 us  [exchange(): return lax.all_to_all(parts, ('row', 'col'), 0, 0, axis_index_groups=groups)]
where the time goes in v8:
time: 96.1 us; the launch traced here: 95.6 us
  starting transfers between devices  29.4 us (31%)
  blocking collectives  27.9 us (29%)
  Pallas kernels  18.6 us (19%)
  waiting for transfers between devices  11 us (11%)
  local copies, waits for them, and re-layouts  7.77 us (8%)
    all_to_all x2, blocking collectives, exchange(): return lax.all_to_all(parts, ('row', 'col'), 0, 0, axis_index_groups=groups)  27.9 us
    ppermute x1, starting transfers between devices, on_device(): window = lax.ppermute(mine, ('row', 'col'), window_pairs())  17.6 us
    all_to_all x2, starting transfers between devices, exchange(): return lax.all_to_all(parts, ('row', 'col'), 0, 0, axis_index_groups=groups)  11.8 us
    all_to_all x2, waiting for transfers between devices, exchange(): return lax.all_to_all(parts, ('row', 'col'), 0, 0, axis_index_groups=groups)  11 us
    pallas_call x1, Pallas kernels, run_main(): pl.pallas_call(main_kernel, out_shape=(whole((32, 16, I), F32), whole((80...  9.02 us
    unnamed x14, local copies, waits for them, and re-layouts  5.37 us
    pallas_call x1, Pallas kernels, run_forward(): pl.pallas_call(forward_kernel, out_shape=whole((J, C, I), F32), in_specs=...  4.36 us
    pallas_call x1, Pallas kernels, run_back(): pl.pallas_call(back_kernel, out_shape=(whole((80, C, I), F32), whole((10,...  2.94 us
  transfers between devices with their start and end apart: 3, of which 2 were waited for; matrix products, arithmetic and copies ran while one was open for 2% of the time, Pallas kernels for 8%

profile of v8, /device:TPU:1, one launch (start us, length us, event | category | flops | bytes accessed | tf_op | source)
XLA Modules:
  0.0 95.6 jit_solution(8904226726051619399)
XLA Ops:
  0.7 0.7 constant_dynamic-slice_fusion
  1.4 17.6 %collective-permute-start = (bf16[72,128]{1,0:T(8,128)(2,1)S(1)}, bf16[72,128]{1,0:T(8,128)(2,1)S(1)}, u32[]{:S(2)}, u32[]{:S(2)}) collective-permute-start(bf16[72,128]{1,0:T(8,128)(2,1)S(1)} %constant_dynamic-slice_fusion), channel_id=1, source_target_pairs={{16,0},{18,1},{49,2},{51,3},{87,4},{81,5},{112,6},{114,7},{144,8},... | collective-permute-start | bytes 55304 | tf_op jit(solution)/shard_map/ppermute | solution.py:460
  19.0 0.7 fusion
  19.7 0.6 broadcast_in_dim.2
  20.4 4.4 %all-to-all-start = ((bf16[16,16,128]{2,1,0:T(8,128)(2,1)}), bf16[16,16,128]{2,1,0:T(8,128)(2,1)S(1)}, u32[]{:S(2)}, u32[]{:S(2)}) async-start(bf16[16,16,128]{2,1,0:T(8,128)(2,1)} %broadcast_in_dim.2), calls=%async_computation | async-start | bytes 131072 | tf_op jit(solution)/shard_map/all_to_all | solution.py:55
  24.8 0.0 copy-start
  24.8 0.9 copy-done
  25.7 0.0 copy-start.3
  25.7 1.2 %copy-done.3 = bf16[128,64,64]{0,2,1:T(8,128)(2,1)S(1)} copy-done((bf16[128,64,64]{0,2,1:T(8,128)(2,1)S(1)}, bf16[128,64,64]{0,2,1:T(8,128)(2,1)}, u32[]{:S(2)}) %copy-start.3) | copy-done | bytes 1048600
  26.9 0.0 copy-start.2
  26.9 0.0 copy-start.4
  26.9 2.9 %tile_back.1 = (f32[80,64,128]{2,1,0:T(8,128)S(1)}, f32[10,64,128]{2,1,0:T(8,128)S(1)}) custom-call(bf16[64,64,128]{2,1,0:T(8,128)(2,1)S(1)} %bitcast.9, bf16[9,64,64]{2,1,0:T(8,128)(2,1)S(1)} %bitcast.7), custom_call_target="tpu_custom_call" | custom-call | flops 2400000000 | bytes 4000000 | tf_op jit(solution)/shard_map/tile_back/pallas_call | solution.py:269
  29.9 0.0 copy-start.5
  29.9 1.5 %copy-done.5 = f32[80,64,128]{2,1,0:T(8,128)} copy-done((f32[80,64,128]{2,1,0:T(8,128)}, f32[80,64,128]{2,1,0:T(8,128)S(1)}, u32[]{:S(2)}) %copy-start.5) | copy-done | bytes 2621464
  31.4 0.1 pad_add_fusion.ids
  31.4 0.0 collective-permute-done.window
  31.4 3.1 %all-to-all-done.ends = bf16[16,16,128]{2,1,0:T(8,128)(2,1)S(1)} async-done(((bf16[16,16,128]{2,1,0:T(8,128)(2,1)}), bf16[16,16,128]{2,1,0:T(8,128)(2,1)S(1)}, u32[]{:S(2)}, u32[]{:S(2)}) %all-to-all-start) | async-done | bytes 65568 | tf_op jit(solution)/shard_map/all_to_all | solution.py:55
  34.5 0.0 copy-done.2
  34.5 0.0 copy-done.4
  34.5 0.0 copy-start.6
  34.5 1.7 %copy-done.6 = f32[80,64,128]{2,1,0:T(8,128)S(1)} copy-done((f32[80,64,128]{2,1,0:T(8,128)S(1)}, f32[80,64,128]{2,1,0:T(8,128)}, u32[]{:S(2)}) %copy-start.6) | copy-done | bytes 2621464
  36.3 0.0 copy-start.1
  36.3 9.0 %tile_gradients.1 = (f32[32,16,128]{2,1,0:T(8,128)S(1)}, bf16[80,64,128]{2,1,0:T(8,128)(2,1)S(1)}, bf16[10,64,128]{2,1,0:T(8,128)(2,1)S(1)}) custom-call(bf16[64,64,128]{2,1,0:T(8,128)(2,1)S(1)} %bitcast.10, f32[80,64,128]{2,1,0:T(8,128)S(1)} %copy-done.6, f32[10,64,128]{2,1,0:T(8,128)S(1)} %get-tuple-element.13.gae, bf16[128,128]{1,0:T(8,128)(2,1)S(1)} %copy-done.2, ...), custom_call_target="tpu_custom_call" | custom-call | flops 1300000000 | bytes 6000000 | tf_op jit(solution)/shard_map/tile_gradients/pallas_call | solution.py:281
  45.3 11.5 %all_to_all.20.got = f32[32,16,128]{2,1,0:T(8,128)S(1)} all-to-all(f32[32,16,128]{2,1,0:T(8,128)S(1)} %get-tuple-element.14), channel_id=1, replica_groups={{0,8,16,24,128,136,144,152,256,264,272,280,384,392,400,408,32,40,48,56,..., dimensions={0} | all-to-all | bytes 524288 | tf_op jit(solution)/shard_map/all_to_all | solution.py:55
  56.7 0.8 plane_sums.1
  57.5 7.4 %all-to-all-start.2 = ((bf16[16,56,128]{2,1,0:T(8,128)(2,1)}), bf16[16,56,128]{2,1,0:T(8,128)(2,1)S(1)}, u32[]{:S(2)}, u32[]{:S(2)}) async-start(bf16[16,56,128]{2,1,0:T(8,128)(2,1)} %plane_sums.1), calls=%async_computation.2 | async-start | bytes 458752 | tf_op jit(solution)/shard_map/all_to_all | solution.py:55
  65.0 0.0 copy-done.1
  65.0 0.2 copy.7
  65.1 0.2 reshape.17.w
  65.3 4.4 %tile_forward.1 = f32[64,64,128]{2,1,0:T(8,128)} custom-call(bf16[80,64,128]{2,1,0:T(8,128)(2,1)S(1)} %get-tuple-element.15.act, bf16[10,64,128]{2,1,0:T(8,128)(2,1)S(1)} %get-tuple-element.16.edge, bf16[192,192]{1,0:T(8,128)(2,1)S(1)} %reshape.17.w), custom_call_target="tpu_custom_call" | custom-call | flops 700000000 | bytes 3500000 | tf_op jit(solution)/shard_map/tile_forward/pallas_call | solution.py:330
  69.7 7.9 %all-to-all-done.2.got = bf16[16,56,128]{2,1,0:T(8,128)(2,1)S(1)} async-done(((bf16[16,56,128]{2,1,0:T(8,128)(2,1)}), bf16[16,56,128]{2,1,0:T(8,128)(2,1)S(1)}, u32[]{:S(2)}, u32[]{:S(2)}) %all-to-all-start.2) | async-done | bytes 229408 | tf_op jit(solution)/shard_map/all_to_all | solution.py:55
  77.6 0.7 line_sums.1
  78.2 16.5 %all_to_all.21.got = bf16[32,16,128]{2,1,0:T(8,128)(2,1)S(1)} all-to-all(bf16[32,16,128]{2,1,0:T(8,128)(2,1)S(1)} %line_sums.1), channel_id=1, replica_groups={{0,8,16,24,128,136,144,152,256,264,272,280,384,392,400,408,32,40,48,56,..., dimensions={0} | all-to-all | bytes 262144 | tf_op jit(solution)/shard_map/all_to_all | solution.py:55
  94.7 0.9 unpack.1
  (1 shorter events, 0.0 us)
Async XLA Ops:
  1.4 30.0 %collective-permute-start = (bf16[72,128]{1,0:T(8,128)(2,1)S(1)}, bf16[72,128]{1,0:T(8,128)(2,1)S(1)}, u32[]{:S(2)}, u32[]{:S(2)}) collective-permute-start(bf16[72,128]{1,0:T(8,128)(2,1)S(1)} %constant_dynamic-slice_fusion), channel_id=1, source_target_pairs={{16,0},{18,1},{49,2},{51,3},{87,4},{81,5},{112,6},{114,7},{144,8},... | collective-permute-start | bytes 55304 | tf_op jit(solution)/shard_map/ppermute | solution.py:460
  20.4 14.2 %all-to-all-start = ((bf16[16,16,128]{2,1,0:T(8,128)(2,1)}), bf16[16,16,128]{2,1,0:T(8,128)(2,1)S(1)}, u32[]{:S(2)}, u32[]{:S(2)}) async-start(bf16[16,16,128]{2,1,0:T(8,128)(2,1)} %broadcast_in_dim.2), calls=%async_computation | async-start | bytes 131072 | tf_op jit(solution)/shard_map/all_to_all | solution.py:55
  24.8 0.9 copy-start
  25.7 1.2 %copy-start.3 = (bf16[128,64,64]{0,2,1:T(8,128)(2,1)S(1)}, bf16[128,64,64]{0,2,1:T(8,128)(2,1)}, u32[]{:S(2)}) copy-start(bf16[128,64,64]{0,2,1:T(8,128)(2,1)} %param.5) | copy-start | bytes 3145732
  26.9 7.6 %copy-start.2 = (bf16[128,128]{1,0:T(8,128)(2,1)S(1)}, bf16[128,128]{1,0:T(8,128)(2,1)}, u32[]{:S(2)}) copy-start(bf16[128,128]{1,0:T(8,128)(2,1)} %own.1) | copy-start | bytes 98308
  26.9 7.6 %copy-start.4 = (bf16[128,64,64]{0,2,1:T(8,128)(2,1)S(1)}, bf16[128,64,64]{0,2,1:T(8,128)(2,1)}, u32[]{:S(2)}) copy-start(bf16[128,64,64]{0,2,1:T(8,128)(2,1)} %param.5) | copy-start | bytes 3145732
  29.9 1.5 %copy-start.5 = (f32[80,64,128]{2,1,0:T(8,128)}, f32[80,64,128]{2,1,0:T(8,128)S(1)}, u32[]{:S(2)}) copy-start(f32[80,64,128]{2,1,0:T(8,128)S(1)} %get-tuple-element.12.ga) | copy-start | bytes 7864324
  34.5 1.7 %copy-start.6 = (f32[80,64,128]{2,1,0:T(8,128)S(1)}, f32[80,64,128]{2,1,0:T(8,128)}, u32[]{:S(2)}) copy-start(f32[80,64,128]{2,1,0:T(8,128)} %copy-done.5) | copy-start | bytes 7864324
  36.3 28.7 %copy-start.1 = (bf16[3,3,64,64]{3,2,1,0:T(8,128)(2,1)S(1)}, bf16[3,3,64,64]{3,2,1,0:T(8,128)(2,1)}, u32[]{:S(2)}) copy-start(bf16[3,3,64,64]{3,2,1,0:T(8,128)(2,1)} %param.4) | copy-start | bytes 221188
  57.5 20.0 %all-to-all-start.2 = ((bf16[16,56,128]{2,1,0:T(8,128)(2,1)}), bf16[16,56,128]{2,1,0:T(8,128)(2,1)S(1)}, u32[]{:S(2)}, u32[]{:S(2)}) async-start(bf16[16,56,128]{2,1,0:T(8,128)(2,1)} %plane_sums.1), calls=%async_computation.2 | async-start | bytes 458752 | tf_op jit(solution)/shard_map/all_to_all | solution.py:55
